TPU v7x, 32 devices: a whole 2x2x4 slice. The times are simulated.
32 devices in a mesh: group: 2 (over y), fsdp: 4 (over z), tensor: 2 (over x), seq: 2 (over core).
Axes of the slice: x: 2, y: 2, z: 4, core: 2. Of those that a mesh axis runs over, the one named last changes fastest.
Arguments:
- tokens: bfloat16 [4096, 4096], P(('group', 'fsdp', 'seq'), 'tensor'), parts along dimension 0, may hold values from -6 to 6
- hidden_grad: bfloat16 [4096, 28672], P(('group', 'fsdp', 'seq'), 'tensor'), parts along dimension 0, may hold values from -0.59765625 to 0.59765625
- tile_blocks: bfloat16 [4, 2, 2, 2, 128, 128], P('fsdp', 'tensor'), may hold values from -0.5 to 0.5
- tile_keep: int32 [4, 2, 2, 2], P('fsdp', 'tensor'), may hold values from 0 to 3583, as said below
- tile_count: int32 [4, 2, 2], P('fsdp', 'tensor'), may hold values from 0 to 2, as said below
Outputs:
- token_grad: bfloat16 [4096, 4096], P(('group', 'fsdp', 'seq')), parts along dimension 0
- tile_grads: bfloat16 [8, 2, 2, 2, 128, 128], P(('group', 'fsdp'), 'tensor', 'seq'), parts along dimension 0
There are 2 independent parts, one for each index of `group`. A program takes and returns all parts, laid end to end along the dimension named above; an argument that names none is the same for every part. Nothing has to cross between parts.
Inputs may be any that keep to these rules, and one draw needn't show every extreme that they name: `tile_keep`: within one tensor index and one matrix the live slots of all fsdp shards name distinct blocks; other slots hold arbitrary block numbers. `tile_count`: for every tensor index and matrix the counts over the fsdp shards sum to exactly 4; in each, some shard holds 2 and some holds none.
All inputs are finite; a program needn't handle non-finite values.
Results may differ from a plain program's by a relative error of at most 0.0049.
Values may be sent and summed in bfloat16 or wider, within the bound.
No kernel may reach another device: no remote copies, remote signals or barrier semaphores. Data moves between devices by JAX's collectives and lax.ppermute only.
A program may use at most 192 MiB of HBM per device.

v0:
```python
import jax
import jax.numpy as jnp
from jax import lax
from jax.sharding import PartitionSpec as P

HIGHEST = lax.Precision.HIGHEST


def slot_terms(x_full, hidden_grad, tile_data, row_index, col_index, live_mask, tile_size):
    tok_rows = x_full.shape[0]
    row_blocks = x_full.shape[1] // tile_size
    col_blocks = hidden_grad.shape[1] // tile_size
    x_taken = jnp.take(x_full.reshape(tok_rows, row_blocks, tile_size), row_index, axis=1)
    products = jnp.einsum("tsmk,smkn->tsmn", x_taken, tile_data, preferred_element_type=jnp.float32)
    col_table = (
        col_index[:, :, None] == jnp.arange(col_blocks, dtype=jnp.int32)[None, None, :]
    ).astype(jnp.float32) * live_mask[:, :, None]
    pre_acts = jnp.einsum("tsmn,smc->tmcn", products, col_table, precision=HIGHEST)
    gate_pre = pre_acts[:, 0]
    up_pre = pre_acts[:, 1]
    upstream = hidden_grad.reshape(tok_rows, col_blocks, tile_size).astype(jnp.float32)
    sigmoid_gate = 1.0 / (1.0 + jnp.exp(-gate_pre))
    grad_gate = upstream * up_pre * sigmoid_gate * (1.0 + gate_pre * (1.0 - sigmoid_gate))
    grad_up = upstream * gate_pre * sigmoid_gate
    grad_pair = jnp.stack([grad_gate, grad_up], axis=1).astype(jnp.bfloat16)
    flat_index = col_index + jnp.arange(2, dtype=jnp.int32)[None, :] * col_blocks
    grad_taken = jnp.take(
        grad_pair.reshape(tok_rows, 2 * col_blocks, tile_size), flat_index, axis=1
    )
    back_terms = jnp.einsum(
        "tsmn,smkn->tsmk", grad_taken, tile_data, preferred_element_type=jnp.float32
    )
    row_table = (
        row_index[:, :, None] == jnp.arange(row_blocks, dtype=jnp.int32)[None, None, :]
    ).astype(jnp.float32) * live_mask[:, :, None]
    token_part = jnp.einsum("tsmk,smr->trk", back_terms, row_table, precision=HIGHEST).reshape(
        tok_rows, row_blocks * tile_size
    )
    return (x_taken, grad_taken, grad_pair, token_part)


def local(tokens, hidden_grad, tile_blocks, tile_keep, tile_count):
    tile_size = tile_blocks.shape[-1]
    cap_slots = tile_blocks.shape[2]
    half_slots = cap_slots // 2
    x_full = lax.all_gather(tokens, "tensor", axis=1, tiled=True)
    tile_all = lax.all_gather(tile_blocks, "fsdp", axis=0, tiled=True)
    keep_all, count_all = (
        lax.all_gather(tile_keep, "fsdp", axis=0, tiled=True),
        lax.all_gather(tile_count, "fsdp", axis=0, tiled=True),
    )
    shard_total = tile_all.shape[0]
    slot_total = shard_total * cap_slots
    col_blocks = hidden_grad.shape[1] // tile_size
    tile_data = tile_all.reshape(slot_total, 2, tile_size, tile_size)
    block_index = keep_all.reshape(slot_total, 2)
    live_bool = (jnp.arange(cap_slots, dtype=jnp.int32)[None, :, None] < count_all).reshape(
        slot_total, 2
    )
    live_mask = live_bool.astype(jnp.float32)
    row_index = block_index // col_blocks
    col_index = block_index % col_blocks
    x_taken, grad_taken, grad_pair, token_part = slot_terms(
        x_full, hidden_grad, tile_data, row_index, col_index, live_mask, tile_size
    )
    token_grad = lax.psum(token_part, "tensor").astype(jnp.bfloat16)
    block_grads = jnp.einsum(
        "tsmk,tsmn->smkn", x_taken, grad_taken, preferred_element_type=jnp.float32
    )
    summed = lax.psum_scatter(
        block_grads * live_mask[:, :, None, None], ("fsdp", "seq"), scatter_dimension=0, tiled=True
    )
    tile_grads = summed.astype(jnp.bfloat16).reshape(1, 1, half_slots, 2, tile_size, tile_size)
    return (token_grad, tile_grads)


def solution(mesh):
    return jax.shard_map(
        local,
        mesh=mesh,
        in_specs=(
            P(("group", "fsdp", "seq"), "tensor"),
            P(("group", "fsdp", "seq"), "tensor"),
            P("fsdp", "tensor", None, None, None, None),
            P("fsdp", "tensor", None, None),
            P("fsdp", "tensor", None),
        ),
        out_specs=(
            P(("group", "fsdp", "seq"), None),
            P(("group", "fsdp"), "tensor", "seq", None, None, None),
        ),
        check_vma=False,
    )
```

profile of v0, /device:TPU:0, one launch (start us, length us, event | category | flops | bytes accessed | tf_op | source)
XLA Modules:
  0.0 267.6 jit_solution(14242219400160680829)
XLA Ops:
  7.2 2.3 copy.93
  9.5 12.9 %all_gather.12 = s32[4,1,2,2]{3,2,1,0:T(2,128)S(1)} all-gather(s32[1,1,2,2]{3,2,1,0:T(2,128)} %param.8), channel_id=1, replica_groups=mesh['group'=2,'fsdp'=4,'tensor'=2,'seq'=2] {'fsdp'}, dimensions={0}, use_global_device_ids=true | all-gather | bytes 80 | tf_op jit(solution)/shard_map/all_gather | solution.py:49
  23.4 7.7 %all_gather.13 = s32[4,1,2]{2,1,0:T(1,128)S(1)} all-gather(s32[1,1,2]{2,1,0:T(1,128)} %param.9), channel_id=1, replica_groups=mesh['group'=2,'fsdp'=4,'tensor'=2,'seq'=2] {'fsdp'}, dimensions={0}, use_global_device_ids=true | all-gather | bytes 40 | tf_op jit(solution)/shard_map/all_gather | solution.py:50
  31.9 10.0 %convert_bitcast_fusion = f32[32,8,112,128]{3,1,2,0:T(8,128)} fusion(bf16[256,14336]{1,0:T(8,128)(2,1)} %param.6), kind=kLoop, calls=%fused_computation.11 | loop fusion | flops 3670016 | bytes 22020096
  41.9 13.0 %copy.115 = f32[32,8,112,128]{3,2,1,0:T(8,128)} copy(f32[32,8,112,128]{3,1,2,0:T(8,128)} %convert_bitcast_fusion) | data formatting | bytes 29360128
  55.3 14.9 %all_gather.15 = bf16[4,1,2,2,128,128]{5,4,3,2,1,0:T(8,128)(2,1)S(1)} all-gather(bf16[1,1,2,2,128,128]{5,4,3,2,1,0:T(8,128)(2,1)S(1)} %copy-done.3), channel_id=1, replica_groups=mesh['group'=2,'fsdp'=4,'tensor'=2,'seq'=2] {'fsdp'}, dimensions={0}, use_global_device_ids=true | all-gather | bytes 655360 | tf_op jit(solution)/shard_map/all_gather | solution.py:47
  70.2 3.4 %copy.98 = bf16[256,32,128]{2,0,1:T(8,128)(2,1)S(1)} copy(bf16[256,32,128]{0,2,1:T(8,128)(2,1)} %bitcast.86) | data formatting | bytes 4194304 | tf_op jit(solution)/shard_map/reshape | solution.py:13
  73.6 1.7 gather_fusion
  75.3 1.5 copy.99
  76.8 1.0 copy-done
  77.7 0.5 convolution_bitcast_fusion.2
  78.3 26.9 %convolution_bitcast_fusion = f32[256,2,112,128]{3,2,0,1:T(8,128)} fusion(f32[256,8,2,128]{3,0,2,1:T(8,128)S(1)} %convolution_bitcast_fusion.2, f32[8,2]{0,1:T(2,128)S(1)} %get-tuple-element.11, s32[8,2]{0,1:T(2,128)S(1)} %and_select_fusion.2), kind=kOutput, calls=%fused_computation.2 | convolution fusion | flops 704646656 | bytes 31457408 | tf_op jit(solution)/shard_map/tsmn,smc->tmcn/dot_general | solution.py:18
  105.3 14.6 %fusion.2 = (bf16[256,1,112,128]{3,2,0,1:T(8,128)(2,1)S(1)}, bf16[256,1,112,128]{3,2,0,1:T(8,128)(2,1)}) fusion(f32[32,8,112,128]{3,2,1,0:T(8,128)S(1)} %bitcast.78, f32[256,2,112,128]{3,2,0,1:T(8,128)} %convolution_bitcast_fusion), kind=kLoop, calls=%fused_computation.7 | loop fusion | flops 47710208 | bytes 58720256 | tf_op jit(solution)/shard_map/convert.1
  119.9 6.0 %pad_maximum_fusion = bf16[256,2,112,128]{3,2,0,1:T(8,128)(2,1)S(1)} fusion(bf16[256,1,112,128]{3,2,0,1:T(8,128)(2,1)} %get-tuple-element.5, bf16[256,1,112,128]{3,2,0,1:T(8,128)(2,1)S(1)} %get-tuple-element.4), kind=kLoop, calls=%fused_computation.10 | loop fusion | flops 7340032 | bytes 29360128 | tf_op jit(solution)/shard_map/stack | solution.py:25
  125.9 2.1 copy.102
  128.0 17.3 %copy.104 = bf16[256,224,128]{2,0,1:T(8,128)(2,1)} copy(bf16[256,224,128]{2,1,0:T(8,128)(2,1)S(1)} %bitcast.79) | data formatting | bytes 29360128 | tf_op jit(solution)/shard_map/convert_element_type | solution.py:25
  145.3 6.0 %gather_fusion.1 = bf16[16,256,128]{2,1,0:T(8,128)(2,1)S(1)} fusion(bf16[256,224,128]{2,0,1:T(8,128)(2,1)} %copy.104, s32[1024]{0:T(1024)S(1)} %pad_clamp_fusion), kind=kCustom, calls=%fused_computation.1 | custom fusion | bytes 2097216 | tf_op jit(solution)/shard_map/jit(_take)/gather | solution.py:27
  151.3 1.3 copy.105
  152.6 1.9 convolution_bitcast_fusion.1
  154.5 4.3 %fusion.5 = f32[32,256,128,1]{2,0,3,1:T(8,128)S(1)} fusion(f32[256,8,2,128]{3,0,2,1:T(8,128)S(1)} %convolution_bitcast_fusion.1, f32[8,2]{0,1:T(2,128)S(1)} %get-tuple-element.11, s32[8,2]{0,1:T(2,128)S(1)} %get-tuple-element.3), kind=kOutput, calls=%fused_computation.14 | convolution fusion | flops 201327616 | bytes 6291584 | tf_op jit(solution)/shard_map/tsmk,smr->trk/dot_general | solution.py:36
  158.8 5.8 %copy.122 = f32[32,8,32,128]{3,1,2,0:T(8,128)} copy(f32[32,8,32,128]{3,2,1,0:T(8,128)S(1)} %bitcast.81) | data formatting | bytes 8388608
  164.6 1.5 convolution_multiply_fusion
  166.1 93.1 %all-reduce.1 = bf16[256,4096]{1,0:T(8,128)(2,1)} all-reduce(f32[256,4096]{1,0:T(8,128)} %bitcast.80), channel_id=1, replica_groups=mesh['group'=2,'fsdp'=4,'tensor'=2,'seq'=2] {'tensor'}, use_global_device_ids=true, to_apply=%region_0.1 | all-reduce | flops 1048576 | bytes 6291456 | tf_op jit(solution)/shard_map/psum | solution.py:66
  259.2 1.5 convert_bitcast_fusion.1
  (52 shorter events, 2.2 us)
Async XLA Ops:
  7.2 63.1 %all-gather.2.cloned.1.call-start = ((), (), s32[]{:S(2)}) async-start(), calls=%async_computation.1 | async-start | bytes 3145728 | tf_op jit(solution)/shard_map/all_gather | solution.py:46
  9.5 249.7 %reduce-scatter.2.cloned.1.call-start = ((), (), s32[]{:S(2)}) async-start(), calls=%async_computation.2 | async-start | bytes 1179648 | tf_op jit(solution)/shard_map/reduce_scatter | solution.py:70
  41.9 13.4 %copy-start.3 = (bf16[1,1,2,2,128,128]{5,4,3,2,1,0:T(8,128)(2,1)S(1)}, bf16[1,1,2,2,128,128]{5,4,3,2,1,0:T(8,128)(2,1)}, u32[]{:S(2)}) copy-start(bf16[1,1,2,2,128,128]{5,4,3,2,1,0:T(8,128)(2,1)} %param.7) | copy-start | bytes 393220
  76.8 1.0 copy-start
  77.7 27.5 %slice-start = ((s8[14680064]{0:T(1024)(128)(4,1)}), s8[4194304]{0:T(1024)(128)(4,1)S(1)}, s32[]{:S(2)}) async-start(s8[14680064]{0:T(1024)(128)(4,1)} %bitcast.77), calls=%async_computation.3 | async-start | bytes 8388608
  78.3 27.0 %slice-start.1 = ((s8[14680064]{0:T(1024)(128)(4,1)}), s8[4194304]{0:T(1024)(128)(4,1)S(1)}, s32[]{:S(2)}) async-start(s8[14680064]{0:T(1024)(128)(4,1)} %bitcast.77), calls=%async_computation.4 | async-start | bytes 8388608
  78.3 27.0 %slice-start.2 = ((s8[14680064]{0:T(1024)(128)(4,1)}), s8[4194304]{0:T(1024)(128)(4,1)S(1)}, s32[]{:S(2)}) async-start(s8[14680064]{0:T(1024)(128)(4,1)} %bitcast.77), calls=%async_computation.5 | async-start | bytes 8388608
  78.3 27.0 %slice-start.3 = ((s8[14680064]{0:T(1024)(128)(4,1)}), s8[2097152]{0:T(1024)(128)(4,1)S(1)}, s32[]{:S(2)}) async-start(s8[14680064]{0:T(1024)(128)(4,1)} %bitcast.77), calls=%async_computation.6 | async-start | bytes 4194304
  145.3 19.3 %copy-start.1 = (bf16[8,2,256,128]{2,3,1,0:T(8,128)(2,1)S(1)}, bf16[8,2,256,128]{2,3,1,0:T(8,128)(2,1)}, u32[]{:S(2)}) copy-start(bf16[8,2,256,128]{2,3,1,0:T(8,128)(2,1)} %copy-done) | copy-start | bytes 3145732
  152.6 12.0 %copy-start.2 = (bf16[8,2,256,128]{2,3,1,0:T(8,128)(2,1)S(1)}, bf16[8,2,256,128]{2,3,1,0:T(8,128)(2,1)}, u32[]{:S(2)}) copy-start(bf16[8,2,256,128]{2,3,1,0:T(8,128)(2,1)} %copy.105) | copy-start | bytes 3145732
Sparse Core Ops, SparseCore 0:
  10.1 35.8 all-gather.1
  166.2 31.9 reduce-scatter.1
where the time goes:
time: 268 us
  blocking collectives  129 us (48%)
  local copies, waits for them, and re-layouts  57.2 us (21%)
  matrix products  35.2 us (13%)
  other arithmetic  32.4 us (12%)
  between operations  14.2 us (5%)
    psum x1, blocking collectives, local(): token_grad = lax.psum(token_part, 'tensor').astype(jnp.bfloat16)  93.1 us
    dot_general x1, matrix products, slot_terms(): jnp.einsum('tsmn,smc->tmcn', products, col_table, precision=HIGHEST)  26.9 us
    unnamed x19, local copies, waits for them, and re-layouts  22 us
    convert_element_type x1, local copies, waits for them, and re-layouts, slot_terms(): grad_pair = jnp.stack([grad_gate, grad_up], axis=1).astype(jnp.bfloat16)  17.3 us
    all_gather x1, blocking collectives, local(): tile_all = lax.all_gather(tile_blocks, 'fsdp', axis=0, tiled=True)  14.9 us
    another operation x1, other arithmetic  14.6 us
    all_gather x1, blocking collectives, local(): lax.all_gather(tile_keep, 'fsdp', axis=0, tiled=True)  12.9 us
    unnamed x2, other arithmetic  10 us
  transfers between devices with their start and end apart: 2, of which 0 were waited for; matrix products, arithmetic and copies ran while one was open for 9% of the time, Pallas kernels for 0%

commit v1 on v0

v1 whole, which is shorter than its diff:
```python
import functools

import jax
import jax.numpy as jnp
from jax import lax
from jax.experimental import pallas as pl
from jax.experimental.pallas import tpu as pltpu
from jax.sharding import PartitionSpec as P

F32 = jnp.float32
BF16 = jnp.bfloat16
VMEM_BYTES = 56 * 2**20


def shift(axis, size, k):
    return [(i, (i + k) % size) for i in range(size)]


def loop(count, body):
    if count <= 8:
        for i in range(count):
            body(i)
    else:
        lax.fori_loop(0, count, lambda i, c: (body(i), c)[1], 0)


def compact(info, row, col, slot, cols):
    shards, width = info.shape
    cap = width // 2
    live = shards * cap // 2
    for m in range(2):
        p = jnp.int32(m * live)
        for k in range(shards):
            for j in range(cap):
                v = info[k, 2 * j + m]
                r = lax.div(v, jnp.int32(cols))
                row[p] = r
                if col is not None:
                    col[p] = v - r * cols
                    slot[p] = k * cap + j
                p = p + jnp.where(v >= 0, 1, 0).astype(jnp.int32)


def find_first(values, first, count):
    def one(i):
        v = values[i]

        def step(n, best):
            at = i - 1 - n
            return jnp.where(values[at] == v, at, best).astype(jnp.int32)

        if isinstance(i, int):
            best = jnp.int32(i)
            for n in range(i):
                best = step(n, best)
        else:
            best = lax.fori_loop(0, i, step, i)
        first[i] = best

    loop(count, one)


def dot(a, b, dims):
    return lax.dot_general(a, b, (dims, ((), ())), preferred_element_type=F32)


def tile_kernel(n_tensor, cols, info, *refs):
    xs, refs = refs[:n_tensor], refs[n_tensor:]
    hid, tiles, back, own, send = refs[:5]
    row, col, slot, cfirst, rfirst, xb, hb, pre, acc, tg, xsem, hsem = refs[5:]
    blk = tiles.shape[-1]
    live = row.shape[0] // 2
    count = 2 * live
    rows_here = xs[0].shape[1] // blk
    t = lax.axis_index("tensor")
    s = lax.axis_index("seq")
    compact(info, row, col, slot, cols)

    def copies(i):
        at = pl.multiple_of(lax.rem(row[i], rows_here) * blk, blk)
        ch = pl.multiple_of(col[i] * blk, blk)
        found = [
            pltpu.make_async_copy(x.at[:, pl.ds(at, blk)], xb.at[n, i], xsem.at[n, i])
            for n, x in enumerate(xs)
        ]
        return found + [pltpu.make_async_copy(hid.at[:, pl.ds(ch, blk)], hb.at[i], hsem.at[i])]

    def start(i):
        for c in copies(i):
            c.start()

    loop(count, start)
    find_first(col, cfirst, count)
    find_first(row, rfirst, count)
    pre[...] = jnp.zeros_like(pre)
    acc[...] = jnp.zeros_like(acc)
    tg[...] = jnp.zeros_like(tg)

    def x_of(i):
        part = lax.rem(lax.div(row[i], rows_here) - t + n_tensor, n_tensor)
        return xb[part, i]

    def forward(i):
        m = i // live
        for c in copies(i):
            c.wait()
        f = cfirst[i]
        pre[m, f] += dot(x_of(i), tiles[2 * slot[i] + m], ((1,), (0,)))

    loop(count, forward)

    def backward(i):
        m = i // live
        f = cfirst[i]
        gate = pre[0, f]
        h = hb[i].astype(F32)
        sig = 1.0 / (1.0 + jnp.exp(-gate))

        def of_gate():
            return h * pre[1, f] * sig * (1.0 + gate * (1.0 - sig))

        def of_up():
            return h * gate * sig

        if isinstance(m, int):
            grad = of_up() if m else of_gate()
        else:
            grad = jnp.where(m == 0, of_gate(), of_up())
        grad = grad.astype(BF16)
        w = tiles[2 * slot[i] + m]
        acc[rfirst[i]] += dot(grad, w, ((1,), (1,)))
        at = slot[i]
        tg[lax.rem(at, 2), lax.div(at, 2), m] = dot(x_of(i), grad, ((0,), (0,)))

    loop(count, backward)
    back[...] = acc[...].astype(BF16)
    own[...] = tg[s]
    send[...] = tg[1 - s]


def final_kernel(n_tensor, shards, cols, infos, *refs):
    parts, refs = refs[:n_tensor], refs[n_tensor:]
    mine, refs = refs[0], refs[1:]
    others, refs = refs[: shards - 1], refs[shards - 1 :]
    token_grad, tile_grads, row, wide = refs
    count, _, blk = parts[0].shape
    total = token_grad if n_tensor == 2 else wide
    total[...] = jnp.zeros_like(total)
    for n in range(n_tensor):
        compact(infos.at[n], row, None, None, cols)

        def add(i):
            at = pl.ds(pl.multiple_of(row[i] * blk, blk), blk)
            total[:, at] = (total[:, at].astype(F32) + parts[n][i].astype(F32)).astype(total.dtype)

        loop(count, add)
    if n_tensor != 2:
        token_grad[...] = wide[...].astype(BF16)
    tile_sum = mine[...]
    for other in others:
        tile_sum = tile_sum + other[...].astype(F32)
    tile_grads[...] = tile_sum.astype(BF16)


def local(sizes, tokens, hidden_grad, tile_blocks, tile_keep, tile_count):
    shards, n_tensor = sizes["fsdp"], sizes["tensor"]
    blk = tile_blocks.shape[-1]
    cap = tile_blocks.shape[2]
    toks = tokens.shape[0]
    width = tokens.shape[1] * n_tensor
    cols = hidden_grad.shape[1] // blk
    live = shards * cap // 2
    count = 2 * live
    vmem = pl.BlockSpec(memory_space=pltpu.VMEM)
    smem = pl.BlockSpec(memory_space=pltpu.SMEM)
    hbm = pl.BlockSpec(memory_space=pl.ANY)
    params = pltpu.CompilerParams(vmem_limit_bytes=VMEM_BYTES)

    is_live = jnp.arange(cap, dtype=jnp.int32)[None, :, None] < tile_count.reshape(1, 1, 2)
    info = jnp.where(is_live, tile_keep.reshape(1, cap, 2), -1).reshape(1, 2 * cap)
    tiles = tile_blocks.reshape(2 * cap, blk, blk)

    def from_shards(a):
        return [a] + [lax.ppermute(a, "fsdp", shift("fsdp", shards, k)) for k in range(1, shards)]

    xs = [tokens] + [
        lax.ppermute(tokens, "tensor", shift("tensor", n_tensor, n_tensor - k))
        for k in range(1, n_tensor)
    ]
    info_all = jnp.concatenate(from_shards(info), axis=0)
    tiles_all = jnp.concatenate(from_shards(tiles), axis=0)

    back, own, send = pl.pallas_call(
        functools.partial(tile_kernel, n_tensor, cols),
        out_shape=(
            jax.ShapeDtypeStruct((count, toks, blk), BF16),
            jax.ShapeDtypeStruct((shards, 2, blk, blk), F32),
            jax.ShapeDtypeStruct((shards, 2, blk, blk), F32),
        ),
        in_specs=[smem] + [hbm] * n_tensor + [hbm, vmem],
        out_specs=(vmem, vmem, vmem),
        scratch_shapes=[
            pltpu.SMEM((count + 1,), jnp.int32),
            pltpu.SMEM((count + 1,), jnp.int32),
            pltpu.SMEM((count + 1,), jnp.int32),
            pltpu.SMEM((count,), jnp.int32),
            pltpu.SMEM((count,), jnp.int32),
            pltpu.VMEM((n_tensor, count, toks, blk), BF16),
            pltpu.VMEM((count, toks, blk), BF16),
            pltpu.VMEM((2, count, toks, blk), F32),
            pltpu.VMEM((count, toks, blk), F32),
            pltpu.VMEM((cap, shards, 2, blk, blk), F32),
            pltpu.SemaphoreType.DMA((n_tensor, count)),
            pltpu.SemaphoreType.DMA((count,)),
        ],
        compiler_params=params,
        name="tile_terms",
    )(info_all, *xs, hidden_grad, tiles_all)

    if n_tensor == 2:
        swap = shift("tensor", 2, 1)
        parts = [back, lax.ppermute(back, "tensor", swap)]
        infos = jnp.stack([info_all, lax.ppermute(info_all, "tensor", swap)])
    else:
        gathered = lax.all_gather(back, "tensor")
        parts = [gathered[n] for n in range(n_tensor)]
        infos = lax.all_gather(info_all, "tensor")

    pair = own + lax.ppermute(send, "seq", shift("seq", 2, 1))
    rounded = pair.astype(BF16)
    others = [
        lax.ppermute(rounded[k], "fsdp", shift("fsdp", shards, shards - k)) for k in range(1, shards)
    ]

    token_grad, tile_grads = pl.pallas_call(
        functools.partial(final_kernel, n_tensor, shards, cols),
        out_shape=(
            jax.ShapeDtypeStruct((toks, width), BF16),
            jax.ShapeDtypeStruct((2, blk, blk), BF16),
        ),
        in_specs=[smem] + [vmem] * (n_tensor + shards),
        out_specs=(vmem, vmem),
        scratch_shapes=[
            pltpu.SMEM((count + 1,), jnp.int32),
            pltpu.VMEM((toks, width) if n_tensor != 2 else (8, 128), F32),
        ],
        compiler_params=params,
        name="assemble",
    )(infos, *parts, pair[0], *others)
    return token_grad, tile_grads.reshape(1, 1, 1, 2, blk, blk)


def solution(mesh):
    return jax.shard_map(
        functools.partial(local, dict(mesh.shape)),
        mesh=mesh,
        in_specs=(
            P(("group", "fsdp", "seq"), "tensor"),
            P(("group", "fsdp", "seq"), "tensor"),
            P("fsdp", "tensor", None, None, None, None),
            P("fsdp", "tensor", None, None),
            P("fsdp", "tensor", None),
        ),
        out_specs=(
            P(("group", "fsdp", "seq"), None),
            P(("group", "fsdp"), "tensor", "seq", None, None, None),
        ),
        check_vma=False,
    )
```

time: 268 us -> 57.5 us (0.21)
  blocking collectives: 129 us -> 0 us
  local copies, waits for them, and re-layouts: 57.2 us -> 4.67 us
  matrix products: 35.2 us -> 0 us
  other arithmetic: 32.4 us -> 4.09 us
  starting transfers between devices: 0.08 us -> 22.5 us
  waiting for transfers between devices: 0.04 us -> 16.3 us
  between operations: 14.2 us -> 0.72 us
  Pallas kernels: 0 us -> 8.9 us
    psum x1 -> x0, blocking collectives: 93.1 us -> none  [local(): token_grad = lax.psum(token_part, 'tensor').astype(jnp.bfloat16)]
    all_gather x3 -> x0, blocking collectives: 35.5 us -> none  [the longest x1 14.9 us: local(): tile_all = lax.all_gather(tile_blocks, 'fsdp', axis=0, tiled=True)]
    dot_general x5 -> x0, matrix products: 35.2 us -> none  [the longest x1 26.9 us: slot_terms(): jnp.einsum('tsmn,smc->tmcn', products, col_table, precision=HIGHEST)]
    ppermute x0 -> x13, starting transfers between devices: none -> 22.5 us  [the longest x6 12.8 us: from_shards(): lax.ppermute(a, 'fsdp', shift('fsdp', shards, k))]
    unnamed x19 -> x12, local copies, waits for them, and re-layouts: 22 us -> 2.41 us
    another operation x2, other arithmetic: 20.6 us -> 1.18 us  [local(): infos = jnp.stack([info_all, lax.ppermute(info_all, 'tensor', swap)])]
    convert_element_type x2 -> x0, local copies, waits for them, and re-layouts: 17.4 us -> none  [the longest x1 17.3 us: slot_terms(): grad_pair = jnp.stack([grad_gate, grad_up], axis=1).astype(jnp.bfloat16)]
    ppermute x0 -> x13, waiting for transfers between devices: none -> 16.3 us  [the longest x6 7.82 us: from_shards(): lax.ppermute(a, 'fsdp', shift('fsdp', shards, k))]
  transfers between devices with their start and end apart: 2 -> 13, of which waited for: 0 -> 5; matrix products, arithmetic and copies ran while one was open for 9% -> 11% of each run, Pallas kernels for 0% -> 0%
where the time goes in v1:
time: 57.5 us; the launch traced here: 57.2 us
  starting transfers between devices  22.5 us (39%)
  waiting for transfers between devices  16.3 us (28%)
  Pallas kernels  8.9 us (15%)
  local copies, waits for them, and re-layouts  4.67 us (8%)
  other arithmetic  4.09 us (7%)
  between operations  0.72 us (1%)
    ppermute x6, starting transfers between devices, from_shards(): lax.ppermute(a, 'fsdp', shift('fsdp', shards, k))  12.8 us
    ppermute x6, waiting for transfers between devices, from_shards(): lax.ppermute(a, 'fsdp', shift('fsdp', shards, k))  7.82 us
    ppermute x3, starting transfers between devices, local(): lax.ppermute(rounded[k], 'fsdp', shift('fsdp', shards, shards - k))  5.57 us
    pallas_call x1, Pallas kernels, local(): pl.pallas_call(functools.partial(tile_kernel, n_tensor, cols), out_shape=...  5.54 us
    ppermute x1, waiting for transfers between devices, local(): parts = [back, lax.ppermute(back, 'tensor', swap)]  5.41 us
    pallas_call x1, Pallas kernels, local(): pl.pallas_call(functools.partial(final_kernel, n_tensor, shards, cols), o...  3.36 us
    ppermute x1, waiting for transfers between devices, local(): infos = jnp.stack([info_all, lax.ppermute(info_all, 'tensor', swap)])  3.05 us
    ppermute x1, starting transfers between devices, local(): lax.ppermute(tokens, 'tensor', shift('tensor', n_tensor, n_tensor - k))  3 us
  transfers between devices with their start and end apart: 13, of which 5 were waited for; matrix products, arithmetic and copies ran while one was open for 11% of the time, Pallas kernels for 0%

profile of v1, /device:TPU:0, one launch (start us, length us, event | category | flops | bytes accessed | tf_op | source)
XLA Modules:
  0.0 57.2 jit_solution(17367514002766754925)
XLA Ops:
  0.6 3.0 %collective-permute-start.4 = (bf16[256,2048]{1,0:T(8,128)(2,1)}, bf16[256,2048]{1,0:T(8,128)(2,1)S(1)}, u32[]{:S(2)}, u32[]{:S(2)}) collective-permute-start(bf16[256,2048]{1,0:T(8,128)(2,1)} %refs_0_.1), channel_id=1, source_target_pairs={{0,2},{2,0},{1,3},{3,1},{4,6},{6,4},{5,7},{7,5},{8,10},{10,8},{9,1... | collective-permute-start | bytes 3145736 | tf_op jit(solution)/shard_map/ppermute | solution.py:187
  3.6 3.6 %collective-permute-start.7 = (bf16[4,128,128]{2,1,0:T(8,128)(2,1)}, bf16[4,128,128]{2,1,0:T(8,128)(2,1)S(1)}, u32[]{:S(2)}, u32[]{:S(2)}) collective-permute-start(bf16[4,128,128]{2,1,0:T(8,128)(2,1)} %bitcast.16), channel_id=1, source_target_pairs={{0,12},{4,0},{8,4},{12,8},{1,13},{5,1},{9,5},{13,9},{2,14},{6,2},{... | collective-permute-start | bytes 393224 | tf_op jit(solution)/shard_map/ppermute | solution.py:184
  7.2 1.0 %collective-permute-start.5 = (bf16[4,128,128]{2,1,0:T(8,128)(2,1)}, bf16[4,128,128]{2,1,0:T(8,128)(2,1)S(1)}, u32[]{:S(2)}, u32[]{:S(2)}) collective-permute-start(bf16[4,128,128]{2,1,0:T(8,128)(2,1)} %bitcast.18), channel_id=1, source_target_pairs={{0,4},{4,8},{8,12},{12,0},{1,5},{5,9},{9,13},{13,1},{2,6},{6,10},{... | collective-permute-start | bytes 393224 | tf_op jit(solution)/shard_map/ppermute | solution.py:184
  8.2 0.8 %reshape.55 = s32[1,4]{1,0:T(1,128)S(1)} reshape(s32[1,1,2,2]{3,2,1,0:T(2,128)} %param.8) | data formatting | bytes 32 | tf_op jit(solution)/shard_map/reshape | solution.py:180
  9.0 0.7 %lt.31 = s32[2,2]{1,0:T(2,128)S(1)} broadcast(s32[2]{0:T(128)} %bitcast.22), dimensions={1} | broadcast | bytes 24 | tf_op jit(solution)/shard_map/lt | solution.py:179
  9.8 2.8 %collective-permute-start.2 = (s32[1,4]{1,0:T(1,128)S(1)}, s32[1,4]{1,0:T(1,128)S(1)}, u32[]{:S(2)}, u32[]{:S(2)}) collective-permute-start(s32[1,4]{1,0:T(1,128)S(1)} %compare_select_fusion), channel_id=1, source_target_pairs={{0,12},{4,0},{8,4},{12,8},{1,13},{5,1},{9,5},{13,9},{2,14},{6,2},{... | collective-permute-start | bytes 56 | tf_op jit(solution)/shard_map/ppermute | solution.py:184
  12.7 3.0 %collective-permute-done.2 = s32[1,4]{1,0:T(1,128)S(1)} collective-permute-done((s32[1,4]{1,0:T(1,128)S(1)}, s32[1,4]{1,0:T(1,128)S(1)}, u32[]{:S(2)}, u32[]{:S(2)}) %collective-permute-start.2) | collective-permute-done | bytes 48 | tf_op jit(solution)/shard_map/ppermute | solution.py:184
  15.7 2.2 %collective-permute-start.1 = (s32[1,4]{1,0:T(1,128)S(1)}, s32[1,4]{1,0:T(1,128)S(1)}, u32[]{:S(2)}, u32[]{:S(2)}) collective-permute-start(s32[1,4]{1,0:T(1,128)S(1)} %compare_select_fusion), channel_id=1, source_target_pairs={{0,8},{4,12},{8,0},{12,4},{1,9},{5,13},{9,1},{13,5},{2,10},{6,14},... | collective-permute-start | bytes 56 | tf_op jit(solution)/shard_map/ppermute | solution.py:184
  17.9 2.2 %collective-permute-done.1 = s32[1,4]{1,0:T(1,128)S(1)} collective-permute-done((s32[1,4]{1,0:T(1,128)S(1)}, s32[1,4]{1,0:T(1,128)S(1)}, u32[]{:S(2)}, u32[]{:S(2)}) %collective-permute-start.1) | collective-permute-done | bytes 48 | tf_op jit(solution)/shard_map/ppermute | solution.py:184
  20.1 3.1 %collective-permute-start = (s32[1,4]{1,0:T(1,128)S(1)}, s32[1,4]{1,0:T(1,128)S(1)}, u32[]{:S(2)}, u32[]{:S(2)}) collective-permute-start(s32[1,4]{1,0:T(1,128)S(1)} %compare_select_fusion), channel_id=1, source_target_pairs={{0,4},{4,8},{8,12},{12,0},{1,5},{5,9},{9,13},{13,1},{2,6},{6,10},{... | collective-permute-start | bytes 56 | tf_op jit(solution)/shard_map/ppermute | solution.py:184
  23.2 2.6 %collective-permute-done = s32[1,4]{1,0:T(1,128)S(1)} collective-permute-done((s32[1,4]{1,0:T(1,128)S(1)}, s32[1,4]{1,0:T(1,128)S(1)}, u32[]{:S(2)}, u32[]{:S(2)}) %collective-permute-start) | collective-permute-done | bytes 48 | tf_op jit(solution)/shard_map/ppermute | solution.py:184
  26.4 1.8 %pad_maximum_fusion.refs_3_ = bf16[16,128,128]{2,1,0:T(8,128)(2,1)} fusion(bf16[4,128,128]{2,1,0:T(8,128)(2,1)S(1)} %collective-permute-done.7, bf16[4,128,128]{2,1,0:T(8,128)(2,1)S(1)} %collective-permute-done.6, bf16[4,128,128]{2,1,0:T(8,128)(2,1)S(1)} %collective-permute-done.5, bf16[4,128,128]{2,1,0:T(8,128)(2,1)} %bitcast.19), kind=kLoop, calls=%fused_computation | loop fusion | flops 786432 | bytes 1048576 | tf_op jit(solution)/shard_map/concatenate | solution.py:191
  28.2 1.0 %copy-done = bf16[256,2048]{1,0:T(8,128)(2,1)} copy-done((bf16[256,2048]{1,0:T(8,128)(2,1)}, bf16[256,2048]{1,0:T(8,128)(2,1)S(1)}, u32[]{:S(2)}) %copy-start) | copy-done | bytes 1048600
  29.2 5.5 %tile_terms.1 = (bf16[8,256,128]{2,1,0:T(8,128)(2,1)}, f32[4,2,128,128]{3,2,1,0:T(8,128)}, f32[4,2,128,128]{3,2,1,0:T(8,128)}) custom-call(s32[4,4]{1,0:T(4,128)} %get-tuple-element.18.info, bf16[256,2048]{1,0:T(8,128)(2,1)} %refs_0_.1, bf16[256,2048]{1,0:T(8,128)(2,1)} %copy-done, bf16[256,14336]{1,0:T(8,128)(2,1)} %refs_2_.1, ...), custom_call_target="tpu_custom_call" | custom-call | tf_op jit(solution)/shard_map/tile_terms/pallas_call | solution.py:193
  35.4 3.0 %collective-permute-done.3 = s32[4,4]{1,0:T(4,128)S(1)} collective-permute-done((s32[4,4]{1,0:T(4,128)S(1)}, s32[4,4]{1,0:T(4,128)S(1)}, u32[]{:S(2)}, u32[]{:S(2)}) %collective-permute-start.3) | collective-permute-done | bytes 96 | tf_op jit(solution)/shard_map/ppermute | solution.py:223
  39.6 1.1 %fusion.1 = (bf16[4,2,128,128]{3,2,1,0:T(8,128)(2,1)S(1)}, f32[4,2,128,128]{3,2,1,0:T(8,128)S(1)}) fusion(f32[4,2,128,128]{3,2,1,0:T(8,128)} %get-tuple-element.8, f32[4,2,128,128]{3,2,1,0:T(8,128)S(1)} %collective-permute-done.9), kind=kLoop, calls=%fused_computation.9 | loop fusion | flops 262144 | bytes 1835008 | tf_op jit(solution)/shard_map/convert_element_type | solution.py:230
  40.7 1.6 %collective-permute-start.12 = (bf16[2,128,128]{2,1,0:T(8,128)(2,1)S(1)}, bf16[2,128,128]{2,1,0:T(8,128)(2,1)S(1)}, u32[]{:S(2)}, u32[]{:S(2)}) collective-permute-start(bf16[2,128,128]{2,1,0:T(8,128)(2,1)S(1)} %get-tuple-element.14), channel_id=1, source_target_pairs={{0,4},{4,8},{8,12},{12,0},{1,5},{5,9},{9,13},{13,1},{2,6},{6,10},{... | collective-permute-start | bytes 196616 | tf_op jit(solution)/shard_map/ppermute | solution.py:232
  42.4 2.6 %collective-permute-start.11 = (bf16[2,128,128]{2,1,0:T(8,128)(2,1)S(1)}, bf16[2,128,128]{2,1,0:T(8,128)(2,1)S(1)}, u32[]{:S(2)}, u32[]{:S(2)}) collective-permute-start(bf16[2,128,128]{2,1,0:T(8,128)(2,1)S(1)} %get-tuple-element.15), channel_id=1, source_target_pairs={{0,8},{4,12},{8,0},{12,4},{1,9},{5,13},{9,1},{13,5},{2,10},{6,14},... | collective-permute-start | bytes 196616 | tf_op jit(solution)/shard_map/ppermute | solution.py:232
  45.0 1.3 %collective-permute-start.10 = (bf16[2,128,128]{2,1,0:T(8,128)(2,1)S(1)}, bf16[2,128,128]{2,1,0:T(8,128)(2,1)S(1)}, u32[]{:S(2)}, u32[]{:S(2)}) collective-permute-start(bf16[2,128,128]{2,1,0:T(8,128)(2,1)S(1)} %get-tuple-element.16), channel_id=1, source_target_pairs={{0,12},{4,0},{8,4},{12,8},{1,13},{5,1},{9,5},{13,9},{2,14},{6,2},{... | collective-permute-start | bytes 196616 | tf_op jit(solution)/shard_map/ppermute | solution.py:232
  46.3 0.7 %slice_bitcast_fusion.refs_2_ = f32[2,128,128]{2,1,0:T(8,128)} fusion(f32[4,2,128,128]{3,2,1,0:T(8,128)S(1)} %get-tuple-element.13), kind=kLoop, calls=%fused_computation.1 | loop fusion | bytes 262144 | tf_op jit(solution)/shard_map/squeeze | solution.py:249
  47.0 5.4 %collective-permute-done.8.refs_1_ = bf16[8,256,128]{2,1,0:T(8,128)(2,1)S(1)} collective-permute-done((bf16[8,256,128]{2,1,0:T(8,128)(2,1)}, bf16[8,256,128]{2,1,0:T(8,128)(2,1)S(1)}, u32[]{:S(2)}, u32[]{:S(2)}) %collective-permute-start.8) | collective-permute-done | bytes 524320 | tf_op jit(solution)/shard_map/ppermute | solution.py:222
  52.4 0.8 %copy-done.1 = bf16[8,256,128]{2,1,0:T(8,128)(2,1)} copy-done((bf16[8,256,128]{2,1,0:T(8,128)(2,1)}, bf16[8,256,128]{2,1,0:T(8,128)(2,1)S(1)}, u32[]{:S(2)}) %copy-start.1) | copy-done | bytes 524312
  53.2 0.6 %copy-done.4 = bf16[2,128,128]{2,1,0:T(8,128)(2,1)} copy-done((bf16[2,128,128]{2,1,0:T(8,128)(2,1)}, bf16[2,128,128]{2,1,0:T(8,128)(2,1)S(1)}, u32[]{:S(2)}) %copy-start.4) | copy-done | bytes 65560
  53.8 3.4 %assemble.1 = (bf16[256,4096]{1,0:T(8,128)(2,1)}, bf16[2,128,128]{2,1,0:T(8,128)(2,1)}) custom-call(s32[2,4,4]{2,1,0:T(4,128)} %pad_add_fusion.infos, bf16[8,256,128]{2,1,0:T(8,128)(2,1)} %get-tuple-element.7.refs_0_, bf16[8,256,128]{2,1,0:T(8,128)(2,1)} %copy-done.1, f32[2,128,128]{2,1,0:T(8,128)} %slice_bitcast_fusion.refs_2_, ...), custom_call_target="tpu_custom_call" | custom-call | tf_op jit(solution)/shard_map/assemble/pallas_call | solution.py:235
  (28 shorter events, 2.7 us)
Async XLA Ops:
  0.6 27.6 %collective-permute-start.4 = (bf16[256,2048]{1,0:T(8,128)(2,1)}, bf16[256,2048]{1,0:T(8,128)(2,1)S(1)}, u32[]{:S(2)}, u32[]{:S(2)}) collective-permute-start(bf16[256,2048]{1,0:T(8,128)(2,1)} %refs_0_.1), channel_id=1, source_target_pairs={{0,2},{2,0},{1,3},{3,1},{4,6},{6,4},{5,7},{7,5},{8,10},{10,8},{9,1... | collective-permute-start | bytes 3145736 | tf_op jit(solution)/shard_map/ppermute | solution.py:187
  3.6 22.8 %collective-permute-start.7 = (bf16[4,128,128]{2,1,0:T(8,128)(2,1)}, bf16[4,128,128]{2,1,0:T(8,128)(2,1)S(1)}, u32[]{:S(2)}, u32[]{:S(2)}) collective-permute-start(bf16[4,128,128]{2,1,0:T(8,128)(2,1)} %bitcast.16), channel_id=1, source_target_pairs={{0,12},{4,0},{8,4},{12,8},{1,13},{5,1},{9,5},{13,9},{2,14},{6,2},{... | collective-permute-start | bytes 393224 | tf_op jit(solution)/shard_map/ppermute | solution.py:184
  7.2 19.2 %collective-permute-start.6 = (bf16[4,128,128]{2,1,0:T(8,128)(2,1)}, bf16[4,128,128]{2,1,0:T(8,128)(2,1)S(1)}, u32[]{:S(2)}, u32[]{:S(2)}) collective-permute-start(bf16[4,128,128]{2,1,0:T(8,128)(2,1)} %bitcast.17), channel_id=1, source_target_pairs={{0,8},{4,12},{8,0},{12,4},{1,9},{5,13},{9,1},{13,5},{2,10},{6,14},... | collective-permute-start | bytes 393224 | tf_op jit(solution)/shard_map/ppermute | solution.py:184
  7.2 19.2 %collective-permute-start.5 = (bf16[4,128,128]{2,1,0:T(8,128)(2,1)}, bf16[4,128,128]{2,1,0:T(8,128)(2,1)S(1)}, u32[]{:S(2)}, u32[]{:S(2)}) collective-permute-start(bf16[4,128,128]{2,1,0:T(8,128)(2,1)} %bitcast.18), channel_id=1, source_target_pairs={{0,4},{4,8},{8,12},{12,0},{1,5},{5,9},{9,13},{13,1},{2,6},{6,10},{... | collective-permute-start | bytes 393224 | tf_op jit(solution)/shard_map/ppermute | solution.py:184
  9.8 5.8 %collective-permute-start.2 = (s32[1,4]{1,0:T(1,128)S(1)}, s32[1,4]{1,0:T(1,128)S(1)}, u32[]{:S(2)}, u32[]{:S(2)}) collective-permute-start(s32[1,4]{1,0:T(1,128)S(1)} %compare_select_fusion), channel_id=1, source_target_pairs={{0,12},{4,0},{8,4},{12,8},{1,13},{5,1},{9,5},{13,9},{2,14},{6,2},{... | collective-permute-start | bytes 56 | tf_op jit(solution)/shard_map/ppermute | solution.py:184
  15.7 4.4 %collective-permute-start.1 = (s32[1,4]{1,0:T(1,128)S(1)}, s32[1,4]{1,0:T(1,128)S(1)}, u32[]{:S(2)}, u32[]{:S(2)}) collective-permute-start(s32[1,4]{1,0:T(1,128)S(1)} %compare_select_fusion), channel_id=1, source_target_pairs={{0,8},{4,12},{8,0},{12,4},{1,9},{5,13},{9,1},{13,5},{2,10},{6,14},... | collective-permute-start | bytes 56 | tf_op jit(solution)/shard_map/ppermute | solution.py:184
  20.1 5.7 %collective-permute-start = (s32[1,4]{1,0:T(1,128)S(1)}, s32[1,4]{1,0:T(1,128)S(1)}, u32[]{:S(2)}, u32[]{:S(2)}) collective-permute-start(s32[1,4]{1,0:T(1,128)S(1)} %compare_select_fusion), channel_id=1, source_target_pairs={{0,4},{4,8},{8,12},{12,0},{1,5},{5,9},{9,13},{13,1},{2,6},{6,10},{... | collective-permute-start | bytes 56 | tf_op jit(solution)/shard_map/ppermute | solution.py:184
  26.4 8.4 %copy-start.5 = (s32[4,4]{1,0:T(4,128)S(1)}, s32[4,4]{1,0:T(4,128)}, u32[]{:S(2)}) copy-start(s32[4,4]{1,0:T(4,128)} %get-tuple-element.18.info) | copy-start | bytes 196
  28.2 1.0 %copy-start = (bf16[256,2048]{1,0:T(8,128)(2,1)}, bf16[256,2048]{1,0:T(8,128)(2,1)S(1)}, u32[]{:S(2)}) copy-start(bf16[256,2048]{1,0:T(8,128)(2,1)S(1)} %collective-permute-done.4.refs_1_) | copy-start | bytes 3145732
  34.7 4.9 %collective-permute-start.9 = (f32[4,2,128,128]{3,2,1,0:T(8,128)}, f32[4,2,128,128]{3,2,1,0:T(8,128)S(1)}, u32[]{:S(2)}, u32[]{:S(2)}) collective-permute-start(f32[4,2,128,128]{3,2,1,0:T(8,128)} %get-tuple-element.9), channel_id=1, source_target_pairs={{0,1},{1,0},{2,3},{3,2},{4,5},{5,4},{6,7},{7,6},{8,9},{9,8},{10,11... | collective-permute-start | bytes 1572872 | tf_op jit(solution)/shard_map/ppermute | solution.py:229
  34.8 3.7 %collective-permute-start.3 = (s32[4,4]{1,0:T(4,128)S(1)}, s32[4,4]{1,0:T(4,128)S(1)}, u32[]{:S(2)}, u32[]{:S(2)}) collective-permute-start(s32[4,4]{1,0:T(4,128)S(1)} %copy-done.5), channel_id=1, source_target_pairs={{0,2},{2,0},{1,3},{3,1},{4,6},{6,4},{5,7},{7,5},{8,10},{10,8},{9,1... | collective-permute-start | bytes 200 | tf_op jit(solution)/shard_map/ppermute | solution.py:223
  39.0 13.3 %collective-permute-start.8 = (bf16[8,256,128]{2,1,0:T(8,128)(2,1)}, bf16[8,256,128]{2,1,0:T(8,128)(2,1)S(1)}, u32[]{:S(2)}, u32[]{:S(2)}) collective-permute-start(bf16[8,256,128]{2,1,0:T(8,128)(2,1)} %get-tuple-element.7.refs_0_), channel_id=1, source_target_pairs={{0,2},{2,0},{1,3},{3,1},{4,6},{6,4},{5,7},{7,5},{8,10},{10,8},{9,1... | collective-permute-start | bytes 1572872 | tf_op jit(solution)/shard_map/ppermute | solution.py:222
  40.7 11.6 %collective-permute-start.12 = (bf16[2,128,128]{2,1,0:T(8,128)(2,1)S(1)}, bf16[2,128,128]{2,1,0:T(8,128)(2,1)S(1)}, u32[]{:S(2)}, u32[]{:S(2)}) collective-permute-start(bf16[2,128,128]{2,1,0:T(8,128)(2,1)S(1)} %get-tuple-element.14), channel_id=1, source_target_pairs={{0,4},{4,8},{8,12},{12,0},{1,5},{5,9},{9,13},{13,1},{2,6},{6,10},{... | collective-permute-start | bytes 196616 | tf_op jit(solution)/shard_map/ppermute | solution.py:232
  42.4 10.0 %collective-permute-start.11 = (bf16[2,128,128]{2,1,0:T(8,128)(2,1)S(1)}, bf16[2,128,128]{2,1,0:T(8,128)(2,1)S(1)}, u32[]{:S(2)}, u32[]{:S(2)}) collective-permute-start(bf16[2,128,128]{2,1,0:T(8,128)(2,1)S(1)} %get-tuple-element.15), channel_id=1, source_target_pairs={{0,8},{4,12},{8,0},{12,4},{1,9},{5,13},{9,1},{13,5},{2,10},{6,14},... | collective-permute-start | bytes 196616 | tf_op jit(solution)/shard_map/ppermute | solution.py:232
  45.0 7.4 %collective-permute-start.10 = (bf16[2,128,128]{2,1,0:T(8,128)(2,1)S(1)}, bf16[2,128,128]{2,1,0:T(8,128)(2,1)S(1)}, u32[]{:S(2)}, u32[]{:S(2)}) collective-permute-start(bf16[2,128,128]{2,1,0:T(8,128)(2,1)S(1)} %get-tuple-element.16), channel_id=1, source_target_pairs={{0,12},{4,0},{8,4},{12,8},{1,13},{5,1},{9,5},{13,9},{2,14},{6,2},{... | collective-permute-start | bytes 196616 | tf_op jit(solution)/shard_map/ppermute | solution.py:232
  52.4 0.8 %copy-start.1 = (bf16[8,256,128]{2,1,0:T(8,128)(2,1)}, bf16[8,256,128]{2,1,0:T(8,128)(2,1)S(1)}, u32[]{:S(2)}) copy-start(bf16[8,256,128]{2,1,0:T(8,128)(2,1)S(1)} %collective-permute-done.8.refs_1_) | copy-start | bytes 1572868
  52.4 0.8 %copy-start.2 = (bf16[2,128,128]{2,1,0:T(8,128)(2,1)}, bf16[2,128,128]{2,1,0:T(8,128)(2,1)S(1)}, u32[]{:S(2)}) copy-start(bf16[2,128,128]{2,1,0:T(8,128)(2,1)S(1)} %collective-permute-done.12.refs_5_) | copy-start | bytes 196612
  52.4 0.8 %copy-start.3 = (bf16[2,128,128]{2,1,0:T(8,128)(2,1)}, bf16[2,128,128]{2,1,0:T(8,128)(2,1)S(1)}, u32[]{:S(2)}) copy-start(bf16[2,128,128]{2,1,0:T(8,128)(2,1)S(1)} %collective-permute-done.11.refs_4_) | copy-start | bytes 196612
  53.2 0.6 %copy-start.4 = (bf16[2,128,128]{2,1,0:T(8,128)(2,1)}, bf16[2,128,128]{2,1,0:T(8,128)(2,1)S(1)}, u32[]{:S(2)}) copy-start(bf16[2,128,128]{2,1,0:T(8,128)(2,1)S(1)} %collective-permute-done.10.refs_3_) | copy-start | bytes 196612

commit v2 on v1

v2 whole, which is shorter than its diff:
```python
import functools

import jax
import jax.numpy as jnp
from jax import lax
from jax.experimental import pallas as pl
from jax.experimental.pallas import tpu as pltpu
from jax.sharding import PartitionSpec as P

F32 = jnp.float32
BF16 = jnp.bfloat16
I32 = jnp.int32
ROW, COL, SLOT, CFIRST, RFIRST = range(5)
INFO_ROWS = 16


def shift(size, k):
    return [(i, (i + k) % size) for i in range(size)]


def swaps(size, k):
    return [(i, i ^ k) for i in range(size)]


def loop(count, body):
    if count <= 8:
        for i in range(count):
            body(i)
    else:
        lax.fori_loop(0, count, lambda i, c: (body(i), c)[1], 0)


def find_first(table, src, dst, count):
    def one(i):
        v = table[src, i]

        def step(n, best):
            at = i - 1 - n
            return jnp.where(table[src, at] == v, at, best).astype(I32)

        if isinstance(i, int):
            best = jnp.int32(i)
            for n in range(i):
                best = step(n, best)
        else:
            best = lax.fori_loop(0, i, step, i)
        table[dst, i] = best

    loop(count, one)


def cost(us):
    return pl.CostEstimate(flops=0, bytes_accessed=int(us * 3.69e6), transcendentals=0)


def dot(a, b, dims):
    return lax.dot_general(a, b, (dims, ((), ())), preferred_element_type=F32)


def pack_kernel(cols, keep, count, tiles, packed):
    _, _, cap, _, blk, _ = tiles.shape
    for j in range(cap):
        for m in range(2):
            packed[pl.ds((2 * j + m) * blk, blk), :] = tiles[0, 0, j, m]
    line = lax.broadcasted_iota(I32, (INFO_ROWS, blk), 0)
    lane = lax.broadcasted_iota(I32, (INFO_ROWS, blk), 1)
    info = jnp.zeros((INFO_ROWS, blk), I32)
    for j in range(cap):
        for m in range(2):
            b = keep[0, 0, j, m]
            r = lax.div(b, jnp.int32(cols))
            c = b - r * cols
            r = jnp.where(j < count[0, 0, m], r, -1)
            here = lane == 2 * j + m
            info = jnp.where(here & (line == 0), r, jnp.where(here & (line == 1), c, info))
    packed[pl.ds(2 * cap * blk, INFO_ROWS), :] = info.astype(F32).astype(BF16)


def prepare_kernel(shards, cap, *refs):
    packed, refs = refs[:shards], refs[shards:]
    tokens, hidden, table, weights, xo, hb, ints, info, isem, xsem, hsem = refs
    blk = weights.shape[-1]
    base = 2 * cap * blk
    rows_here = tokens.shape[1] // blk
    count = xo.shape[0]
    live = count // 2
    for k in range(shards):
        ints[k] = packed[k][pl.ds(base, INFO_ROWS), :].astype(F32)[:8].astype(I32)
    fetch = pltpu.make_async_copy(ints, info, isem)
    fetch.start()
    fetch.wait()
    for m in range(2):
        p = jnp.int32(m * live)
        for k in range(shards):
            for j in range(cap):
                r = info[k, 0, 2 * j + m]
                table[ROW, p] = r
                table[COL, p] = info[k, 1, 2 * j + m]
                table[SLOT, p] = k * cap + j
                weights[p] = packed[k][pl.ds((2 * j + m) * blk, blk), :]
                p = p + jnp.where(r >= 0, 1, 0).astype(I32)

    def copies(i):
        at = pl.multiple_of(lax.rem(table[ROW, i], rows_here) * blk, blk)
        ch = pl.multiple_of(table[COL, i] * blk, blk)
        return (
            pltpu.make_async_copy(tokens.at[:, pl.ds(at, blk)], xo.at[i], xsem.at[i]),
            pltpu.make_async_copy(hidden.at[:, pl.ds(ch, blk)], hb.at[i], hsem.at[i]),
        )

    def start(i):
        for c in copies(i):
            c.start()

    def wait(i):
        for c in copies(i):
            c.wait()

    loop(count, start)
    find_first(table, COL, CFIRST, count)
    find_first(table, ROW, RFIRST, count)
    loop(count, wait)


def forward_backward(lo, table, weights, xo, hb, remote, xs, pre, grads):
    count, size, blk = xs.shape
    live = count // 2
    rows_here = remote[0].shape[1] // blk
    n_tensor = len(remote) + 1
    t = lax.axis_index("tensor")
    pre[...] = jnp.zeros_like(pre)

    def forward(i):
        r = table[ROW, i]
        part = lax.rem(lax.div(r, rows_here) - t + n_tensor, n_tensor)
        at = pl.multiple_of(lax.rem(r, rows_here) * blk, blk)
        x = xo[i, pl.ds(lo, size), :]
        for n, ref in enumerate(remote):
            x = jnp.where(part == n + 1, ref[:, pl.ds(at, blk)], x)
        xs[i] = x
        pre[i // live, table[CFIRST, i]] += dot(x, weights[i], ((1,), (0,)))

    loop(count, forward)

    def backward(i):
        m = i // live
        f = table[CFIRST, i]
        gate = pre[0, f]
        h = hb[i, pl.ds(lo, size), :].astype(F32)
        sig = 1.0 / (1.0 + jnp.exp(-gate))

        def of_gate():
            return h * pre[1, f] * sig * (1.0 + gate * (1.0 - sig))

        def of_up():
            return h * gate * sig

        if isinstance(m, int):
            grad = of_up() if m else of_gate()
        else:
            grad = jnp.where(m == 0, of_gate(), of_up())
        grads[i] = grad.astype(BF16)

    loop(count, backward)


def back_terms(table, weights, grads, acc, back):
    count, size, _ = acc.shape
    acc[...] = jnp.zeros_like(acc)

    def one(i):
        acc[table[RFIRST, i]] += dot(grads[i], weights[i], ((1,), (1,)))

    def put(i):
        back[pl.ds(pl.multiple_of(i * size, size), size), :] = acc[i].astype(BF16)

    loop(count, one)
    loop(count, put)


def first_kernel(n_tensor, table, weights, xo, hb, *refs):
    remote, refs = refs[: n_tensor - 1], refs[n_tensor - 1 :]
    back, tile_sums, xs, pre, grads, acc = refs
    forward_backward(0, table, weights, xo, hb, remote, xs, pre, grads)

    def tile(i):
        tile_sums[i] = dot(xs[i], grads[i], ((0,), (0,)))

    count, size, blk = xs.shape
    loop(count, tile)
    back_terms(table, weights, grads, acc, back)
    lane = lax.broadcasted_iota(I32, (INFO_ROWS, blk), 1)
    rows = jnp.zeros((INFO_ROWS, blk), I32)
    for i in range(count):
        rows = jnp.where(lane == i, table[ROW, i], rows)
    back[pl.ds(count * size, INFO_ROWS), :] = rows.astype(F32).astype(BF16)


def second_kernel(n_tensor, lo, cap, table, weights, xo, hb, tile_sums, *refs):
    remote, refs = refs[: n_tensor - 1], refs[n_tensor - 1 :]
    own, send, grads, xs, pre, both = refs
    forward_backward(lo, table, weights, xo, hb, remote, xs, pre, grads)
    both[...] = jnp.zeros_like(both)
    s = lax.axis_index("seq")
    live = xs.shape[0] // 2

    def tile(i):
        value = tile_sums[i] + dot(xs[i], grads[i], ((0,), (0,)))
        slot = table[SLOT, i]
        both[lax.rem(slot + s, cap), lax.div(slot, cap), i // live] = value

    loop(xs.shape[0], tile)
    own[...] = both[0]
    send[...] = both[1].astype(send.dtype)


def back_kernel(table, weights, grads, back, acc):
    back_terms(table, weights, grads, acc, back)


def add_blocks(rows, parts, count, block, wide, out, lo, sem):
    size = block.shape[0]
    blk = parts[0].shape[1]
    n_tensor = len(parts)
    total = block if n_tensor == 2 else wide
    total[...] = jnp.zeros_like(total)
    for n, part in enumerate(parts):

        def add(i):
            at = pl.ds(pl.multiple_of(rows[n, i] * blk, blk), blk)
            term = part[pl.ds(pl.multiple_of(i * size, size), size), :].astype(F32)
            total[:, at] = (total[:, at].astype(F32) + term).astype(total.dtype)

        loop(count, add)
    if n_tensor != 2:
        block[...] = wide[...].astype(BF16)
    copy = pltpu.make_async_copy(block, out.at[pl.ds(lo, size), :], sem)
    copy.start()
    return copy


def place_early_kernel(n_tensor, count, *refs):
    parts, refs = refs[:n_tensor], refs[n_tensor:]
    out, rows, ints, info, block, wide, isem, sem = refs
    size = block.shape[0]
    for n, part in enumerate(parts):
        ints[n] = part[pl.ds(count * size, INFO_ROWS), :].astype(F32)[:8].astype(I32)
    fetch = pltpu.make_async_copy(ints, info, isem)
    fetch.start()
    fetch.wait()
    for n in range(n_tensor):
        for i in range(count):
            rows[n, i] = info[n, 0, i]
    add_blocks(rows, parts, count, block, wide, out, 0, sem).wait()


def place_late_kernel(n_tensor, lo, count, rows, *refs):
    parts, refs = refs[:n_tensor], refs[n_tensor:]
    _, mine, *others, out, tile_grads, block, wide, sem = refs
    copy = add_blocks(rows, parts, count, block, wide, out, lo, sem)
    tile_sum = mine[...]
    for other in others:
        tile_sum = tile_sum + other[...].astype(F32)
    tile_grads[...] = tile_sum.astype(BF16)
    copy.wait()


def local(sizes, tokens, hidden_grad, tile_blocks, tile_keep, tile_count):
    shards, n_tensor = sizes["fsdp"], sizes["tensor"]
    blk = tile_blocks.shape[-1]
    cap = tile_blocks.shape[2]
    toks = tokens.shape[0]
    width = tokens.shape[1] * n_tensor
    cols = hidden_grad.shape[1] // blk
    count = shards * cap
    cut = toks * 3 // 4 // 16 * 16
    rest = toks - cut
    vmem = pl.BlockSpec(memory_space=pltpu.VMEM)
    smem = pl.BlockSpec(memory_space=pltpu.SMEM)
    hbm = pl.BlockSpec(memory_space=pltpu.HBM)
    spare = pltpu.CompilerParams(vmem_limit_bytes=(16 if count <= 8 else 40) * 2**20)
    swap = shift(2, 1)

    def shape(dims, kind):
        return jax.ShapeDtypeStruct(dims, kind)

    def to_partners(a):
        return [
            lax.ppermute(a, "tensor", shift(n_tensor, n_tensor - k)) for k in range(1, n_tensor)
        ]

    early = to_partners(tokens[:cut])
    packed = pl.pallas_call(
        functools.partial(pack_kernel, cols),
        out_shape=shape((2 * cap * blk + INFO_ROWS, blk), BF16),
        in_specs=[smem, smem, vmem],
        out_specs=vmem,
        compiler_params=spare,
        cost_estimate=cost(0.001),
        name="pack",
    )(tile_keep, tile_count, tile_blocks)
    late = to_partners(tokens[cut:])
    gathered = [packed] + [
        lax.ppermute(packed, "fsdp", swaps(shards, k)) for k in range(1, shards)
    ]

    table, weights, xo, hb = pl.pallas_call(
        functools.partial(prepare_kernel, shards, cap),
        out_shape=(
            shape((5, count + 1), I32),
            shape((count + 1, blk, blk), BF16),
            shape((count, toks, blk), BF16),
            shape((count, toks, blk), BF16),
        ),
        in_specs=[vmem] * shards + [hbm, hbm],
        out_specs=(smem, vmem, vmem, vmem),
        scratch_shapes=[
            pltpu.VMEM((shards, 8, blk), I32),
            pltpu.SMEM((shards, 8, blk), I32),
            pltpu.SemaphoreType.DMA,
            pltpu.SemaphoreType.DMA((count,)),
            pltpu.SemaphoreType.DMA((count,)),
        ],
        compiler_params=pltpu.CompilerParams(vmem_limit_bytes=50 * 2**20),
        cost_estimate=cost(0.001),
        name="prepare",
    )(*gathered, tokens, hidden_grad)

    back_early, tile_sums = pl.pallas_call(
        functools.partial(first_kernel, n_tensor),
        out_shape=(shape((count * cut + INFO_ROWS, blk), BF16), shape((count, blk, blk), F32)),
        in_specs=[smem] + [vmem] * (2 + n_tensor),
        out_specs=(vmem, vmem),
        scratch_shapes=[
            pltpu.VMEM((count, cut, blk), BF16),
            pltpu.VMEM((2, count, cut, blk), F32),
            pltpu.VMEM((count, cut, blk), BF16),
            pltpu.VMEM((count, cut, blk), F32),
        ],
        compiler_params=spare,
        cost_estimate=cost(0.001),
        name="early_terms",
    )(table, weights, xo, hb, *early)

    own, send, grads = pl.pallas_call(
        functools.partial(second_kernel, n_tensor, cut, cap),
        out_shape=(
            shape((shards, 2, blk, blk), F32),
            shape((shards, 2, blk, blk), F32),
            shape((count, rest, blk), BF16),
        ),
        in_specs=[smem] + [vmem] * (3 + n_tensor),
        out_specs=(vmem,) * 3,
        scratch_shapes=[
            pltpu.VMEM((count, rest, blk), BF16),
            pltpu.VMEM((2, count, rest, blk), F32),
            pltpu.VMEM((cap, shards, 2, blk, blk), F32),
        ],
        compiler_params=spare,
        cost_estimate=cost(0.001),
        name="late_tiles",
    )(table, weights, xo, hb, tile_sums, *late)
    other = lax.ppermute(send, "seq", swap)
    pairs = [own[k] + other[k].astype(F32) for k in range(shards)]
    others = [
        lax.ppermute(pairs[k].astype(BF16), "fsdp", swaps(shards, k)) for k in range(1, shards)
    ]

    back_late = pl.pallas_call(
        back_kernel,
        out_shape=shape((count * rest, blk), BF16),
        in_specs=[smem, vmem, vmem],
        out_specs=vmem,
        scratch_shapes=[pltpu.VMEM((count, rest, blk), F32)],
        compiler_params=spare,
        cost_estimate=cost(0.001),
        name="late_terms",
    )(table, weights, grads)

    def of_all(a):
        if n_tensor == 2:
            return [a, lax.ppermute(a, "tensor", swap)]
        everyone = lax.all_gather(a, "tensor")
        return [everyone[n] for n in range(n_tensor)]

    def block_scratch(size):
        return [
            pltpu.VMEM((size, width), BF16),
            pltpu.VMEM((size, width) if n_tensor != 2 else (8, 128), F32),
        ]

    token_grad, rows = pl.pallas_call(
        functools.partial(place_early_kernel, n_tensor, count),
        out_shape=(shape((toks, width), BF16), shape((n_tensor, count), I32)),
        in_specs=[vmem] * n_tensor,
        out_specs=(hbm, smem),
        scratch_shapes=[
            pltpu.VMEM((n_tensor, 8, blk), I32),
            pltpu.SMEM((n_tensor, 8, blk), I32),
            *block_scratch(cut),
            pltpu.SemaphoreType.DMA,
            pltpu.SemaphoreType.DMA,
        ],
        compiler_params=spare,
        cost_estimate=cost(0.001),
        name="place_early",
    )(*of_all(back_early))
    token_grad, tile_grads = pl.pallas_call(
        functools.partial(place_late_kernel, n_tensor, cut, count),
        out_shape=(shape((toks, width), BF16), shape((2, blk, blk), BF16)),
        in_specs=[smem] + [vmem] * n_tensor + [hbm] + [vmem] * shards,
        out_specs=(hbm, vmem),
        scratch_shapes=[*block_scratch(rest), pltpu.SemaphoreType.DMA],
        input_output_aliases={n_tensor + 1: 0},
        compiler_params=spare,
        cost_estimate=cost(0.001),
        name="place_late",
    )(rows, *of_all(back_late), token_grad, pairs[0], *others)
    return token_grad, tile_grads.reshape(1, 1, 1, 2, blk, blk)


def solution(mesh):
    return jax.shard_map(
        functools.partial(local, dict(mesh.shape)),
        mesh=mesh,
        in_specs=(
            P(("group", "fsdp", "seq"), "tensor"),
            P(("group", "fsdp", "seq"), "tensor"),
            P("fsdp", "tensor", None, None, None, None),
            P("fsdp", "tensor", None, None),
            P("fsdp", "tensor", None),
        ),
        out_specs=(
            P(("group", "fsdp", "seq"), None),
            P(("group", "fsdp"), "tensor", "seq", None, None, None),
        ),
        check_vma=False,
    )
```

time: 57.5 us -> 46.8 us (0.81)
  starting transfers between devices: 22.5 us -> 14.7 us
  other arithmetic: 4.09 us -> 0.06 us
  Pallas kernels: 8.9 us -> 12.4 us
  local copies, waits for them, and re-layouts: 4.67 us -> 2.26 us
    ppermute x13 -> x11, starting transfers between devices: 22.5 us -> 14.7 us  [the longest x3 4.81 us: local(): lax.ppermute(packed, 'fsdp', swaps(shards, k))]
    pallas_call x2 -> x7, Pallas kernels: 8.9 us -> 12.4 us  [the longest x1 2.9 us: local(): pl.pallas_call(functools.partial(place_early_kernel, n_tensor, count), ou...]
    unnamed x12 -> x8, local copies, waits for them, and re-layouts: 2.41 us -> 0.02 us
    slice x0 -> x2, local copies, waits for them, and re-layouts: none -> 2.24 us  [the longest x1 1.27 us: local(): early = to_partners(tokens[:cut])]
    concatenate x1 -> x0, other arithmetic: 1.78 us -> none  [local(): tiles_all = jnp.concatenate(from_shards(tiles), axis=0)]
    another operation x2 -> x0, other arithmetic: 1.18 us -> none  [local(): infos = jnp.stack([info_all, lax.ppermute(info_all, 'tensor', swap)])]
    convert_element_type x1, other arithmetic: 1.12 us -> 0.06 us  [local(): pairs[k].astype(BF16)]
    lt x4 -> x0, local copies, waits for them, and re-layouts: 0.83 us -> none  [local(): jnp.arange(cap, dtype=jnp.int32)[None, :, None]]
  transfers between devices with their start and end apart: 13 -> 11, of which waited for: 5 -> 4; matrix products, arithmetic and copies ran while one was open for 11% -> 2% of each run, Pallas kernels for 0% -> 19%
where the time goes in v2:
time: 46.8 us; the launch traced here: 46.6 us
  waiting for transfers between devices  16.4 us (35%)
  starting transfers between devices  14.7 us (31%)
  Pallas kernels  12.4 us (26%)
  local copies, waits for them, and re-layouts  2.26 us (5%)
  between operations  0.79 us (2%)
    ppermute x3, waiting for transfers between devices, local(): lax.ppermute(packed, 'fsdp', swaps(shards, k))  10.2 us
    ppermute x3, starting transfers between devices, local(): lax.ppermute(packed, 'fsdp', swaps(shards, k))  4.81 us
    ppermute x3, starting transfers between devices, local(): lax.ppermute(pairs[k].astype(BF16), 'fsdp', swaps(shards, k))  4.56 us
    ppermute x2, waiting for transfers between devices, of_all(): return [a, lax.ppermute(a, 'tensor', swap)]  4.38 us
    ppermute x2, starting transfers between devices, to_partners(): lax.ppermute(a, 'tensor', shift(n_tensor, n_tensor - k))  3.09 us
    pallas_call x1, Pallas kernels, local(): pl.pallas_call(functools.partial(place_early_kernel, n_tensor, count), ou...  2.9 us
    pallas_call x1, Pallas kernels, local(): pl.pallas_call(functools.partial(prepare_kernel, shards, cap), out_shape=...  2.81 us
    pallas_call x1, Pallas kernels, local(): pl.pallas_call(functools.partial(place_late_kernel, n_tensor, cut, count)...  2.17 us
  transfers between devices with their start and end apart: 11, of which 4 were waited for; matrix products, arithmetic and copies ran while one was open for 2% of the time, Pallas kernels for 19%

profile of v2, /device:TPU:0, one launch (start us, length us, event | category | flops | bytes accessed | tf_op | source)
XLA Modules:
  0.0 46.6 jit_solution(5379613373231375673)
XLA Ops:
  0.6 0.0 copy-start
  0.7 1.3 %slice.30 = bf16[192,2048]{1,0:T(8,128)(2,1)S(1)} slice(bf16[256,2048]{1,0:T(8,128)(2,1)} %refs_4_.1), slice={[0:192], [0:2048]} | slice | bytes 1572864 | tf_op jit(solution)/shard_map/slice | solution.py:292
  1.9 3.0 %collective-permute-start.3 = (bf16[192,2048]{1,0:T(8,128)(2,1)S(1)}, bf16[192,2048]{1,0:T(8,128)(2,1)S(1)}, u32[]{:S(2)}, u32[]{:S(2)}) collective-permute-start(bf16[192,2048]{1,0:T(8,128)(2,1)S(1)} %slice.30), channel_id=1, source_target_pairs={{0,2},{2,0},{1,3},{3,1},{4,6},{6,4},{5,7},{7,5},{8,10},{10,8},{9,1... | collective-permute-start | bytes 2359304 | tf_op jit(solution)/shard_map/ppermute | solution.py:289
  5.0 1.0 %slice.31 = bf16[64,2048]{1,0:T(8,128)(2,1)S(1)} slice(bf16[256,2048]{1,0:T(8,128)(2,1)} %refs_4_.1), slice={[192:256], [0:2048]} | slice | bytes 524288 | tf_op jit(solution)/shard_map/slice | solution.py:302
  5.9 0.1 collective-permute-start.5
  6.0 0.6 %pack.1.refs_0_ = bf16[528,128]{1,0:T(8,128)(2,1)S(1)} custom-call(s32[1,1,2,2]{3,2,1,0:T(2,128)S(1)} %copy-done.2, s32[1,1,2]{2,1,0:T(1,128)S(1)} %copy-done.3, bf16[1,1,2,2,128,128]{5,4,3,2,1,0:T(8,128)(2,1)S(1)} %copy-done.1), custom_call_target="tpu_custom_call" | custom-call | bytes 3690 | tf_op jit(solution)/shard_map/pack/pallas_call | solution.py:293
  6.6 4.2 %collective-permute-start.2 = (bf16[528,128]{1,0:T(8,128)(2,1)S(1)}, bf16[528,128]{1,0:T(8,128)(2,1)S(1)}, u32[]{:S(2)}, u32[]{:S(2)}) collective-permute-start(bf16[528,128]{1,0:T(8,128)(2,1)S(1)} %pack.1.refs_0_), channel_id=1, source_target_pairs={{0,12},{4,8},{8,4},{12,0},{1,13},{5,9},{9,5},{13,1},{2,14},{6,10},... | collective-permute-start | bytes 405512 | tf_op jit(solution)/shard_map/ppermute | solution.py:304
  10.8 0.6 %collective-permute-start = (bf16[528,128]{1,0:T(8,128)(2,1)S(1)}, bf16[528,128]{1,0:T(8,128)(2,1)S(1)}, u32[]{:S(2)}, u32[]{:S(2)}) collective-permute-start(bf16[528,128]{1,0:T(8,128)(2,1)S(1)} %pack.1.refs_0_), channel_id=1, source_target_pairs={{0,4},{4,0},{8,12},{12,8},{1,5},{5,1},{9,13},{13,9},{2,6},{6,2},{1... | collective-permute-start | bytes 405512 | tf_op jit(solution)/shard_map/ppermute | solution.py:304
  11.4 3.9 %collective-permute-done.2.refs_3_ = bf16[528,128]{1,0:T(8,128)(2,1)S(1)} collective-permute-done((bf16[528,128]{1,0:T(8,128)(2,1)S(1)}, bf16[528,128]{1,0:T(8,128)(2,1)S(1)}, u32[]{:S(2)}, u32[]{:S(2)}) %collective-permute-start.2) | collective-permute-done | bytes 135200 | tf_op jit(solution)/shard_map/ppermute | solution.py:304
  15.3 6.3 %collective-permute-done.1.refs_2_ = bf16[528,128]{1,0:T(8,128)(2,1)S(1)} collective-permute-done((bf16[528,128]{1,0:T(8,128)(2,1)S(1)}, bf16[528,128]{1,0:T(8,128)(2,1)S(1)}, u32[]{:S(2)}, u32[]{:S(2)}) %collective-permute-start.1) | collective-permute-done | bytes 135200 | tf_op jit(solution)/shard_map/ppermute | solution.py:304
  21.7 2.8 %prepare.1 = (s32[5,9]{1,0:T(8,128)S(1)}, bf16[9,128,128]{2,1,0:T(8,128)(2,1)S(1)}, bf16[8,256,128]{2,1,0:T(8,128)(2,1)S(1)}, bf16[8,256,128]{2,1,0:T(8,128)(2,1)S(1)}) custom-call(bf16[528,128]{1,0:T(8,128)(2,1)S(1)} %pack.1.refs_0_, bf16[528,128]{1,0:T(8,128)(2,1)S(1)} %collective-permute-done.refs_1_, ...), custom_call_target="tpu_custom_call" | custom-call | bytes 3690 | tf_op jit(solution)/shard_map/prepare/pallas_call | solution.py:307
  24.5 1.8 %early_terms.1 = (bf16[1552,128]{1,0:T(8,128)(2,1)S(1)}, f32[8,128,128]{2,1,0:T(8,128)S(1)}) custom-call(s32[5,9]{1,0:T(8,128)S(1)} %get-tuple-element.15.table, bf16[9,128,128]{2,1,0:T(8,128)(2,1)S(1)} %get-tuple-element.16.weights, bf16[8,256,128]{2,1,0:T(8,128)(2,1)S(1)} %get-tuple-element.17.xo, bf16[8,256,128]{2,1,0:T(8,128)(2,1)S(1)} %get-tuple-element.18.hb, ...), custom_call_target="tpu_custom_call" | custom-call | bytes 3690 | tf_op jit(solution)/shard_map/early_terms/pallas_call | solution.py:329
  26.3 1.8 %collective-permute-done.5.refs_0_ = bf16[64,2048]{1,0:T(8,128)(2,1)S(1)} collective-permute-done((bf16[64,2048]{1,0:T(8,128)(2,1)S(1)}, bf16[64,2048]{1,0:T(8,128)(2,1)S(1)}, u32[]{:S(2)}, u32[]{:S(2)}) %collective-permute-start.5) | collective-permute-done | bytes 262176 | tf_op jit(solution)/shard_map/ppermute | solution.py:289
  28.1 1.2 %late_tiles.1 = (f32[4,2,128,128]{3,2,1,0:T(8,128)S(1)}, f32[4,2,128,128]{3,2,1,0:T(8,128)S(1)}, bf16[8,64,128]{2,1,0:T(8,128)(2,1)S(1)}) custom-call(s32[5,9]{1,0:T(8,128)S(1)} %get-tuple-element.15.table, bf16[9,128,128]{2,1,0:T(8,128)(2,1)S(1)} %get-tuple-element.16.weights, bf16[8,256,128]{2,1,0:T(8,128)(2,1)S(1)} %get-tuple-element.17.xo, ...), custom_call_target="tpu_custom_call" | custom-call | bytes 3690 | tf_op jit(solution)/shard_map/late_tiles/pallas_call | solution.py:345
  29.3 0.1 collective-permute-start.7
  29.4 1.8 %collective-permute-start.4 = (bf16[1552,128]{1,0:T(8,128)(2,1)S(1)}, bf16[1552,128]{1,0:T(8,128)(2,1)S(1)}, u32[]{:S(2)}, u32[]{:S(2)}) collective-permute-start(bf16[1552,128]{1,0:T(8,128)(2,1)S(1)} %get-tuple-element.19.refs_0_), channel_id=1, source_target_pairs={{0,2},{2,0},{1,3},{3,1},{4,6},{6,4},{5,7},{7,5},{8,10},{10,8},{9,1... | collective-permute-start | bytes 1191944 | tf_op jit(solution)/shard_map/ppermute | solution.py:382
  31.2 0.9 %late_terms.1.refs_0_ = bf16[512,128]{1,0:T(8,128)(2,1)S(1)} custom-call(s32[5,9]{1,0:T(8,128)S(1)} %get-tuple-element.15.table, bf16[9,128,128]{2,1,0:T(8,128)(2,1)S(1)} %get-tuple-element.16.weights, bf16[8,64,128]{2,1,0:T(8,128)(2,1)S(1)} %get-tuple-element.22.grads), custom_call_target="tpu_custom_call" | custom-call | bytes 3690 | tf_op jit(solution)/shard_map/late_terms/pallas_call | solution.py:369
  32.1 0.4 collective-permute-start.6
  32.5 0.1 fusion.6
  32.5 3.9 %collective-permute-start.10 = (bf16[2,128,128]{2,1,0:T(8,128)(2,1)S(1)}, bf16[2,128,128]{2,1,0:T(8,128)(2,1)S(1)}, u32[]{:S(2)}, u32[]{:S(2)}) collective-permute-start(bf16[2,128,128]{2,1,0:T(8,128)(2,1)S(1)} %get-tuple-element.28), channel_id=1, source_target_pairs={{0,12},{4,8},{8,4},{12,0},{1,13},{5,9},{9,5},{13,1},{2,14},{6,10},... | collective-permute-start | bytes 196616 | tf_op jit(solution)/shard_map/ppermute | solution.py:366
  36.5 0.6 %collective-permute-start.8 = (bf16[2,128,128]{2,1,0:T(8,128)(2,1)S(1)}, bf16[2,128,128]{2,1,0:T(8,128)(2,1)S(1)}, u32[]{:S(2)}, u32[]{:S(2)}) collective-permute-start(bf16[2,128,128]{2,1,0:T(8,128)(2,1)S(1)} %get-tuple-element.30), channel_id=1, source_target_pairs={{0,4},{4,0},{8,12},{12,8},{1,5},{5,1},{9,13},{13,9},{2,6},{6,2},{1... | collective-permute-start | bytes 196616 | tf_op jit(solution)/shard_map/ppermute | solution.py:366
  37.1 4.4 %collective-permute-done.4.refs_1_ = bf16[1552,128]{1,0:T(8,128)(2,1)S(1)} collective-permute-done((bf16[1552,128]{1,0:T(8,128)(2,1)S(1)}, bf16[1552,128]{1,0:T(8,128)(2,1)S(1)}, u32[]{:S(2)}, u32[]{:S(2)}) %collective-permute-start.4) | collective-permute-done | bytes 397344 | tf_op jit(solution)/shard_map/ppermute | solution.py:382
  41.5 2.9 %place_early.1 = (bf16[256,4096]{1,0:T(8,128)(2,1)}, s32[2,8]{1,0:T(2,128)S(1)}) custom-call(bf16[1552,128]{1,0:T(8,128)(2,1)S(1)} %get-tuple-element.19.refs_0_, bf16[1552,128]{1,0:T(8,128)(2,1)S(1)} %collective-permute-done.4.refs_1_), custom_call_target="tpu_custom_call" | custom-call | bytes 3690 | tf_op jit(solution)/shard_map/place_early/pallas_call | solution.py:392
  44.4 2.2 %place_late.1 = (bf16[256,4096]{1,0:T(8,128)(2,1)}, bf16[2,128,128]{2,1,0:T(8,128)(2,1)}) custom-call(s32[2,8]{1,0:T(2,128)S(1)} %get-tuple-element.20.rows, bf16[512,128]{1,0:T(8,128)(2,1)S(1)} %late_terms.1.refs_0_, bf16[512,128]{1,0:T(8,128)(2,1)S(1)} %collective-permute-done.6.refs_1_, ...), custom_call_target="tpu_custom_call", output_to_operand_aliasing={{0}: (3, {})} | custom-call | bytes 3690 | tf_op jit(solution)/shard_map/place_late/pallas_call | solution.py:408
  (16 shorter events, 0.0 us)
Async XLA Ops:
  0.6 21.0 %copy-start = (bf16[256,2048]{1,0:T(8,128)(2,1)S(1)}, bf16[256,2048]{1,0:T(8,128)(2,1)}, u32[]{:S(2)}) copy-start(bf16[256,2048]{1,0:T(8,128)(2,1)} %refs_4_.1) | copy-start | bytes 3145732
  0.6 5.4 %copy-start.3 = (s32[1,1,2]{2,1,0:T(1,128)S(1)}, s32[1,1,2]{2,1,0:T(1,128)}, u32[]{:S(2)}) copy-start(s32[1,1,2]{2,1,0:T(1,128)} %count.1) | copy-start | bytes 28
  0.7 5.4 %copy-start.2 = (s32[1,1,2,2]{3,2,1,0:T(2,128)S(1)}, s32[1,1,2,2]{3,2,1,0:T(2,128)}, u32[]{:S(2)}) copy-start(s32[1,1,2,2]{3,2,1,0:T(2,128)} %keep.1) | copy-start | bytes 52
  0.7 5.4 %copy-start.1 = (bf16[1,1,2,2,128,128]{5,4,3,2,1,0:T(8,128)(2,1)S(1)}, bf16[1,1,2,2,128,128]{5,4,3,2,1,0:T(8,128)(2,1)}, u32[]{:S(2)}) copy-start(bf16[1,1,2,2,128,128]{5,4,3,2,1,0:T(8,128)(2,1)} %tiles.1) | copy-start | bytes 393220
  1.9 22.5 %collective-permute-start.3 = (bf16[192,2048]{1,0:T(8,128)(2,1)S(1)}, bf16[192,2048]{1,0:T(8,128)(2,1)S(1)}, u32[]{:S(2)}, u32[]{:S(2)}) collective-permute-start(bf16[192,2048]{1,0:T(8,128)(2,1)S(1)} %slice.30), channel_id=1, source_target_pairs={{0,2},{2,0},{1,3},{3,1},{4,6},{6,4},{5,7},{7,5},{8,10},{10,8},{9,1... | collective-permute-start | bytes 2359304 | tf_op jit(solution)/shard_map/ppermute | solution.py:289
  5.9 22.2 %collective-permute-start.5 = (bf16[64,2048]{1,0:T(8,128)(2,1)S(1)}, bf16[64,2048]{1,0:T(8,128)(2,1)S(1)}, u32[]{:S(2)}, u32[]{:S(2)}) collective-permute-start(bf16[64,2048]{1,0:T(8,128)(2,1)S(1)} %slice.31), channel_id=1, source_target_pairs={{0,2},{2,0},{1,3},{3,1},{4,6},{6,4},{5,7},{7,5},{8,10},{10,8},{9,1... | collective-permute-start | bytes 786440 | tf_op jit(solution)/shard_map/ppermute | solution.py:289
  6.6 8.7 %collective-permute-start.2 = (bf16[528,128]{1,0:T(8,128)(2,1)S(1)}, bf16[528,128]{1,0:T(8,128)(2,1)S(1)}, u32[]{:S(2)}, u32[]{:S(2)}) collective-permute-start(bf16[528,128]{1,0:T(8,128)(2,1)S(1)} %pack.1.refs_0_), channel_id=1, source_target_pairs={{0,12},{4,8},{8,4},{12,0},{1,13},{5,9},{9,5},{13,1},{2,14},{6,10},... | collective-permute-start | bytes 405512 | tf_op jit(solution)/shard_map/ppermute | solution.py:304
  10.8 10.9 %collective-permute-start.1 = (bf16[528,128]{1,0:T(8,128)(2,1)S(1)}, bf16[528,128]{1,0:T(8,128)(2,1)S(1)}, u32[]{:S(2)}, u32[]{:S(2)}) collective-permute-start(bf16[528,128]{1,0:T(8,128)(2,1)S(1)} %pack.1.refs_0_), channel_id=1, source_target_pairs={{0,8},{4,12},{8,0},{12,4},{1,9},{5,13},{9,1},{13,5},{2,10},{6,14},... | collective-permute-start | bytes 405512 | tf_op jit(solution)/shard_map/ppermute | solution.py:304
  10.8 10.9 %collective-permute-start = (bf16[528,128]{1,0:T(8,128)(2,1)S(1)}, bf16[528,128]{1,0:T(8,128)(2,1)S(1)}, u32[]{:S(2)}, u32[]{:S(2)}) collective-permute-start(bf16[528,128]{1,0:T(8,128)(2,1)S(1)} %pack.1.refs_0_), channel_id=1, source_target_pairs={{0,4},{4,0},{8,12},{12,8},{1,5},{5,1},{9,13},{13,9},{2,6},{6,2},{1... | collective-permute-start | bytes 405512 | tf_op jit(solution)/shard_map/ppermute | solution.py:304
  29.3 3.1 %collective-permute-start.7 = (f32[4,2,128,128]{3,2,1,0:T(8,128)S(1)}, f32[4,2,128,128]{3,2,1,0:T(8,128)S(1)}, u32[]{:S(2)}, u32[]{:S(2)}) collective-permute-start(f32[4,2,128,128]{3,2,1,0:T(8,128)S(1)} %get-tuple-element.25), channel_id=1, source_target_pairs={{0,1},{1,0},{2,3},{3,2},{4,5},{5,4},{6,7},{7,6},{8,9},{9,8},{10,11... | collective-permute-start | bytes 1572872 | tf_op jit(solution)/shard_map/ppermute | solution.py:363
  29.4 12.1 %collective-permute-start.4 = (bf16[1552,128]{1,0:T(8,128)(2,1)S(1)}, bf16[1552,128]{1,0:T(8,128)(2,1)S(1)}, u32[]{:S(2)}, u32[]{:S(2)}) collective-permute-start(bf16[1552,128]{1,0:T(8,128)(2,1)S(1)} %get-tuple-element.19.refs_0_), channel_id=1, source_target_pairs={{0,2},{2,0},{1,3},{3,1},{4,6},{6,4},{5,7},{7,5},{8,10},{10,8},{9,1... | collective-permute-start | bytes 1191944 | tf_op jit(solution)/shard_map/ppermute | solution.py:382
  32.1 12.3 %collective-permute-start.6 = (bf16[512,128]{1,0:T(8,128)(2,1)S(1)}, bf16[512,128]{1,0:T(8,128)(2,1)S(1)}, u32[]{:S(2)}, u32[]{:S(2)}) collective-permute-start(bf16[512,128]{1,0:T(8,128)(2,1)S(1)} %late_terms.1.refs_0_), channel_id=1, source_target_pairs={{0,2},{2,0},{1,3},{3,1},{4,6},{6,4},{5,7},{7,5},{8,10},{10,8},{9,1... | collective-permute-start | bytes 393224 | tf_op jit(solution)/shard_map/ppermute | solution.py:382
  32.5 11.9 %collective-permute-start.10 = (bf16[2,128,128]{2,1,0:T(8,128)(2,1)S(1)}, bf16[2,128,128]{2,1,0:T(8,128)(2,1)S(1)}, u32[]{:S(2)}, u32[]{:S(2)}) collective-permute-start(bf16[2,128,128]{2,1,0:T(8,128)(2,1)S(1)} %get-tuple-element.28), channel_id=1, source_target_pairs={{0,12},{4,8},{8,4},{12,0},{1,13},{5,9},{9,5},{13,1},{2,14},{6,10},... | collective-permute-start | bytes 196616 | tf_op jit(solution)/shard_map/ppermute | solution.py:366
  36.5 8.0 %collective-permute-start.9 = (bf16[2,128,128]{2,1,0:T(8,128)(2,1)S(1)}, bf16[2,128,128]{2,1,0:T(8,128)(2,1)S(1)}, u32[]{:S(2)}, u32[]{:S(2)}) collective-permute-start(bf16[2,128,128]{2,1,0:T(8,128)(2,1)S(1)} %get-tuple-element.29), channel_id=1, source_target_pairs={{0,8},{4,12},{8,0},{12,4},{1,9},{5,13},{9,1},{13,5},{2,10},{6,14},... | collective-permute-start | bytes 196616 | tf_op jit(solution)/shard_map/ppermute | solution.py:366
  36.5 8.0 %collective-permute-start.8 = (bf16[2,128,128]{2,1,0:T(8,128)(2,1)S(1)}, bf16[2,128,128]{2,1,0:T(8,128)(2,1)S(1)}, u32[]{:S(2)}, u32[]{:S(2)}) collective-permute-start(bf16[2,128,128]{2,1,0:T(8,128)(2,1)S(1)} %get-tuple-element.30), channel_id=1, source_target_pairs={{0,4},{4,0},{8,12},{12,8},{1,5},{5,1},{9,13},{13,9},{2,6},{6,2},{1... | collective-permute-start | bytes 196616 | tf_op jit(solution)/shard_map/ppermute | solution.py:366

commit v3 on v2

--- a/solution.py
+++ b/solution.py
@@ -198,7 +198,7 @@
 
 def second_kernel(n_tensor, lo, cap, table, weights, xo, hb, tile_sums, *refs):
     remote, refs = refs[: n_tensor - 1], refs[n_tensor - 1 :]
-    own, send, grads, xs, pre, both = refs
+    own, send, back, grads, xs, pre, both, acc = refs
     forward_backward(lo, table, weights, xo, hb, remote, xs, pre, grads)
     both[...] = jnp.zeros_like(both)
     s = lax.axis_index("seq")
@@ -212,10 +212,12 @@
     loop(xs.shape[0], tile)
     own[...] = both[0]
     send[...] = both[1].astype(send.dtype)
-
-
-def back_kernel(table, weights, grads, back, acc):
     back_terms(table, weights, grads, acc, back)
+
+
+def pair_kernel(own, other, *sums):
+    for k, total in enumerate(sums):
+        total[...] = (own[k] + other[k].astype(F32)).astype(total.dtype)
 
 
 def add_blocks(rows, parts, count, block, wide, out, lo, sem):
@@ -240,11 +242,11 @@
 
 
 def place_early_kernel(n_tensor, count, *refs):
+    infos, refs = refs[:n_tensor], refs[n_tensor:]
     parts, refs = refs[:n_tensor], refs[n_tensor:]
-    out, rows, ints, info, block, wide, isem, sem = refs
-    size = block.shape[0]
-    for n, part in enumerate(parts):
-        ints[n] = part[pl.ds(count * size, INFO_ROWS), :].astype(F32)[:8].astype(I32)
+    out, rows, ints, info, isem, block, wide, sem = refs
+    for n, part in enumerate(infos):
+        ints[n] = part[...].astype(F32)[:8].astype(I32)
     fetch = pltpu.make_async_copy(ints, info, isem)
     fetch.start()
     fetch.wait()
@@ -254,14 +256,18 @@
     add_blocks(rows, parts, count, block, wide, out, 0, sem).wait()
 
 
-def place_late_kernel(n_tensor, lo, count, rows, *refs):
+def place_late_kernel(n_tensor, shards, lo, count, rows, *refs):
     parts, refs = refs[:n_tensor], refs[n_tensor:]
-    _, mine, *others, out, tile_grads, block, wide, sem = refs
+    _, mine, *others = refs[: shards + 1]
+    out, tile_grads, block, wide, sem, tile_sum, tile_sem = refs[shards + 1 :]
+    total = mine[...]
+    for other in others:
+        total = total + other[...].astype(F32)
+    tile_sum[...] = total.astype(BF16)
+    tile_copy = pltpu.make_async_copy(tile_sum, tile_grads, tile_sem)
+    tile_copy.start()
     copy = add_blocks(rows, parts, count, block, wide, out, lo, sem)
-    tile_sum = mine[...]
-    for other in others:
-        tile_sum = tile_sum + other[...].astype(F32)
-    tile_grads[...] = tile_sum.astype(BF16)
+    tile_copy.wait()
     copy.wait()
 
 
@@ -342,40 +348,39 @@
         name="early_terms",
     )(table, weights, xo, hb, *early)
 
-    own, send, grads = pl.pallas_call(
+    own, send, back_late = pl.pallas_call(
         functools.partial(second_kernel, n_tensor, cut, cap),
         out_shape=(
             shape((shards, 2, blk, blk), F32),
-            shape((shards, 2, blk, blk), F32),
-            shape((count, rest, blk), BF16),
+            shape((shards, 2, blk, blk), BF16),
+            shape((count * rest, blk), BF16),
         ),
         in_specs=[smem] + [vmem] * (3 + n_tensor),
         out_specs=(vmem,) * 3,
         scratch_shapes=[
             pltpu.VMEM((count, rest, blk), BF16),
+            pltpu.VMEM((count, rest, blk), BF16),
             pltpu.VMEM((2, count, rest, blk), F32),
             pltpu.VMEM((cap, shards, 2, blk, blk), F32),
+            pltpu.VMEM((count, rest, blk), F32),
         ],
         compiler_params=spare,
         cost_estimate=cost(0.001),
         name="late_tiles",
     )(table, weights, xo, hb, tile_sums, *late)
     other = lax.ppermute(send, "seq", swap)
-    pairs = [own[k] + other[k].astype(F32) for k in range(shards)]
+    mine, *rounded = pl.pallas_call(
+        pair_kernel,
+        out_shape=(shape((2, blk, blk), F32),) + (shape((2, blk, blk), BF16),) * (shards - 1),
+        in_specs=[vmem, vmem],
+        out_specs=(vmem,) * shards,
+        compiler_params=spare,
+        cost_estimate=cost(0.001),
+        name="pair",
+    )(own, other)
     others = [
-        lax.ppermute(pairs[k].astype(BF16), "fsdp", swaps(shards, k)) for k in range(1, shards)
+        lax.ppermute(rounded[k - 1], "fsdp", swaps(shards, k)) for k in range(shards - 1, 0, -1)
     ]
-
-    back_late = pl.pallas_call(
-        back_kernel,
-        out_shape=shape((count * rest, blk), BF16),
-        in_specs=[smem, vmem, vmem],
-        out_specs=vmem,
-        scratch_shapes=[pltpu.VMEM((count, rest, blk), F32)],
-        compiler_params=spare,
-        cost_estimate=cost(0.001),
-        name="late_terms",
-    )(table, weights, grads)
 
     def of_all(a):
         if n_tensor == 2:
@@ -389,33 +394,42 @@
             pltpu.VMEM((size, width) if n_tensor != 2 else (8, 128), F32),
         ]
 
+    parts = of_all(back_early)
+    infos = [part[count * cut :] for part in parts]
+    if n_tensor == 2:
+        pass
     token_grad, rows = pl.pallas_call(
         functools.partial(place_early_kernel, n_tensor, count),
         out_shape=(shape((toks, width), BF16), shape((n_tensor, count), I32)),
-        in_specs=[vmem] * n_tensor,
+        in_specs=[vmem] * (2 * n_tensor),
         out_specs=(hbm, smem),
         scratch_shapes=[
             pltpu.VMEM((n_tensor, 8, blk), I32),
             pltpu.SMEM((n_tensor, 8, blk), I32),
+            pltpu.SemaphoreType.DMA,
             *block_scratch(cut),
             pltpu.SemaphoreType.DMA,
+        ],
+        compiler_params=spare,
+        cost_estimate=cost(0.001),
+        name="place_early",
+    )(*infos, *parts)
+    token_grad, tile_grads = pl.pallas_call(
+        functools.partial(place_late_kernel, n_tensor, shards, cut, count),
+        out_shape=(shape((toks, width), BF16), shape((2, blk, blk), BF16)),
+        in_specs=[smem] + [vmem] * n_tensor + [hbm] + [vmem] * shards,
+        out_specs=(hbm, hbm),
+        scratch_shapes=[
+            *block_scratch(rest),
+            pltpu.SemaphoreType.DMA,
+            pltpu.VMEM((2, blk, blk), BF16),
             pltpu.SemaphoreType.DMA,
         ],
-        compiler_params=spare,
-        cost_estimate=cost(0.001),
-        name="place_early",
-    )(*of_all(back_early))
-    token_grad, tile_grads = pl.pallas_call(
-        functools.partial(place_late_kernel, n_tensor, cut, count),
-        out_shape=(shape((toks, width), BF16), shape((2, blk, blk), BF16)),
-        in_specs=[smem] + [vmem] * n_tensor + [hbm] + [vmem] * shards,
-        out_specs=(hbm, vmem),
-        scratch_shapes=[*block_scratch(rest), pltpu.SemaphoreType.DMA],
         input_output_aliases={n_tensor + 1: 0},
         compiler_params=spare,
         cost_estimate=cost(0.001),
         name="place_late",
-    )(rows, *of_all(back_late), token_grad, pairs[0], *others)
+    )(rows, *of_all(back_late), token_grad, mine, *others)
     return token_grad, tile_grads.reshape(1, 1, 1, 2, blk, blk)
 
 

time: 46.8 us -> 43.9 us (0.938)
  waiting for transfers between devices: 16.4 us -> 12.8 us
  starting transfers between devices: 14.7 us -> 16.8 us
  Pallas kernels: 12.4 us -> 11 us
    ppermute x2, waiting for transfers between devices: 4.38 us -> 1.19 us  [of_all(): return [a, lax.ppermute(a, 'tensor', swap)]]
    ppermute x2, waiting for transfers between devices: 1.81 us -> 0.25 us  [to_partners(): lax.ppermute(a, 'tensor', shift(n_tensor, n_tensor - k))]
    pallas_call x2, Pallas kernels: 3.07 us -> 1.61 us  [the longest x1 1.56 us: local(): pl.pallas_call(functools.partial(place_late_kernel, n_tensor, shards, cut...]
    ppermute x2, starting transfers between devices: 2.16 us -> 3.59 us  [of_all(): return [a, lax.ppermute(a, 'tensor', swap)]]
    ppermute x3, waiting for transfers between devices: 0.01 us -> 1.13 us  [local(): lax.ppermute(rounded[k - 1], 'fsdp', swaps(shards, k))]
    ppermute x3, starting transfers between devices: 4.56 us -> 5.22 us  [local(): lax.ppermute(rounded[k - 1], 'fsdp', swaps(shards, k))]
  transfers between devices with their start and end apart: 11 -> 11, of which waited for: 4 -> 5; matrix products, arithmetic and copies ran while one was open for 2% -> 2% of each run, Pallas kernels for 19% -> 22%
where the time goes in v3:
time: 43.9 us; the launch traced here: 43.7 us
  starting transfers between devices  16.8 us (38%)
  waiting for transfers between devices  12.8 us (29%)
  Pallas kernels  11 us (25%)
  local copies, waits for them, and re-layouts  2.26 us (5%)
  between operations  0.77 us (2%)
    ppermute x3, waiting for transfers between devices, local(): lax.ppermute(packed, 'fsdp', swaps(shards, k))  10.2 us
    ppermute x3, starting transfers between devices, local(): lax.ppermute(rounded[k - 1], 'fsdp', swaps(shards, k))  5.22 us
    ppermute x3, starting transfers between devices, local(): lax.ppermute(packed, 'fsdp', swaps(shards, k))  4.81 us
    ppermute x2, starting transfers between devices, of_all(): return [a, lax.ppermute(a, 'tensor', swap)]  3.59 us
    ppermute x2, starting transfers between devices, to_partners(): lax.ppermute(a, 'tensor', shift(n_tensor, n_tensor - k))  3.09 us
    pallas_call x1, Pallas kernels, local(): pl.pallas_call(functools.partial(place_early_kernel, n_tensor, count), ou...  2.91 us
    pallas_call x1, Pallas kernels, local(): pl.pallas_call(functools.partial(prepare_kernel, shards, cap), out_shape=...  2.81 us
    pallas_call x1, Pallas kernels, local(): pl.pallas_call(functools.partial(first_kernel, n_tensor), out_shape=(shap...  1.82 us
  transfers between devices with their start and end apart: 11, of which 5 were waited for; matrix products, arithmetic and copies ran while one was open for 2% of the time, Pallas kernels for 22%

profile of v3, /device:TPU:0, one launch (start us, length us, event | category | flops | bytes accessed | tf_op | source)
XLA Modules:
  0.0 43.7 jit_solution(17231016198131428880)
XLA Ops:
  0.6 0.0 copy-start
  0.7 1.3 %slice.12 = bf16[192,2048]{1,0:T(8,128)(2,1)S(1)} slice(bf16[256,2048]{1,0:T(8,128)(2,1)} %refs_4_.1), slice={[0:192], [0:2048]} | slice | bytes 1572864 | tf_op jit(solution)/shard_map/slice | solution.py:298
  1.9 3.0 %collective-permute-start.3 = (bf16[192,2048]{1,0:T(8,128)(2,1)S(1)}, bf16[192,2048]{1,0:T(8,128)(2,1)S(1)}, u32[]{:S(2)}, u32[]{:S(2)}) collective-permute-start(bf16[192,2048]{1,0:T(8,128)(2,1)S(1)} %slice.12), channel_id=1, source_target_pairs={{0,2},{2,0},{1,3},{3,1},{4,6},{6,4},{5,7},{7,5},{8,10},{10,8},{9,1... | collective-permute-start | bytes 2359304 | tf_op jit(solution)/shard_map/ppermute | solution.py:295
  5.0 1.0 %slice.15 = bf16[64,2048]{1,0:T(8,128)(2,1)S(1)} slice(bf16[256,2048]{1,0:T(8,128)(2,1)} %refs_4_.1), slice={[192:256], [0:2048]} | slice | bytes 524288 | tf_op jit(solution)/shard_map/slice | solution.py:308
  5.9 0.1 collective-permute-start.5
  6.0 0.6 %pack.1.refs_0_ = bf16[528,128]{1,0:T(8,128)(2,1)S(1)} custom-call(s32[1,1,2,2]{3,2,1,0:T(2,128)S(1)} %copy-done.2, s32[1,1,2]{2,1,0:T(1,128)S(1)} %copy-done.3, bf16[1,1,2,2,128,128]{5,4,3,2,1,0:T(8,128)(2,1)S(1)} %copy-done.1), custom_call_target="tpu_custom_call" | custom-call | bytes 3690 | tf_op jit(solution)/shard_map/pack/pallas_call | solution.py:299
  6.6 4.2 %collective-permute-start.2 = (bf16[528,128]{1,0:T(8,128)(2,1)S(1)}, bf16[528,128]{1,0:T(8,128)(2,1)S(1)}, u32[]{:S(2)}, u32[]{:S(2)}) collective-permute-start(bf16[528,128]{1,0:T(8,128)(2,1)S(1)} %pack.1.refs_0_), channel_id=1, source_target_pairs={{0,12},{4,8},{8,4},{12,0},{1,13},{5,9},{9,5},{13,1},{2,14},{6,10},... | collective-permute-start | bytes 405512 | tf_op jit(solution)/shard_map/ppermute | solution.py:310
  10.8 0.6 %collective-permute-start = (bf16[528,128]{1,0:T(8,128)(2,1)S(1)}, bf16[528,128]{1,0:T(8,128)(2,1)S(1)}, u32[]{:S(2)}, u32[]{:S(2)}) collective-permute-start(bf16[528,128]{1,0:T(8,128)(2,1)S(1)} %pack.1.refs_0_), channel_id=1, source_target_pairs={{0,4},{4,0},{8,12},{12,8},{1,5},{5,1},{9,13},{13,9},{2,6},{6,2},{1... | collective-permute-start | bytes 405512 | tf_op jit(solution)/shard_map/ppermute | solution.py:310
  11.4 3.9 %collective-permute-done.2.refs_3_ = bf16[528,128]{1,0:T(8,128)(2,1)S(1)} collective-permute-done((bf16[528,128]{1,0:T(8,128)(2,1)S(1)}, bf16[528,128]{1,0:T(8,128)(2,1)S(1)}, u32[]{:S(2)}, u32[]{:S(2)}) %collective-permute-start.2) | collective-permute-done | bytes 135200 | tf_op jit(solution)/shard_map/ppermute | solution.py:310
  15.3 6.3 %collective-permute-done.1.refs_2_ = bf16[528,128]{1,0:T(8,128)(2,1)S(1)} collective-permute-done((bf16[528,128]{1,0:T(8,128)(2,1)S(1)}, bf16[528,128]{1,0:T(8,128)(2,1)S(1)}, u32[]{:S(2)}, u32[]{:S(2)}) %collective-permute-start.1) | collective-permute-done | bytes 135200 | tf_op jit(solution)/shard_map/ppermute | solution.py:310
  21.6 0.0 collective-permute-done.refs_1_
  21.7 2.8 %prepare.1 = (s32[5,9]{1,0:T(8,128)S(1)}, bf16[9,128,128]{2,1,0:T(8,128)(2,1)S(1)}, bf16[8,256,128]{2,1,0:T(8,128)(2,1)S(1)}, bf16[8,256,128]{2,1,0:T(8,128)(2,1)S(1)}) custom-call(bf16[528,128]{1,0:T(8,128)(2,1)S(1)} %pack.1.refs_0_, bf16[528,128]{1,0:T(8,128)(2,1)S(1)} %collective-permute-done.refs_1_, ...), custom_call_target="tpu_custom_call" | custom-call | bytes 3690 | tf_op jit(solution)/shard_map/prepare/pallas_call | solution.py:313
  24.5 1.8 %early_terms.1 = (bf16[1552,128]{1,0:T(8,128)(2,1)S(1)}, f32[8,128,128]{2,1,0:T(8,128)S(1)}) custom-call(s32[5,9]{1,0:T(8,128)S(1)} %get-tuple-element.19.table, bf16[9,128,128]{2,1,0:T(8,128)(2,1)S(1)} %get-tuple-element.20.weights, bf16[8,256,128]{2,1,0:T(8,128)(2,1)S(1)} %get-tuple-element.21.xo, bf16[8,256,128]{2,1,0:T(8,128)(2,1)S(1)} %get-tuple-element.22.hb, ...), custom_call_target="tpu_custom_call" | custom-call | bytes 3690 | tf_op jit(solution)/shard_map/early_terms/pallas_call | solution.py:335
  26.3 1.6 %collective-permute-start.4 = (bf16[1552,128]{1,0:T(8,128)(2,1)S(1)}, bf16[1552,128]{1,0:T(8,128)(2,1)S(1)}, u32[]{:S(2)}, u32[]{:S(2)}) collective-permute-start(bf16[1552,128]{1,0:T(8,128)(2,1)S(1)} %get-tuple-element.23.refs_2_), channel_id=1, source_target_pairs={{0,2},{2,0},{1,3},{3,1},{4,6},{6,4},{5,7},{7,5},{8,10},{10,8},{9,1... | collective-permute-start | bytes 1191944 | tf_op jit(solution)/shard_map/ppermute | solution.py:387
  27.9 0.2 collective-permute-done.5.refs_0_
  28.1 1.3 %late_tiles.1 = (f32[4,2,128,128]{3,2,1,0:T(8,128)S(1)}, bf16[4,2,128,128]{3,2,1,0:T(8,128)(2,1)S(1)}, bf16[512,128]{1,0:T(8,128)(2,1)S(1)}) custom-call(s32[5,9]{1,0:T(8,128)S(1)} %get-tuple-element.19.table, bf16[9,128,128]{2,1,0:T(8,128)(2,1)S(1)} %get-tuple-element.20.weights, bf16[8,256,128]{2,1,0:T(8,128)(2,1)S(1)} %get-tuple-element.21.xo, ...), custom_call_target="tpu_custom_call" | custom-call | bytes 3690 | tf_op jit(solution)/shard_map/late_tiles/pallas_call | solution.py:351
  29.4 0.1 collective-permute-start.7
  29.5 2.0 %collective-permute-start.6 = (bf16[512,128]{1,0:T(8,128)(2,1)S(1)}, bf16[512,128]{1,0:T(8,128)(2,1)S(1)}, u32[]{:S(2)}, u32[]{:S(2)}) collective-permute-start(bf16[512,128]{1,0:T(8,128)(2,1)S(1)} %get-tuple-element.26.refs_0_), channel_id=1, source_target_pairs={{0,2},{2,0},{1,3},{3,1},{4,6},{6,4},{5,7},{7,5},{8,10},{10,8},{9,1... | collective-permute-start | bytes 393224 | tf_op jit(solution)/shard_map/ppermute | solution.py:387
  31.6 4.6 %collective-permute-start.8 = (bf16[2,128,128]{2,1,0:T(8,128)(2,1)S(1)}, bf16[2,128,128]{2,1,0:T(8,128)(2,1)S(1)}, u32[]{:S(2)}, u32[]{:S(2)}) collective-permute-start(bf16[2,128,128]{2,1,0:T(8,128)(2,1)S(1)} %get-tuple-element.31), channel_id=1, source_target_pairs={{0,12},{4,8},{8,4},{12,0},{1,13},{5,9},{9,5},{13,1},{2,14},{6,10},... | collective-permute-start | bytes 196616 | tf_op jit(solution)/shard_map/ppermute | solution.py:382
  36.2 0.6 %collective-permute-start.10 = (bf16[2,128,128]{2,1,0:T(8,128)(2,1)S(1)}, bf16[2,128,128]{2,1,0:T(8,128)(2,1)S(1)}, u32[]{:S(2)}, u32[]{:S(2)}) collective-permute-start(bf16[2,128,128]{2,1,0:T(8,128)(2,1)S(1)} %get-tuple-element.33), channel_id=1, source_target_pairs={{0,4},{4,0},{8,12},{12,8},{1,5},{5,1},{9,13},{13,9},{2,6},{6,2},{1... | collective-permute-start | bytes 196616 | tf_op jit(solution)/shard_map/ppermute | solution.py:382
  36.8 1.2 %collective-permute-done.4.refs_3_ = bf16[1552,128]{1,0:T(8,128)(2,1)S(1)} collective-permute-done((bf16[1552,128]{1,0:T(8,128)(2,1)S(1)}, bf16[1552,128]{1,0:T(8,128)(2,1)S(1)}, u32[]{:S(2)}, u32[]{:S(2)}) %collective-permute-start.4) | collective-permute-done | bytes 397344 | tf_op jit(solution)/shard_map/ppermute | solution.py:387
  38.0 2.9 %place_early.1 = (bf16[256,4096]{1,0:T(8,128)(2,1)}, s32[2,8]{1,0:T(2,128)S(1)}) custom-call(bf16[16,128]{1,0:T(8,128)(2,1)S(1)} %slice.13.refs_0_, bf16[16,128]{1,0:T(8,128)(2,1)S(1)} %slice.16.refs_1_, bf16[1552,128]{1,0:T(8,128)(2,1)S(1)} %get-tuple-element.23.refs_2_, bf16[1552,128]{1,0:T(8,128)(2,1)S(1)} %collective-permute-done.4.refs_3_), custom_call_target="tpu_custom_call" | custom-call | bytes 3690 | tf_op jit(solution)/shard_map/place_early/pallas_call | solution.py:401
  41.0 1.1 %collective-permute-done.9.refs_5_ = bf16[2,128,128]{2,1,0:T(8,128)(2,1)S(1)} collective-permute-done((bf16[2,128,128]{2,1,0:T(8,128)(2,1)S(1)}, bf16[2,128,128]{2,1,0:T(8,128)(2,1)S(1)}, u32[]{:S(2)}, u32[]{:S(2)}) %collective-permute-start.9) | collective-permute-done | bytes 65568 | tf_op jit(solution)/shard_map/ppermute | solution.py:382
  42.1 1.6 %place_late.1 = (bf16[256,4096]{1,0:T(8,128)(2,1)}, bf16[2,128,128]{2,1,0:T(8,128)(2,1)}) custom-call(s32[2,8]{1,0:T(2,128)S(1)} %get-tuple-element.24.rows, bf16[512,128]{1,0:T(8,128)(2,1)S(1)} %get-tuple-element.26.refs_0_, bf16[512,128]{1,0:T(8,128)(2,1)S(1)} %collective-permute-done.6.refs_1_, ...), custom_call_target="tpu_custom_call", output_to_operand_aliasing={{0}: (3, {})} | custom-call | bytes 3690 | tf_op jit(solution)/shard_map/place_late/pallas_call | solution.py:417
  (17 shorter events, 0.1 us)
Async XLA Ops:
  0.6 21.0 %copy-start = (bf16[256,2048]{1,0:T(8,128)(2,1)S(1)}, bf16[256,2048]{1,0:T(8,128)(2,1)}, u32[]{:S(2)}) copy-start(bf16[256,2048]{1,0:T(8,128)(2,1)} %refs_4_.1) | copy-start | bytes 3145732
  0.6 5.4 %copy-start.3 = (s32[1,1,2]{2,1,0:T(1,128)S(1)}, s32[1,1,2]{2,1,0:T(1,128)}, u32[]{:S(2)}) copy-start(s32[1,1,2]{2,1,0:T(1,128)} %count.1) | copy-start | bytes 28
  0.7 5.4 %copy-start.2 = (s32[1,1,2,2]{3,2,1,0:T(2,128)S(1)}, s32[1,1,2,2]{3,2,1,0:T(2,128)}, u32[]{:S(2)}) copy-start(s32[1,1,2,2]{3,2,1,0:T(2,128)} %keep.1) | copy-start | bytes 52
  0.7 5.4 %copy-start.1 = (bf16[1,1,2,2,128,128]{5,4,3,2,1,0:T(8,128)(2,1)S(1)}, bf16[1,1,2,2,128,128]{5,4,3,2,1,0:T(8,128)(2,1)}, u32[]{:S(2)}) copy-start(bf16[1,1,2,2,128,128]{5,4,3,2,1,0:T(8,128)(2,1)} %tiles.1) | copy-start | bytes 393220
  1.9 22.5 %collective-permute-start.3 = (bf16[192,2048]{1,0:T(8,128)(2,1)S(1)}, bf16[192,2048]{1,0:T(8,128)(2,1)S(1)}, u32[]{:S(2)}, u32[]{:S(2)}) collective-permute-start(bf16[192,2048]{1,0:T(8,128)(2,1)S(1)} %slice.12), channel_id=1, source_target_pairs={{0,2},{2,0},{1,3},{3,1},{4,6},{6,4},{5,7},{7,5},{8,10},{10,8},{9,1... | collective-permute-start | bytes 2359304 | tf_op jit(solution)/shard_map/ppermute | solution.py:295
  5.9 22.2 %collective-permute-start.5 = (bf16[64,2048]{1,0:T(8,128)(2,1)S(1)}, bf16[64,2048]{1,0:T(8,128)(2,1)S(1)}, u32[]{:S(2)}, u32[]{:S(2)}) collective-permute-start(bf16[64,2048]{1,0:T(8,128)(2,1)S(1)} %slice.15), channel_id=1, source_target_pairs={{0,2},{2,0},{1,3},{3,1},{4,6},{6,4},{5,7},{7,5},{8,10},{10,8},{9,1... | collective-permute-start | bytes 786440 | tf_op jit(solution)/shard_map/ppermute | solution.py:295
  6.6 8.7 %collective-permute-start.2 = (bf16[528,128]{1,0:T(8,128)(2,1)S(1)}, bf16[528,128]{1,0:T(8,128)(2,1)S(1)}, u32[]{:S(2)}, u32[]{:S(2)}) collective-permute-start(bf16[528,128]{1,0:T(8,128)(2,1)S(1)} %pack.1.refs_0_), channel_id=1, source_target_pairs={{0,12},{4,8},{8,4},{12,0},{1,13},{5,9},{9,5},{13,1},{2,14},{6,10},... | collective-permute-start | bytes 405512 | tf_op jit(solution)/shard_map/ppermute | solution.py:310
  10.8 10.9 %collective-permute-start.1 = (bf16[528,128]{1,0:T(8,128)(2,1)S(1)}, bf16[528,128]{1,0:T(8,128)(2,1)S(1)}, u32[]{:S(2)}, u32[]{:S(2)}) collective-permute-start(bf16[528,128]{1,0:T(8,128)(2,1)S(1)} %pack.1.refs_0_), channel_id=1, source_target_pairs={{0,8},{4,12},{8,0},{12,4},{1,9},{5,13},{9,1},{13,5},{2,10},{6,14},... | collective-permute-start | bytes 405512 | tf_op jit(solution)/shard_map/ppermute | solution.py:310
  10.8 10.9 %collective-permute-start = (bf16[528,128]{1,0:T(8,128)(2,1)S(1)}, bf16[528,128]{1,0:T(8,128)(2,1)S(1)}, u32[]{:S(2)}, u32[]{:S(2)}) collective-permute-start(bf16[528,128]{1,0:T(8,128)(2,1)S(1)} %pack.1.refs_0_), channel_id=1, source_target_pairs={{0,4},{4,0},{8,12},{12,8},{1,5},{5,1},{9,13},{13,9},{2,6},{6,2},{1... | collective-permute-start | bytes 405512 | tf_op jit(solution)/shard_map/ppermute | solution.py:310
  26.3 11.7 %collective-permute-start.4 = (bf16[1552,128]{1,0:T(8,128)(2,1)S(1)}, bf16[1552,128]{1,0:T(8,128)(2,1)S(1)}, u32[]{:S(2)}, u32[]{:S(2)}) collective-permute-start(bf16[1552,128]{1,0:T(8,128)(2,1)S(1)} %get-tuple-element.23.refs_2_), channel_id=1, source_target_pairs={{0,2},{2,0},{1,3},{3,1},{4,6},{6,4},{5,7},{7,5},{8,10},{10,8},{9,1... | collective-permute-start | bytes 1191944 | tf_op jit(solution)/shard_map/ppermute | solution.py:387
  29.4 2.1 %collective-permute-start.7 = (bf16[4,2,128,128]{3,2,1,0:T(8,128)(2,1)S(1)}, bf16[4,2,128,128]{3,2,1,0:T(8,128)(2,1)S(1)}, u32[]{:S(2)}, u32[]{:S(2)}) collective-permute-start(bf16[4,2,128,128]{3,2,1,0:T(8,128)(2,1)S(1)} %get-tuple-element.29), channel_id=1, source_target_pairs={{0,1},{1,0},{2,3},{3,2},{4,5},{5,4},{6,7},{7,6},{8,9},{9,8},{10,11... | collective-permute-start | bytes 786440 | tf_op jit(solution)/shard_map/ppermute | solution.py:371
  29.5 11.4 %collective-permute-start.6 = (bf16[512,128]{1,0:T(8,128)(2,1)S(1)}, bf16[512,128]{1,0:T(8,128)(2,1)S(1)}, u32[]{:S(2)}, u32[]{:S(2)}) collective-permute-start(bf16[512,128]{1,0:T(8,128)(2,1)S(1)} %get-tuple-element.26.refs_0_), channel_id=1, source_target_pairs={{0,2},{2,0},{1,3},{3,1},{4,6},{6,4},{5,7},{7,5},{8,10},{10,8},{9,1... | collective-permute-start | bytes 393224 | tf_op jit(solution)/shard_map/ppermute | solution.py:387
  31.6 9.3 %collective-permute-start.8 = (bf16[2,128,128]{2,1,0:T(8,128)(2,1)S(1)}, bf16[2,128,128]{2,1,0:T(8,128)(2,1)S(1)}, u32[]{:S(2)}, u32[]{:S(2)}) collective-permute-start(bf16[2,128,128]{2,1,0:T(8,128)(2,1)S(1)} %get-tuple-element.31), channel_id=1, source_target_pairs={{0,12},{4,8},{8,4},{12,0},{1,13},{5,9},{9,5},{13,1},{2,14},{6,10},... | collective-permute-start | bytes 196616 | tf_op jit(solution)/shard_map/ppermute | solution.py:382
  36.2 5.9 %collective-permute-start.9 = (bf16[2,128,128]{2,1,0:T(8,128)(2,1)S(1)}, bf16[2,128,128]{2,1,0:T(8,128)(2,1)S(1)}, u32[]{:S(2)}, u32[]{:S(2)}) collective-permute-start(bf16[2,128,128]{2,1,0:T(8,128)(2,1)S(1)} %get-tuple-element.32), channel_id=1, source_target_pairs={{0,8},{4,12},{8,0},{12,4},{1,9},{5,13},{9,1},{13,5},{2,10},{6,14},... | collective-permute-start | bytes 196616 | tf_op jit(solution)/shard_map/ppermute | solution.py:382
  36.2 5.9 %collective-permute-start.10 = (bf16[2,128,128]{2,1,0:T(8,128)(2,1)S(1)}, bf16[2,128,128]{2,1,0:T(8,128)(2,1)S(1)}, u32[]{:S(2)}, u32[]{:S(2)}) collective-permute-start(bf16[2,128,128]{2,1,0:T(8,128)(2,1)S(1)} %get-tuple-element.33), channel_id=1, source_target_pairs={{0,4},{4,0},{8,12},{12,8},{1,5},{5,1},{9,13},{13,9},{2,6},{6,2},{1... | collective-permute-start | bytes 196616 | tf_op jit(solution)/shard_map/ppermute | solution.py:382

commit v4 on v3

--- a/solution.py
+++ b/solution.py
@@ -78,11 +78,10 @@
 
 def prepare_kernel(shards, cap, *refs):
     packed, refs = refs[:shards], refs[shards:]
-    tokens, hidden, table, weights, xo, hb, ints, info, isem, xsem, hsem = refs
+    hidden, listed, weights, hb, ints, info, table, isem, tsem, hsem = refs
     blk = weights.shape[-1]
     base = 2 * cap * blk
-    rows_here = tokens.shape[1] // blk
-    count = xo.shape[0]
+    count = hb.shape[0]
     live = count // 2
     for k in range(shards):
         ints[k] = packed[k][pl.ds(base, INFO_ROWS), :].astype(F32)[:8].astype(I32)
@@ -97,44 +96,43 @@
                 table[ROW, p] = r
                 table[COL, p] = info[k, 1, 2 * j + m]
                 table[SLOT, p] = k * cap + j
-                weights[p] = packed[k][pl.ds((2 * j + m) * blk, blk), :]
                 p = p + jnp.where(r >= 0, 1, 0).astype(I32)
 
-    def copies(i):
-        at = pl.multiple_of(lax.rem(table[ROW, i], rows_here) * blk, blk)
-        ch = pl.multiple_of(table[COL, i] * blk, blk)
-        return (
-            pltpu.make_async_copy(tokens.at[:, pl.ds(at, blk)], xo.at[i], xsem.at[i]),
-            pltpu.make_async_copy(hidden.at[:, pl.ds(ch, blk)], hb.at[i], hsem.at[i]),
-        )
-
-    def start(i):
-        for c in copies(i):
-            c.start()
-
-    def wait(i):
-        for c in copies(i):
-            c.wait()
-
-    loop(count, start)
+    def column(i):
+        at = pl.multiple_of(table[COL, i] * blk, blk)
+        return pltpu.make_async_copy(hidden.at[:, pl.ds(at, blk)], hb.at[i], hsem.at[i])
+
+    loop(count, lambda i: column(i).start())
     find_first(table, COL, CFIRST, count)
     find_first(table, ROW, RFIRST, count)
-    loop(count, wait)
-
-
-def forward_backward(lo, table, weights, xo, hb, remote, xs, pre, grads):
+    done = pltpu.make_async_copy(table, listed, tsem)
+    done.start()
+    for m in range(2):
+        p = jnp.int32(m * live)
+        for k in range(shards):
+            for j in range(cap):
+                weights[p] = packed[k][pl.ds((2 * j + m) * blk, blk), :]
+                p = p + jnp.where(info[k, 0, 2 * j + m] >= 0, 1, 0).astype(I32)
+    loop(count, lambda i: column(i).wait())
+    done.wait()
+
+
+def forward_backward(lo, listed, table, tsem, weights, tokens, hb, remote, xs, pre, grads):
+    fetch = pltpu.make_async_copy(listed, table, tsem)
+    fetch.start()
     count, size, blk = xs.shape
     live = count // 2
     rows_here = remote[0].shape[1] // blk
     n_tensor = len(remote) + 1
     t = lax.axis_index("tensor")
     pre[...] = jnp.zeros_like(pre)
+    fetch.wait()
 
     def forward(i):
         r = table[ROW, i]
         part = lax.rem(lax.div(r, rows_here) - t + n_tensor, n_tensor)
         at = pl.multiple_of(lax.rem(r, rows_here) * blk, blk)
-        x = xo[i, pl.ds(lo, size), :]
+        x = tokens[pl.ds(lo, size), pl.ds(at, blk)]
         for n, ref in enumerate(remote):
             x = jnp.where(part == n + 1, ref[:, pl.ds(at, blk)], x)
         xs[i] = x
@@ -178,10 +176,10 @@
     loop(count, put)
 
 
-def first_kernel(n_tensor, table, weights, xo, hb, *refs):
+def first_kernel(n_tensor, listed, weights, tokens, hb, *refs):
     remote, refs = refs[: n_tensor - 1], refs[n_tensor - 1 :]
-    back, tile_sums, xs, pre, grads, acc = refs
-    forward_backward(0, table, weights, xo, hb, remote, xs, pre, grads)
+    back, tile_sums, xs, pre, grads, acc, table, tsem = refs
+    forward_backward(0, listed, table, tsem, weights, tokens, hb, remote, xs, pre, grads)
 
     def tile(i):
         tile_sums[i] = dot(xs[i], grads[i], ((0,), (0,)))
@@ -196,11 +194,11 @@
     back[pl.ds(count * size, INFO_ROWS), :] = rows.astype(F32).astype(BF16)
 
 
-def second_kernel(n_tensor, lo, cap, table, weights, xo, hb, tile_sums, *refs):
+def second_kernel(n_tensor, lo, cap, listed, weights, tokens, hb, tile_sums, *refs):
     remote, refs = refs[: n_tensor - 1], refs[n_tensor - 1 :]
-    own, send, back, grads, xs, pre, both, acc = refs
-    forward_backward(lo, table, weights, xo, hb, remote, xs, pre, grads)
+    own, send, back, grads, xs, pre, both, acc, table, tsem = refs
     both[...] = jnp.zeros_like(both)
+    forward_backward(lo, listed, table, tsem, weights, tokens, hb, remote, xs, pre, grads)
     s = lax.axis_index("seq")
     live = xs.shape[0] // 2
 
@@ -220,16 +218,25 @@
         total[...] = (own[k] + other[k].astype(F32)).astype(total.dtype)
 
 
-def add_blocks(rows, parts, count, block, wide, out, lo, sem):
+def place_chunk(n_tensor, count, lo, refs, meanwhile=None):
+    infos, refs = refs[:n_tensor], refs[n_tensor:]
+    parts, refs = refs[:n_tensor], refs[n_tensor:]
+    out, ints, rows, isem, block, wide, sem = refs
     size = block.shape[0]
     blk = parts[0].shape[1]
-    n_tensor = len(parts)
+    for n, info in enumerate(infos):
+        ints[n] = info[...].astype(F32)[:8].astype(I32)
+    fetch = pltpu.make_async_copy(ints, rows, isem)
+    fetch.start()
     total = block if n_tensor == 2 else wide
     total[...] = jnp.zeros_like(total)
+    if meanwhile is not None:
+        meanwhile()
+    fetch.wait()
     for n, part in enumerate(parts):
 
         def add(i):
-            at = pl.ds(pl.multiple_of(rows[n, i] * blk, blk), blk)
+            at = pl.ds(pl.multiple_of(rows[n, 0, i] * blk, blk), blk)
             term = part[pl.ds(pl.multiple_of(i * size, size), size), :].astype(F32)
             total[:, at] = (total[:, at].astype(F32) + term).astype(total.dtype)
 
@@ -238,37 +245,28 @@
         block[...] = wide[...].astype(BF16)
     copy = pltpu.make_async_copy(block, out.at[pl.ds(lo, size), :], sem)
     copy.start()
-    return copy
+    copy.wait()
 
 
 def place_early_kernel(n_tensor, count, *refs):
-    infos, refs = refs[:n_tensor], refs[n_tensor:]
-    parts, refs = refs[:n_tensor], refs[n_tensor:]
-    out, rows, ints, info, isem, block, wide, sem = refs
-    for n, part in enumerate(infos):
-        ints[n] = part[...].astype(F32)[:8].astype(I32)
-    fetch = pltpu.make_async_copy(ints, info, isem)
-    fetch.start()
-    fetch.wait()
-    for n in range(n_tensor):
-        for i in range(count):
-            rows[n, i] = info[n, 0, i]
-    add_blocks(rows, parts, count, block, wide, out, 0, sem).wait()
-
-
-def place_late_kernel(n_tensor, shards, lo, count, rows, *refs):
-    parts, refs = refs[:n_tensor], refs[n_tensor:]
+    place_chunk(n_tensor, count, 0, refs)
+
+
+def place_late_kernel(n_tensor, shards, lo, count, *refs):
+    first, refs = refs[: 2 * n_tensor], refs[2 * n_tensor :]
     _, mine, *others = refs[: shards + 1]
-    out, tile_grads, block, wide, sem, tile_sum, tile_sem = refs[shards + 1 :]
-    total = mine[...]
-    for other in others:
-        total = total + other[...].astype(F32)
-    tile_sum[...] = total.astype(BF16)
+    out, tile_grads, *scratch, tile_sum, tile_sem = refs[shards + 1 :]
     tile_copy = pltpu.make_async_copy(tile_sum, tile_grads, tile_sem)
-    tile_copy.start()
-    copy = add_blocks(rows, parts, count, block, wide, out, lo, sem)
+
+    def add_tiles():
+        total = mine[...]
+        for other in others:
+            total = total + other[...].astype(F32)
+        tile_sum[...] = total.astype(BF16)
+        tile_copy.start()
+
+    place_chunk(n_tensor, count, lo, (*first, out, *scratch), add_tiles)
     tile_copy.wait()
-    copy.wait()
 
 
 def local(sizes, tokens, hidden_grad, tile_blocks, tile_keep, tile_count):
@@ -279,13 +277,14 @@
     width = tokens.shape[1] * n_tensor
     cols = hidden_grad.shape[1] // blk
     count = shards * cap
-    cut = toks * 3 // 4 // 16 * 16
+    cut = toks * 13 // 16 // 16 * 16
     rest = toks - cut
     vmem = pl.BlockSpec(memory_space=pltpu.VMEM)
     smem = pl.BlockSpec(memory_space=pltpu.SMEM)
     hbm = pl.BlockSpec(memory_space=pltpu.HBM)
     spare = pltpu.CompilerParams(vmem_limit_bytes=(16 if count <= 8 else 40) * 2**20)
     swap = shift(2, 1)
+    order = [shards // 2] + [k for k in range(shards - 1, 0, -1) if k != shards // 2]
 
     def shape(dims, kind):
         return jax.ShapeDtypeStruct(dims, kind)
@@ -310,43 +309,45 @@
         lax.ppermute(packed, "fsdp", swaps(shards, k)) for k in range(1, shards)
     ]
 
-    table, weights, xo, hb = pl.pallas_call(
+    listed, weights, hb = pl.pallas_call(
         functools.partial(prepare_kernel, shards, cap),
         out_shape=(
-            shape((5, count + 1), I32),
+            shape((8, blk), I32),
             shape((count + 1, blk, blk), BF16),
             shape((count, toks, blk), BF16),
-            shape((count, toks, blk), BF16),
         ),
-        in_specs=[vmem] * shards + [hbm, hbm],
-        out_specs=(smem, vmem, vmem, vmem),
+        in_specs=[vmem] * shards + [hbm],
+        out_specs=(vmem, vmem, vmem),
         scratch_shapes=[
             pltpu.VMEM((shards, 8, blk), I32),
             pltpu.SMEM((shards, 8, blk), I32),
-            pltpu.SemaphoreType.DMA,
-            pltpu.SemaphoreType.DMA((count,)),
+            pltpu.SMEM((8, blk), I32),
+            pltpu.SemaphoreType.DMA,
+            pltpu.SemaphoreType.DMA,
             pltpu.SemaphoreType.DMA((count,)),
         ],
         compiler_params=pltpu.CompilerParams(vmem_limit_bytes=50 * 2**20),
         cost_estimate=cost(0.001),
         name="prepare",
-    )(*gathered, tokens, hidden_grad)
+    )(*gathered, hidden_grad)
 
     back_early, tile_sums = pl.pallas_call(
         functools.partial(first_kernel, n_tensor),
         out_shape=(shape((count * cut + INFO_ROWS, blk), BF16), shape((count, blk, blk), F32)),
-        in_specs=[smem] + [vmem] * (2 + n_tensor),
+        in_specs=[vmem] * (3 + n_tensor),
         out_specs=(vmem, vmem),
         scratch_shapes=[
             pltpu.VMEM((count, cut, blk), BF16),
             pltpu.VMEM((2, count, cut, blk), F32),
             pltpu.VMEM((count, cut, blk), BF16),
             pltpu.VMEM((count, cut, blk), F32),
+            pltpu.SMEM((8, blk), I32),
+            pltpu.SemaphoreType.DMA,
         ],
         compiler_params=spare,
         cost_estimate=cost(0.001),
         name="early_terms",
-    )(table, weights, xo, hb, *early)
+    )(listed, weights, tokens, hb, *early)
 
     own, send, back_late = pl.pallas_call(
         functools.partial(second_kernel, n_tensor, cut, cap),
@@ -355,7 +356,7 @@
             shape((shards, 2, blk, blk), BF16),
             shape((count * rest, blk), BF16),
         ),
-        in_specs=[smem] + [vmem] * (3 + n_tensor),
+        in_specs=[vmem] * (4 + n_tensor),
         out_specs=(vmem,) * 3,
         scratch_shapes=[
             pltpu.VMEM((count, rest, blk), BF16),
@@ -363,11 +364,13 @@
             pltpu.VMEM((2, count, rest, blk), F32),
             pltpu.VMEM((cap, shards, 2, blk, blk), F32),
             pltpu.VMEM((count, rest, blk), F32),
+            pltpu.SMEM((8, blk), I32),
+            pltpu.SemaphoreType.DMA,
         ],
         compiler_params=spare,
         cost_estimate=cost(0.001),
         name="late_tiles",
-    )(table, weights, xo, hb, tile_sums, *late)
+    )(listed, weights, tokens, hb, tile_sums, *late)
     other = lax.ppermute(send, "seq", swap)
     mine, *rounded = pl.pallas_call(
         pair_kernel,
@@ -379,7 +382,7 @@
         name="pair",
     )(own, other)
     others = [
-        lax.ppermute(rounded[k - 1], "fsdp", swaps(shards, k)) for k in range(shards - 1, 0, -1)
+        lax.ppermute(rounded[k - 1], "fsdp", swaps(shards, k)) for k in order
     ]
 
     def of_all(a):
@@ -388,28 +391,24 @@
         everyone = lax.all_gather(a, "tensor")
         return [everyone[n] for n in range(n_tensor)]
 
-    def block_scratch(size):
+    def scratch(size):
         return [
+            pltpu.VMEM((n_tensor, 8, blk), I32),
+            pltpu.SMEM((n_tensor, 8, blk), I32),
+            pltpu.SemaphoreType.DMA,
             pltpu.VMEM((size, width), BF16),
             pltpu.VMEM((size, width) if n_tensor != 2 else (8, 128), F32),
+            pltpu.SemaphoreType.DMA,
         ]
 
     parts = of_all(back_early)
     infos = [part[count * cut :] for part in parts]
-    if n_tensor == 2:
-        pass
-    token_grad, rows = pl.pallas_call(
+    token_grad = pl.pallas_call(
         functools.partial(place_early_kernel, n_tensor, count),
-        out_shape=(shape((toks, width), BF16), shape((n_tensor, count), I32)),
+        out_shape=shape((toks, width), BF16),
         in_specs=[vmem] * (2 * n_tensor),
-        out_specs=(hbm, smem),
-        scratch_shapes=[
-            pltpu.VMEM((n_tensor, 8, blk), I32),
-            pltpu.SMEM((n_tensor, 8, blk), I32),
-            pltpu.SemaphoreType.DMA,
-            *block_scratch(cut),
-            pltpu.SemaphoreType.DMA,
-        ],
+        out_specs=hbm,
+        scratch_shapes=scratch(cut),
         compiler_params=spare,
         cost_estimate=cost(0.001),
         name="place_early",
@@ -417,19 +416,18 @@
     token_grad, tile_grads = pl.pallas_call(
         functools.partial(place_late_kernel, n_tensor, shards, cut, count),
         out_shape=(shape((toks, width), BF16), shape((2, blk, blk), BF16)),
-        in_specs=[smem] + [vmem] * n_tensor + [hbm] + [vmem] * shards,
+        in_specs=[vmem] * (2 * n_tensor) + [hbm] + [vmem] * shards,
         out_specs=(hbm, hbm),
         scratch_shapes=[
-            *block_scratch(rest),
-            pltpu.SemaphoreType.DMA,
+            *scratch(rest),
             pltpu.VMEM((2, blk, blk), BF16),
             pltpu.SemaphoreType.DMA,
         ],
-        input_output_aliases={n_tensor + 1: 0},
+        input_output_aliases={2 * n_tensor: 0},
         compiler_params=spare,
         cost_estimate=cost(0.001),
         name="place_late",
-    )(rows, *of_all(back_late), token_grad, mine, *others)
+    )(*infos, *of_all(back_late), token_grad, mine, *others)
     return token_grad, tile_grads.reshape(1, 1, 1, 2, blk, blk)
 
 

time: 43.9 us -> 43.1 us (0.982)
  local copies, waits for them, and re-layouts: 2.26 us -> 3.56 us
  Pallas kernels: 11 us -> 9.95 us
  starting transfers between devices: 16.8 us -> 15.9 us
    unnamed x8, local copies, waits for them, and re-layouts: 0.02 us -> 2.24 us
    ppermute x2, waiting for transfers between devices: 1.19 us -> 2.64 us  [of_all(): return [a, lax.ppermute(a, 'tensor', swap)]]
    ppermute x3, starting transfers between devices: 5.22 us -> 4.22 us  [local(): lax.ppermute(rounded[k - 1], 'fsdp', swaps(shards, k))]
    ppermute x3, waiting for transfers between devices: 1.13 us -> 0.14 us  [local(): lax.ppermute(rounded[k - 1], 'fsdp', swaps(shards, k))]
    slice x1, local copies, waits for them, and re-layouts: 0.97 us -> 0.01 us  [local(): late = to_partners(tokens[cut:])]
    pallas_call x1, Pallas kernels: 2.81 us -> 2.07 us  [local(): pl.pallas_call(functools.partial(prepare_kernel, shards, cap), out_shape=...]
    pallas_call x1, Pallas kernels: 2.91 us -> 2.38 us  [local(): pl.pallas_call(functools.partial(place_early_kernel, n_tensor, count), ou...]
  transfers between devices with their start and end apart: 11 -> 11, of which waited for: 5 -> 5; matrix products, arithmetic and copies ran while one was open for 2% -> 0% of each run, Pallas kernels for 22% -> 19%
where the time goes in v4:
time: 43.1 us; the launch traced here: 42.9 us
  starting transfers between devices  15.9 us (37%)
  waiting for transfers between devices  12.7 us (29%)
  Pallas kernels  9.95 us (23%)
  local copies, waits for them, and re-layouts  3.56 us (8%)
  between operations  0.73 us (2%)
    ppermute x3, waiting for transfers between devices, local(): lax.ppermute(packed, 'fsdp', swaps(shards, k))  9.88 us
    ppermute x3, starting transfers between devices, local(): lax.ppermute(packed, 'fsdp', swaps(shards, k))  4.45 us
    ppermute x3, starting transfers between devices, local(): lax.ppermute(rounded[k - 1], 'fsdp', swaps(shards, k))  4.22 us
    ppermute x2, starting transfers between devices, of_all(): return [a, lax.ppermute(a, 'tensor', swap)]  3.7 us
    ppermute x2, starting transfers between devices, to_partners(): lax.ppermute(a, 'tensor', shift(n_tensor, n_tensor - k))  3.46 us
    ppermute x2, waiting for transfers between devices, of_all(): return [a, lax.ppermute(a, 'tensor', swap)]  2.64 us
    pallas_call x1, Pallas kernels, local(): pl.pallas_call(functools.partial(place_early_kernel, n_tensor, count), ou...  2.38 us
    unnamed x8, local copies, waits for them, and re-layouts  2.24 us
  transfers between devices with their start and end apart: 11, of which 5 were waited for; matrix products, arithmetic and copies ran while one was open for 0% of the time, Pallas kernels for 19%

profile of v4, /device:TPU:0, one launch (start us, length us, event | category | flops | bytes accessed | tf_op | source)
XLA Modules:
  0.0 42.9 jit_solution(1498346163891776456)
XLA Ops:
  0.6 1.3 %slice.12 = bf16[208,2048]{1,0:T(8,128)(2,1)S(1)} slice(bf16[256,2048]{1,0:T(8,128)(2,1)} %tokens.3), slice={[0:208], [0:2048]} | slice | bytes 1703936 | tf_op jit(solution)/shard_map/slice | solution.py:297
  1.9 3.0 %collective-permute-start.3 = (bf16[208,2048]{1,0:T(8,128)(2,1)S(1)}, bf16[208,2048]{1,0:T(8,128)(2,1)S(1)}, u32[]{:S(2)}, u32[]{:S(2)}) collective-permute-start(bf16[208,2048]{1,0:T(8,128)(2,1)S(1)} %slice.12), channel_id=1, source_target_pairs={{0,2},{2,0},{1,3},{3,1},{4,6},{6,4},{5,7},{7,5},{8,10},{10,8},{9,1... | collective-permute-start | bytes 2555912 | tf_op jit(solution)/shard_map/ppermute | solution.py:294
  4.9 0.9 %copy-done.1 = bf16[1,1,2,2,128,128]{5,4,3,2,1,0:T(8,128)(2,1)S(1)} copy-done((bf16[1,1,2,2,128,128]{5,4,3,2,1,0:T(8,128)(2,1)S(1)}, bf16[1,1,2,2,128,128]{5,4,3,2,1,0:T(8,128)(2,1)}, u32[]{:S(2)}) %copy-start.1) | copy-done | bytes 131096
  5.9 0.7 %copy-done.2 = s32[1,1,2,2]{3,2,1,0:T(2,128)S(1)} copy-done((s32[1,1,2,2]{3,2,1,0:T(2,128)S(1)}, s32[1,1,2,2]{3,2,1,0:T(2,128)}, u32[]{:S(2)}) %copy-start.2) | copy-done | bytes 40
  6.5 0.7 %copy-done.3 = s32[1,1,2]{2,1,0:T(1,128)S(1)} copy-done((s32[1,1,2]{2,1,0:T(1,128)S(1)}, s32[1,1,2]{2,1,0:T(1,128)}, u32[]{:S(2)}) %copy-start.3) | copy-done | bytes 32
  7.2 0.6 %pack.1.refs_0_ = bf16[528,128]{1,0:T(8,128)(2,1)S(1)} custom-call(s32[1,1,2,2]{3,2,1,0:T(2,128)S(1)} %copy-done.2, s32[1,1,2]{2,1,0:T(1,128)S(1)} %copy-done.3, bf16[1,1,2,2,128,128]{5,4,3,2,1,0:T(8,128)(2,1)S(1)} %copy-done.1), custom_call_target="tpu_custom_call" | custom-call | bytes 3690 | tf_op jit(solution)/shard_map/pack/pallas_call | solution.py:298
  7.8 3.7 %collective-permute-start.2 = (bf16[528,128]{1,0:T(8,128)(2,1)S(1)}, bf16[528,128]{1,0:T(8,128)(2,1)S(1)}, u32[]{:S(2)}, u32[]{:S(2)}) collective-permute-start(bf16[528,128]{1,0:T(8,128)(2,1)S(1)} %pack.1.refs_0_), channel_id=1, source_target_pairs={{0,12},{4,8},{8,4},{12,0},{1,13},{5,9},{9,5},{13,1},{2,14},{6,10},... | collective-permute-start | bytes 405512 | tf_op jit(solution)/shard_map/ppermute | solution.py:309
  11.4 0.8 %collective-permute-start = (bf16[528,128]{1,0:T(8,128)(2,1)S(1)}, bf16[528,128]{1,0:T(8,128)(2,1)S(1)}, u32[]{:S(2)}, u32[]{:S(2)}) collective-permute-start(bf16[528,128]{1,0:T(8,128)(2,1)S(1)} %pack.1.refs_0_), channel_id=1, source_target_pairs={{0,4},{4,0},{8,12},{12,8},{1,5},{5,1},{9,13},{13,9},{2,6},{6,2},{1... | collective-permute-start | bytes 405512 | tf_op jit(solution)/shard_map/ppermute | solution.py:309
  12.2 0.5 %collective-permute-start.5 = (bf16[48,2048]{1,0:T(8,128)(2,1)S(1)}, bf16[48,2048]{1,0:T(8,128)(2,1)S(1)}, u32[]{:S(2)}, u32[]{:S(2)}) collective-permute-start(bf16[48,2048]{1,0:T(8,128)(2,1)S(1)} %slice.15), channel_id=1, source_target_pairs={{0,2},{2,0},{1,3},{3,1},{4,6},{6,4},{5,7},{7,5},{8,10},{10,8},{9,1... | collective-permute-start | bytes 589832 | tf_op jit(solution)/shard_map/ppermute | solution.py:294
  12.7 3.5 %collective-permute-done.2.refs_3_ = bf16[528,128]{1,0:T(8,128)(2,1)S(1)} collective-permute-done((bf16[528,128]{1,0:T(8,128)(2,1)S(1)}, bf16[528,128]{1,0:T(8,128)(2,1)S(1)}, u32[]{:S(2)}, u32[]{:S(2)}) %collective-permute-start.2) | collective-permute-done | bytes 135200 | tf_op jit(solution)/shard_map/ppermute | solution.py:309
  16.2 6.4 %collective-permute-done.1.refs_2_ = bf16[528,128]{1,0:T(8,128)(2,1)S(1)} collective-permute-done((bf16[528,128]{1,0:T(8,128)(2,1)S(1)}, bf16[528,128]{1,0:T(8,128)(2,1)S(1)}, u32[]{:S(2)}, u32[]{:S(2)}) %collective-permute-start.1) | collective-permute-done | bytes 135200 | tf_op jit(solution)/shard_map/ppermute | solution.py:309
  22.6 2.1 %prepare.1 = (s32[8,128]{1,0:T(8,128)S(1)}, bf16[9,128,128]{2,1,0:T(8,128)(2,1)S(1)}, bf16[8,256,128]{2,1,0:T(8,128)(2,1)S(1)}) custom-call(bf16[528,128]{1,0:T(8,128)(2,1)S(1)} %pack.1.refs_0_, bf16[528,128]{1,0:T(8,128)(2,1)S(1)} %collective-permute-done.refs_1_, bf16[528,128]{1,0:T(8,128)(2,1)S(1)} %collective-permute-done.1.refs_2_, ...), custom_call_target="tpu_custom_call" | custom-call | bytes 3690 | tf_op jit(solution)/shard_map/prepare/pallas_call | solution.py:312
  24.7 2.0 %early_terms.1 = (bf16[1680,128]{1,0:T(8,128)(2,1)S(1)}, f32[8,128,128]{2,1,0:T(8,128)S(1)}) custom-call(s32[8,128]{1,0:T(8,128)S(1)} %get-tuple-element.16.listed, bf16[9,128,128]{2,1,0:T(8,128)(2,1)S(1)} %get-tuple-element.17.weights, bf16[256,2048]{1,0:T(8,128)(2,1)S(1)} %copy-done, bf16[8,256,128]{2,1,0:T(8,128)(2,1)S(1)} %get-tuple-element.18.hb, ...), custom_call_target="tpu_custom_call" | custom-call | bytes 3690 | tf_op jit(solution)/shard_map/early_terms/pallas_call | solution.py:334
  26.7 2.1 %collective-permute-start.4 = (bf16[1680,128]{1,0:T(8,128)(2,1)S(1)}, bf16[1680,128]{1,0:T(8,128)(2,1)S(1)}, u32[]{:S(2)}, u32[]{:S(2)}) collective-permute-start(bf16[1680,128]{1,0:T(8,128)(2,1)S(1)} %get-tuple-element.19.refs_2_), channel_id=1, source_target_pairs={{0,2},{2,0},{1,3},{3,1},{4,6},{6,4},{5,7},{7,5},{8,10},{10,8},{9,1... | collective-permute-start | bytes 1290248 | tf_op jit(solution)/shard_map/ppermute | solution.py:390
  28.9 1.3 %late_tiles.1 = (f32[4,2,128,128]{3,2,1,0:T(8,128)S(1)}, bf16[4,2,128,128]{3,2,1,0:T(8,128)(2,1)S(1)}, bf16[384,128]{1,0:T(8,128)(2,1)S(1)}) custom-call(s32[8,128]{1,0:T(8,128)S(1)} %get-tuple-element.16.listed, bf16[9,128,128]{2,1,0:T(8,128)(2,1)S(1)} %get-tuple-element.17.weights, bf16[256,2048]{1,0:T(8,128)(2,1)S(1)} %copy-done, ...), custom_call_target="tpu_custom_call" | custom-call | bytes 3690 | tf_op jit(solution)/shard_map/late_tiles/pallas_call | solution.py:352
  30.1 0.1 collective-permute-start.7
  30.2 1.6 %collective-permute-start.6 = (bf16[384,128]{1,0:T(8,128)(2,1)S(1)}, bf16[384,128]{1,0:T(8,128)(2,1)S(1)}, u32[]{:S(2)}, u32[]{:S(2)}) collective-permute-start(bf16[384,128]{1,0:T(8,128)(2,1)S(1)} %get-tuple-element.21.refs_2_), channel_id=1, source_target_pairs={{0,2},{2,0},{1,3},{3,1},{4,6},{6,4},{5,7},{7,5},{8,10},{10,8},{9,1... | collective-permute-start | bytes 294920 | tf_op jit(solution)/shard_map/ppermute | solution.py:390
  31.9 2.6 %collective-permute-start.8 = (bf16[2,128,128]{2,1,0:T(8,128)(2,1)S(1)}, bf16[2,128,128]{2,1,0:T(8,128)(2,1)S(1)}, u32[]{:S(2)}, u32[]{:S(2)}) collective-permute-start(bf16[2,128,128]{2,1,0:T(8,128)(2,1)S(1)} %get-tuple-element.25), channel_id=1, source_target_pairs={{0,8},{4,12},{8,0},{12,4},{1,9},{5,13},{9,1},{13,5},{2,10},{6,14},... | collective-permute-start | bytes 196616 | tf_op jit(solution)/shard_map/ppermute | solution.py:385
  34.5 1.4 %collective-permute-start.9 = (bf16[2,128,128]{2,1,0:T(8,128)(2,1)S(1)}, bf16[2,128,128]{2,1,0:T(8,128)(2,1)S(1)}, u32[]{:S(2)}, u32[]{:S(2)}) collective-permute-start(bf16[2,128,128]{2,1,0:T(8,128)(2,1)S(1)} %get-tuple-element.26), channel_id=1, source_target_pairs={{0,12},{4,8},{8,4},{12,0},{1,13},{5,9},{9,5},{13,1},{2,14},{6,10},... | collective-permute-start | bytes 196616 | tf_op jit(solution)/shard_map/ppermute | solution.py:385
  35.9 0.2 collective-permute-start.10
  36.1 2.6 %collective-permute-done.4.refs_3_ = bf16[1680,128]{1,0:T(8,128)(2,1)S(1)} collective-permute-done((bf16[1680,128]{1,0:T(8,128)(2,1)S(1)}, bf16[1680,128]{1,0:T(8,128)(2,1)S(1)}, u32[]{:S(2)}, u32[]{:S(2)}) %collective-permute-start.4) | collective-permute-done | bytes 430112 | tf_op jit(solution)/shard_map/ppermute | solution.py:390
  38.7 2.4 %place_early.1.refs_4_ = bf16[256,4096]{1,0:T(8,128)(2,1)} custom-call(bf16[16,128]{1,0:T(8,128)(2,1)S(1)} %slice.13.refs_0_, bf16[16,128]{1,0:T(8,128)(2,1)S(1)} %slice.16.refs_1_, bf16[1680,128]{1,0:T(8,128)(2,1)S(1)} %get-tuple-element.19.refs_2_, bf16[1680,128]{1,0:T(8,128)(2,1)S(1)} %collective-permute-done.4.refs_3_), custom_call_target="tpu_custom_call" | custom-call | bytes 3690 | tf_op jit(solution)/shard_map/place_early/pallas_call | solution.py:406
  41.1 0.1 collective-permute-done.10.refs_8_
  41.3 1.6 %place_late.1 = (bf16[256,4096]{1,0:T(8,128)(2,1)}, bf16[2,128,128]{2,1,0:T(8,128)(2,1)}) custom-call(bf16[16,128]{1,0:T(8,128)(2,1)S(1)} %slice.13.refs_0_, bf16[16,128]{1,0:T(8,128)(2,1)S(1)} %slice.16.refs_1_, bf16[384,128]{1,0:T(8,128)(2,1)S(1)} %get-tuple-element.21.refs_2_, ...), custom_call_target="tpu_custom_call", output_to_operand_aliasing={{0}: (4, {})} | custom-call | bytes 3690 | tf_op jit(solution)/shard_map/place_late/pallas_call | solution.py:416
  (17 shorter events, 0.2 us)
Async XLA Ops:
  0.6 11.6 %copy-start = (bf16[256,2048]{1,0:T(8,128)(2,1)S(1)}, bf16[256,2048]{1,0:T(8,128)(2,1)}, u32[]{:S(2)}) copy-start(bf16[256,2048]{1,0:T(8,128)(2,1)} %tokens.3) | copy-start | bytes 3145732
  1.9 22.8 %collective-permute-start.3 = (bf16[208,2048]{1,0:T(8,128)(2,1)S(1)}, bf16[208,2048]{1,0:T(8,128)(2,1)S(1)}, u32[]{:S(2)}, u32[]{:S(2)}) collective-permute-start(bf16[208,2048]{1,0:T(8,128)(2,1)S(1)} %slice.12), channel_id=1, source_target_pairs={{0,2},{2,0},{1,3},{3,1},{4,6},{6,4},{5,7},{7,5},{8,10},{10,8},{9,1... | collective-permute-start | bytes 2555912 | tf_op jit(solution)/shard_map/ppermute | solution.py:294
  4.9 0.9 %copy-start.1 = (bf16[1,1,2,2,128,128]{5,4,3,2,1,0:T(8,128)(2,1)S(1)}, bf16[1,1,2,2,128,128]{5,4,3,2,1,0:T(8,128)(2,1)}, u32[]{:S(2)}) copy-start(bf16[1,1,2,2,128,128]{5,4,3,2,1,0:T(8,128)(2,1)} %tiles.1) | copy-start | bytes 393220
  5.8 0.7 %copy-start.2 = (s32[1,1,2,2]{3,2,1,0:T(2,128)S(1)}, s32[1,1,2,2]{3,2,1,0:T(2,128)}, u32[]{:S(2)}) copy-start(s32[1,1,2,2]{3,2,1,0:T(2,128)} %keep.1) | copy-start | bytes 52
  6.5 0.7 %copy-start.3 = (s32[1,1,2]{2,1,0:T(1,128)S(1)}, s32[1,1,2]{2,1,0:T(1,128)}, u32[]{:S(2)}) copy-start(s32[1,1,2]{2,1,0:T(1,128)} %count.1) | copy-start | bytes 28
  7.8 8.4 %collective-permute-start.2 = (bf16[528,128]{1,0:T(8,128)(2,1)S(1)}, bf16[528,128]{1,0:T(8,128)(2,1)S(1)}, u32[]{:S(2)}, u32[]{:S(2)}) collective-permute-start(bf16[528,128]{1,0:T(8,128)(2,1)S(1)} %pack.1.refs_0_), channel_id=1, source_target_pairs={{0,12},{4,8},{8,4},{12,0},{1,13},{5,9},{9,5},{13,1},{2,14},{6,10},... | collective-permute-start | bytes 405512 | tf_op jit(solution)/shard_map/ppermute | solution.py:309
  11.4 11.1 %collective-permute-start.1 = (bf16[528,128]{1,0:T(8,128)(2,1)S(1)}, bf16[528,128]{1,0:T(8,128)(2,1)S(1)}, u32[]{:S(2)}, u32[]{:S(2)}) collective-permute-start(bf16[528,128]{1,0:T(8,128)(2,1)S(1)} %pack.1.refs_0_), channel_id=1, source_target_pairs={{0,8},{4,12},{8,0},{12,4},{1,9},{5,13},{9,1},{13,5},{2,10},{6,14},... | collective-permute-start | bytes 405512 | tf_op jit(solution)/shard_map/ppermute | solution.py:309
  11.4 11.1 %collective-permute-start = (bf16[528,128]{1,0:T(8,128)(2,1)S(1)}, bf16[528,128]{1,0:T(8,128)(2,1)S(1)}, u32[]{:S(2)}, u32[]{:S(2)}) collective-permute-start(bf16[528,128]{1,0:T(8,128)(2,1)S(1)} %pack.1.refs_0_), channel_id=1, source_target_pairs={{0,4},{4,0},{8,12},{12,8},{1,5},{5,1},{9,13},{13,9},{2,6},{6,2},{1... | collective-permute-start | bytes 405512 | tf_op jit(solution)/shard_map/ppermute | solution.py:309
  12.2 16.6 %collective-permute-start.5 = (bf16[48,2048]{1,0:T(8,128)(2,1)S(1)}, bf16[48,2048]{1,0:T(8,128)(2,1)S(1)}, u32[]{:S(2)}, u32[]{:S(2)}) collective-permute-start(bf16[48,2048]{1,0:T(8,128)(2,1)S(1)} %slice.15), channel_id=1, source_target_pairs={{0,2},{2,0},{1,3},{3,1},{4,6},{6,4},{5,7},{7,5},{8,10},{10,8},{9,1... | collective-permute-start | bytes 589832 | tf_op jit(solution)/shard_map/ppermute | solution.py:294
  26.7 12.0 %collective-permute-start.4 = (bf16[1680,128]{1,0:T(8,128)(2,1)S(1)}, bf16[1680,128]{1,0:T(8,128)(2,1)S(1)}, u32[]{:S(2)}, u32[]{:S(2)}) collective-permute-start(bf16[1680,128]{1,0:T(8,128)(2,1)S(1)} %get-tuple-element.19.refs_2_), channel_id=1, source_target_pairs={{0,2},{2,0},{1,3},{3,1},{4,6},{6,4},{5,7},{7,5},{8,10},{10,8},{9,1... | collective-permute-start | bytes 1290248 | tf_op jit(solution)/shard_map/ppermute | solution.py:390
  30.1 1.7 %collective-permute-start.7 = (bf16[4,2,128,128]{3,2,1,0:T(8,128)(2,1)S(1)}, bf16[4,2,128,128]{3,2,1,0:T(8,128)(2,1)S(1)}, u32[]{:S(2)}, u32[]{:S(2)}) collective-permute-start(bf16[4,2,128,128]{3,2,1,0:T(8,128)(2,1)S(1)} %get-tuple-element.23), channel_id=1, source_target_pairs={{0,1},{1,0},{2,3},{3,2},{4,5},{5,4},{6,7},{7,6},{8,9},{9,8},{10,11... | collective-permute-start | bytes 786440 | tf_op jit(solution)/shard_map/ppermute | solution.py:374
  30.2 10.9 %collective-permute-start.6 = (bf16[384,128]{1,0:T(8,128)(2,1)S(1)}, bf16[384,128]{1,0:T(8,128)(2,1)S(1)}, u32[]{:S(2)}, u32[]{:S(2)}) collective-permute-start(bf16[384,128]{1,0:T(8,128)(2,1)S(1)} %get-tuple-element.21.refs_2_), channel_id=1, source_target_pairs={{0,2},{2,0},{1,3},{3,1},{4,6},{6,4},{5,7},{7,5},{8,10},{10,8},{9,1... | collective-permute-start | bytes 294920 | tf_op jit(solution)/shard_map/ppermute | solution.py:390
  31.9 9.3 %collective-permute-start.8 = (bf16[2,128,128]{2,1,0:T(8,128)(2,1)S(1)}, bf16[2,128,128]{2,1,0:T(8,128)(2,1)S(1)}, u32[]{:S(2)}, u32[]{:S(2)}) collective-permute-start(bf16[2,128,128]{2,1,0:T(8,128)(2,1)S(1)} %get-tuple-element.25), channel_id=1, source_target_pairs={{0,8},{4,12},{8,0},{12,4},{1,9},{5,13},{9,1},{13,5},{2,10},{6,14},... | collective-permute-start | bytes 196616 | tf_op jit(solution)/shard_map/ppermute | solution.py:385
  34.5 6.6 %collective-permute-start.9 = (bf16[2,128,128]{2,1,0:T(8,128)(2,1)S(1)}, bf16[2,128,128]{2,1,0:T(8,128)(2,1)S(1)}, u32[]{:S(2)}, u32[]{:S(2)}) collective-permute-start(bf16[2,128,128]{2,1,0:T(8,128)(2,1)S(1)} %get-tuple-element.26), channel_id=1, source_target_pairs={{0,12},{4,8},{8,4},{12,0},{1,13},{5,9},{9,5},{13,1},{2,14},{6,10},... | collective-permute-start | bytes 196616 | tf_op jit(solution)/shard_map/ppermute | solution.py:385
  35.9 5.4 %collective-permute-start.10 = (bf16[2,128,128]{2,1,0:T(8,128)(2,1)S(1)}, bf16[2,128,128]{2,1,0:T(8,128)(2,1)S(1)}, u32[]{:S(2)}, u32[]{:S(2)}) collective-permute-start(bf16[2,128,128]{2,1,0:T(8,128)(2,1)S(1)} %get-tuple-element.27), channel_id=1, source_target_pairs={{0,4},{4,0},{8,12},{12,8},{1,5},{5,1},{9,13},{13,9},{2,6},{6,2},{1... | collective-permute-start | bytes 196616 | tf_op jit(solution)/shard_map/ppermute | solution.py:385

commit v5 on v4

--- a/solution.py
+++ b/solution.py
@@ -32,11 +32,11 @@
 
 def find_first(table, src, dst, count):
     def one(i):
-        v = table[src, i]
+        v = table[i, src]
 
         def step(n, best):
             at = i - 1 - n
-            return jnp.where(table[src, at] == v, at, best).astype(I32)
+            return jnp.where(table[at, src] == v, at, best).astype(I32)
 
         if isinstance(i, int):
             best = jnp.int32(i)
@@ -44,7 +44,7 @@
                 best = step(n, best)
         else:
             best = lax.fori_loop(0, i, step, i)
-        table[dst, i] = best
+        table[i, dst] = best
 
     loop(count, one)
 
@@ -78,28 +78,25 @@
 
 def prepare_kernel(shards, cap, *refs):
     packed, refs = refs[:shards], refs[shards:]
-    hidden, listed, weights, hb, ints, info, table, isem, tsem, hsem = refs
+    hidden, listed, weights, hb, info, table, tsem, hsem = refs
     blk = weights.shape[-1]
     base = 2 * cap * blk
     count = hb.shape[0]
     live = count // 2
     for k in range(shards):
-        ints[k] = packed[k][pl.ds(base, INFO_ROWS), :].astype(F32)[:8].astype(I32)
-    fetch = pltpu.make_async_copy(ints, info, isem)
-    fetch.start()
-    fetch.wait()
+        info[k] = packed[k][pl.ds(base, INFO_ROWS), :].astype(F32)[:8].astype(I32)
     for m in range(2):
         p = jnp.int32(m * live)
         for k in range(shards):
             for j in range(cap):
                 r = info[k, 0, 2 * j + m]
-                table[ROW, p] = r
-                table[COL, p] = info[k, 1, 2 * j + m]
-                table[SLOT, p] = k * cap + j
+                table[p, ROW] = r
+                table[p, COL] = info[k, 1, 2 * j + m]
+                table[p, SLOT] = k * cap + j
                 p = p + jnp.where(r >= 0, 1, 0).astype(I32)
 
     def column(i):
-        at = pl.multiple_of(table[COL, i] * blk, blk)
+        at = pl.multiple_of(table[i, COL] * blk, blk)
         return pltpu.make_async_copy(hidden.at[:, pl.ds(at, blk)], hb.at[i], hsem.at[i])
 
     loop(count, lambda i: column(i).start())
@@ -117,32 +114,29 @@
     done.wait()
 
 
-def forward_backward(lo, listed, table, tsem, weights, tokens, hb, remote, xs, pre, grads):
-    fetch = pltpu.make_async_copy(listed, table, tsem)
-    fetch.start()
+def forward_backward(lo, table, weights, tokens, hb, remote, xs, pre, grads):
     count, size, blk = xs.shape
     live = count // 2
     rows_here = remote[0].shape[1] // blk
     n_tensor = len(remote) + 1
     t = lax.axis_index("tensor")
     pre[...] = jnp.zeros_like(pre)
-    fetch.wait()
 
     def forward(i):
-        r = table[ROW, i]
+        r = table[i, ROW]
         part = lax.rem(lax.div(r, rows_here) - t + n_tensor, n_tensor)
         at = pl.multiple_of(lax.rem(r, rows_here) * blk, blk)
         x = tokens[pl.ds(lo, size), pl.ds(at, blk)]
         for n, ref in enumerate(remote):
             x = jnp.where(part == n + 1, ref[:, pl.ds(at, blk)], x)
         xs[i] = x
-        pre[i // live, table[CFIRST, i]] += dot(x, weights[i], ((1,), (0,)))
+        pre[i // live, table[i, CFIRST]] += dot(x, weights[i], ((1,), (0,)))
 
     loop(count, forward)
 
     def backward(i):
         m = i // live
-        f = table[CFIRST, i]
+        f = table[i, CFIRST]
         gate = pre[0, f]
         h = hb[i, pl.ds(lo, size), :].astype(F32)
         sig = 1.0 / (1.0 + jnp.exp(-gate))
@@ -167,7 +161,7 @@
     acc[...] = jnp.zeros_like(acc)
 
     def one(i):
-        acc[table[RFIRST, i]] += dot(grads[i], weights[i], ((1,), (1,)))
+        acc[table[i, RFIRST]] += dot(grads[i], weights[i], ((1,), (1,)))
 
     def put(i):
         back[pl.ds(pl.multiple_of(i * size, size), size), :] = acc[i].astype(BF16)
@@ -176,10 +170,10 @@
     loop(count, put)
 
 
-def first_kernel(n_tensor, listed, weights, tokens, hb, *refs):
+def first_kernel(n_tensor, table, weights, tokens, hb, *refs):
     remote, refs = refs[: n_tensor - 1], refs[n_tensor - 1 :]
-    back, tile_sums, xs, pre, grads, acc, table, tsem = refs
-    forward_backward(0, listed, table, tsem, weights, tokens, hb, remote, xs, pre, grads)
+    back, tile_sums, xs, pre, grads, acc = refs
+    forward_backward(0, table, weights, tokens, hb, remote, xs, pre, grads)
 
     def tile(i):
         tile_sums[i] = dot(xs[i], grads[i], ((0,), (0,)))
@@ -187,24 +181,25 @@
     count, size, blk = xs.shape
     loop(count, tile)
     back_terms(table, weights, grads, acc, back)
-    lane = lax.broadcasted_iota(I32, (INFO_ROWS, blk), 1)
-    rows = jnp.zeros((INFO_ROWS, blk), I32)
+    lines = back.shape[0] - count * size
+    line = lax.broadcasted_iota(I32, (lines, blk), 0)
+    rows = jnp.zeros((lines, blk), I32)
     for i in range(count):
-        rows = jnp.where(lane == i, table[ROW, i], rows)
-    back[pl.ds(count * size, INFO_ROWS), :] = rows.astype(F32).astype(BF16)
-
-
-def second_kernel(n_tensor, lo, cap, listed, weights, tokens, hb, tile_sums, *refs):
+        rows = jnp.where(line == i, table[i, ROW], rows)
+    back[pl.ds(count * size, lines), :] = rows.astype(F32).astype(BF16)
+
+
+def second_kernel(n_tensor, lo, cap, table, weights, tokens, hb, tile_sums, *refs):
     remote, refs = refs[: n_tensor - 1], refs[n_tensor - 1 :]
-    own, send, back, grads, xs, pre, both, acc, table, tsem = refs
+    own, send, back, grads, xs, pre, both, acc = refs
     both[...] = jnp.zeros_like(both)
-    forward_backward(lo, listed, table, tsem, weights, tokens, hb, remote, xs, pre, grads)
+    forward_backward(lo, table, weights, tokens, hb, remote, xs, pre, grads)
     s = lax.axis_index("seq")
     live = xs.shape[0] // 2
 
     def tile(i):
         value = tile_sums[i] + dot(xs[i], grads[i], ((0,), (0,)))
-        slot = table[SLOT, i]
+        slot = table[i, SLOT]
         both[lax.rem(slot + s, cap), lax.div(slot, cap), i // live] = value
 
     loop(xs.shape[0], tile)
@@ -221,22 +216,19 @@
 def place_chunk(n_tensor, count, lo, refs, meanwhile=None):
     infos, refs = refs[:n_tensor], refs[n_tensor:]
     parts, refs = refs[:n_tensor], refs[n_tensor:]
-    out, ints, rows, isem, block, wide, sem = refs
+    out, rows, block, wide, sem = refs
     size = block.shape[0]
     blk = parts[0].shape[1]
     for n, info in enumerate(infos):
-        ints[n] = info[...].astype(F32)[:8].astype(I32)
-    fetch = pltpu.make_async_copy(ints, rows, isem)
-    fetch.start()
+        rows[n] = info[...].astype(F32).astype(I32)
     total = block if n_tensor == 2 else wide
     total[...] = jnp.zeros_like(total)
     if meanwhile is not None:
         meanwhile()
-    fetch.wait()
     for n, part in enumerate(parts):
 
         def add(i):
-            at = pl.ds(pl.multiple_of(rows[n, 0, i] * blk, blk), blk)
+            at = pl.ds(pl.multiple_of(rows[n, i, 0] * blk, blk), blk)
             term = part[pl.ds(pl.multiple_of(i * size, size), size), :].astype(F32)
             total[:, at] = (total[:, at].astype(F32) + term).astype(total.dtype)
 
@@ -279,6 +271,7 @@
     count = shards * cap
     cut = toks * 13 // 16 // 16 * 16
     rest = toks - cut
+    lines = (count // 16 + 1) * 16
     vmem = pl.BlockSpec(memory_space=pltpu.VMEM)
     smem = pl.BlockSpec(memory_space=pltpu.SMEM)
     hbm = pl.BlockSpec(memory_space=pltpu.HBM)
@@ -312,7 +305,7 @@
     listed, weights, hb = pl.pallas_call(
         functools.partial(prepare_kernel, shards, cap),
         out_shape=(
-            shape((8, blk), I32),
+            shape((lines, blk), I32),
             shape((count + 1, blk, blk), BF16),
             shape((count, toks, blk), BF16),
         ),
@@ -320,9 +313,7 @@
         out_specs=(vmem, vmem, vmem),
         scratch_shapes=[
             pltpu.VMEM((shards, 8, blk), I32),
-            pltpu.SMEM((shards, 8, blk), I32),
-            pltpu.SMEM((8, blk), I32),
-            pltpu.SemaphoreType.DMA,
+            pltpu.SMEM((lines, blk), I32),
             pltpu.SemaphoreType.DMA,
             pltpu.SemaphoreType.DMA((count,)),
         ],
@@ -333,7 +324,7 @@
 
     back_early, tile_sums = pl.pallas_call(
         functools.partial(first_kernel, n_tensor),
-        out_shape=(shape((count * cut + INFO_ROWS, blk), BF16), shape((count, blk, blk), F32)),
+        out_shape=(shape((count * cut + lines, blk), BF16), shape((count, blk, blk), F32)),
         in_specs=[vmem] * (3 + n_tensor),
         out_specs=(vmem, vmem),
         scratch_shapes=[
@@ -341,8 +332,6 @@
             pltpu.VMEM((2, count, cut, blk), F32),
             pltpu.VMEM((count, cut, blk), BF16),
             pltpu.VMEM((count, cut, blk), F32),
-            pltpu.SMEM((8, blk), I32),
-            pltpu.SemaphoreType.DMA,
         ],
         compiler_params=spare,
         cost_estimate=cost(0.001),
@@ -364,8 +353,6 @@
             pltpu.VMEM((2, count, rest, blk), F32),
             pltpu.VMEM((cap, shards, 2, blk, blk), F32),
             pltpu.VMEM((count, rest, blk), F32),
-            pltpu.SMEM((8, blk), I32),
-            pltpu.SemaphoreType.DMA,
         ],
         compiler_params=spare,
         cost_estimate=cost(0.001),
@@ -393,9 +380,7 @@
 
     def scratch(size):
         return [
-            pltpu.VMEM((n_tensor, 8, blk), I32),
-            pltpu.SMEM((n_tensor, 8, blk), I32),
-            pltpu.SemaphoreType.DMA,
+            pltpu.VMEM((n_tensor, lines, blk), I32),
             pltpu.VMEM((size, width), BF16),
             pltpu.VMEM((size, width) if n_tensor != 2 else (8, 128), F32),
             pltpu.SemaphoreType.DMA,

time: 43.1 us -> 42.4 us (0.984)
  Pallas kernels: 9.95 us -> 7.28 us
  waiting for transfers between devices: 12.7 us -> 14.1 us
  starting transfers between devices: 15.9 us -> 16.5 us
    ppermute x3, waiting for transfers between devices: 0.14 us -> 1.04 us  [local(): lax.ppermute(rounded[k - 1], 'fsdp', swaps(shards, k))]
    ppermute x2, waiting for transfers between devices: 0.06 us -> 0.82 us  [to_partners(): lax.ppermute(a, 'tensor', shift(n_tensor, n_tensor - k))]
    pallas_call x1, Pallas kernels: 2.07 us -> 1.4 us  [local(): pl.pallas_call(functools.partial(prepare_kernel, shards, cap), out_shape=...]
    pallas_call x1, Pallas kernels: 2.38 us -> 1.73 us  [local(): pl.pallas_call(functools.partial(place_early_kernel, n_tensor, count), ou...]
    pallas_call x1, Pallas kernels: 1.59 us -> 0.98 us  [local(): pl.pallas_call(functools.partial(place_late_kernel, n_tensor, shards, cut...]
    ppermute x2, starting transfers between devices: 3.7 us -> 4.25 us  [of_all(): return [a, lax.ppermute(a, 'tensor', swap)]]
  transfers between devices with their start and end apart: 11 -> 11, of which waited for: 5 -> 7; matrix products, arithmetic and copies ran while one was open for 0% -> 0% of each run, Pallas kernels for 19% -> 15%
where the time goes in v5:
time: 42.4 us; the launch traced here: 42.2 us
  starting transfers between devices  16.5 us (39%)
  waiting for transfers between devices  14.1 us (33%)
  Pallas kernels  7.28 us (17%)
  local copies, waits for them, and re-layouts  3.57 us (8%)
  between operations  0.72 us (2%)
    ppermute x3, waiting for transfers between devices, local(): lax.ppermute(packed, 'fsdp', swaps(shards, k))  9.88 us
    ppermute x3, starting transfers between devices, local(): lax.ppermute(packed, 'fsdp', swaps(shards, k))  4.45 us
    ppermute x2, starting transfers between devices, of_all(): return [a, lax.ppermute(a, 'tensor', swap)]  4.25 us
    ppermute x3, starting transfers between devices, local(): lax.ppermute(rounded[k - 1], 'fsdp', swaps(shards, k))  4.23 us
    ppermute x2, starting transfers between devices, to_partners(): lax.ppermute(a, 'tensor', shift(n_tensor, n_tensor - k))  3.46 us
    ppermute x2, waiting for transfers between devices, of_all(): return [a, lax.ppermute(a, 'tensor', swap)]  2.39 us
    unnamed x8, local copies, waits for them, and re-layouts  2.24 us
    pallas_call x1, Pallas kernels, local(): pl.pallas_call(functools.partial(place_early_kernel, n_tensor, count), ou...  1.73 us
  transfers between devices with their start and end apart: 11, of which 7 were waited for; matrix products, arithmetic and copies ran while one was open for 0% of the time, Pallas kernels for 15%

profile of v5, /device:TPU:0, one launch (start us, length us, event | category | flops | bytes accessed | tf_op | source)
XLA Modules:
  0.0 42.2 jit_solution(6898494325247641538)
XLA Ops:
  0.6 1.3 %slice.12 = bf16[208,2048]{1,0:T(8,128)(2,1)S(1)} slice(bf16[256,2048]{1,0:T(8,128)(2,1)} %tokens.3), slice={[0:208], [0:2048]} | slice | bytes 1703936 | tf_op jit(solution)/shard_map/slice | solution.py:290
  2.0 3.0 %collective-permute-start.3 = (bf16[208,2048]{1,0:T(8,128)(2,1)S(1)}, bf16[208,2048]{1,0:T(8,128)(2,1)S(1)}, u32[]{:S(2)}, u32[]{:S(2)}) collective-permute-start(bf16[208,2048]{1,0:T(8,128)(2,1)S(1)} %slice.12), channel_id=1, source_target_pairs={{0,2},{2,0},{1,3},{3,1},{4,6},{6,4},{5,7},{7,5},{8,10},{10,8},{9,1... | collective-permute-start | bytes 2555912 | tf_op jit(solution)/shard_map/ppermute | solution.py:287
  5.0 0.9 %copy-done.1 = bf16[1,1,2,2,128,128]{5,4,3,2,1,0:T(8,128)(2,1)S(1)} copy-done((bf16[1,1,2,2,128,128]{5,4,3,2,1,0:T(8,128)(2,1)S(1)}, bf16[1,1,2,2,128,128]{5,4,3,2,1,0:T(8,128)(2,1)}, u32[]{:S(2)}) %copy-start.1) | copy-done | bytes 131096
  5.9 0.7 %copy-done.2 = s32[1,1,2,2]{3,2,1,0:T(2,128)S(1)} copy-done((s32[1,1,2,2]{3,2,1,0:T(2,128)S(1)}, s32[1,1,2,2]{3,2,1,0:T(2,128)}, u32[]{:S(2)}) %copy-start.2) | copy-done | bytes 40
  6.6 0.7 %copy-done.3 = s32[1,1,2]{2,1,0:T(1,128)S(1)} copy-done((s32[1,1,2]{2,1,0:T(1,128)S(1)}, s32[1,1,2]{2,1,0:T(1,128)}, u32[]{:S(2)}) %copy-start.3) | copy-done | bytes 32
  7.2 0.6 %pack.1.refs_0_ = bf16[528,128]{1,0:T(8,128)(2,1)S(1)} custom-call(s32[1,1,2,2]{3,2,1,0:T(2,128)S(1)} %copy-done.2, s32[1,1,2]{2,1,0:T(1,128)S(1)} %copy-done.3, bf16[1,1,2,2,128,128]{5,4,3,2,1,0:T(8,128)(2,1)S(1)} %copy-done.1), custom_call_target="tpu_custom_call" | custom-call | bytes 3690 | tf_op jit(solution)/shard_map/pack/pallas_call | solution.py:291
  7.8 3.7 %collective-permute-start.2 = (bf16[528,128]{1,0:T(8,128)(2,1)S(1)}, bf16[528,128]{1,0:T(8,128)(2,1)S(1)}, u32[]{:S(2)}, u32[]{:S(2)}) collective-permute-start(bf16[528,128]{1,0:T(8,128)(2,1)S(1)} %pack.1.refs_0_), channel_id=1, source_target_pairs={{0,12},{4,8},{8,4},{12,0},{1,13},{5,9},{9,5},{13,1},{2,14},{6,10},... | collective-permute-start | bytes 405512 | tf_op jit(solution)/shard_map/ppermute | solution.py:302
  11.5 0.8 %collective-permute-start = (bf16[528,128]{1,0:T(8,128)(2,1)S(1)}, bf16[528,128]{1,0:T(8,128)(2,1)S(1)}, u32[]{:S(2)}, u32[]{:S(2)}) collective-permute-start(bf16[528,128]{1,0:T(8,128)(2,1)S(1)} %pack.1.refs_0_), channel_id=1, source_target_pairs={{0,4},{4,0},{8,12},{12,8},{1,5},{5,1},{9,13},{13,9},{2,6},{6,2},{1... | collective-permute-start | bytes 405512 | tf_op jit(solution)/shard_map/ppermute | solution.py:302
  12.3 0.5 %collective-permute-start.5 = (bf16[48,2048]{1,0:T(8,128)(2,1)S(1)}, bf16[48,2048]{1,0:T(8,128)(2,1)S(1)}, u32[]{:S(2)}, u32[]{:S(2)}) collective-permute-start(bf16[48,2048]{1,0:T(8,128)(2,1)S(1)} %slice.15), channel_id=1, source_target_pairs={{0,2},{2,0},{1,3},{3,1},{4,6},{6,4},{5,7},{7,5},{8,10},{10,8},{9,1... | collective-permute-start | bytes 589832 | tf_op jit(solution)/shard_map/ppermute | solution.py:287
  12.7 3.5 %collective-permute-done.2.refs_3_ = bf16[528,128]{1,0:T(8,128)(2,1)S(1)} collective-permute-done((bf16[528,128]{1,0:T(8,128)(2,1)S(1)}, bf16[528,128]{1,0:T(8,128)(2,1)S(1)}, u32[]{:S(2)}, u32[]{:S(2)}) %collective-permute-start.2) | collective-permute-done | bytes 135200 | tf_op jit(solution)/shard_map/ppermute | solution.py:302
  16.2 6.4 %collective-permute-done.1.refs_2_ = bf16[528,128]{1,0:T(8,128)(2,1)S(1)} collective-permute-done((bf16[528,128]{1,0:T(8,128)(2,1)S(1)}, bf16[528,128]{1,0:T(8,128)(2,1)S(1)}, u32[]{:S(2)}, u32[]{:S(2)}) %collective-permute-start.1) | collective-permute-done | bytes 135200 | tf_op jit(solution)/shard_map/ppermute | solution.py:302
  22.6 1.4 %prepare.1 = (s32[16,128]{1,0:T(8,128)S(1)}, bf16[9,128,128]{2,1,0:T(8,128)(2,1)S(1)}, bf16[8,256,128]{2,1,0:T(8,128)(2,1)S(1)}) custom-call(bf16[528,128]{1,0:T(8,128)(2,1)S(1)} %pack.1.refs_0_, bf16[528,128]{1,0:T(8,128)(2,1)S(1)} %collective-permute-done.refs_1_, bf16[528,128]{1,0:T(8,128)(2,1)S(1)} %collective-permute-done.1.refs_2_, ...), custom_call_target="tpu_custom_call" | custom-call | bytes 3690 | tf_op jit(solution)/shard_map/prepare/pallas_call | solution.py:305
  24.0 0.7 %collective-permute-done.3.refs_0_ = bf16[208,2048]{1,0:T(8,128)(2,1)S(1)} collective-permute-done((bf16[208,2048]{1,0:T(8,128)(2,1)S(1)}, bf16[208,2048]{1,0:T(8,128)(2,1)S(1)}, u32[]{:S(2)}, u32[]{:S(2)}) %collective-permute-start.3) | collective-permute-done | bytes 852000 | tf_op jit(solution)/shard_map/ppermute | solution.py:287
  24.7 1.7 %early_terms.1 = (bf16[1680,128]{1,0:T(8,128)(2,1)S(1)}, f32[8,128,128]{2,1,0:T(8,128)S(1)}) custom-call(s32[16,128]{1,0:T(8,128)S(1)} %get-tuple-element.16.table, bf16[9,128,128]{2,1,0:T(8,128)(2,1)S(1)} %get-tuple-element.17.weights, bf16[256,2048]{1,0:T(8,128)(2,1)S(1)} %copy-done, bf16[8,256,128]{2,1,0:T(8,128)(2,1)S(1)} %get-tuple-element.18.hb, ...), custom_call_target="tpu_custom_call" | custom-call | bytes 3690 | tf_op jit(solution)/shard_map/early_terms/pallas_call | solution.py:325
  26.4 2.1 %collective-permute-start.4 = (bf16[1680,128]{1,0:T(8,128)(2,1)S(1)}, bf16[1680,128]{1,0:T(8,128)(2,1)S(1)}, u32[]{:S(2)}, u32[]{:S(2)}) collective-permute-start(bf16[1680,128]{1,0:T(8,128)(2,1)S(1)} %get-tuple-element.19.refs_2_), channel_id=1, source_target_pairs={{0,2},{2,0},{1,3},{3,1},{4,6},{6,4},{5,7},{7,5},{8,10},{10,8},{9,1... | collective-permute-start | bytes 1290248 | tf_op jit(solution)/shard_map/ppermute | solution.py:377
  28.6 0.9 %late_tiles.1 = (f32[4,2,128,128]{3,2,1,0:T(8,128)S(1)}, bf16[4,2,128,128]{3,2,1,0:T(8,128)(2,1)S(1)}, bf16[384,128]{1,0:T(8,128)(2,1)S(1)}) custom-call(s32[16,128]{1,0:T(8,128)S(1)} %get-tuple-element.16.table, bf16[9,128,128]{2,1,0:T(8,128)(2,1)S(1)} %get-tuple-element.17.weights, bf16[256,2048]{1,0:T(8,128)(2,1)S(1)} %copy-done, ...), custom_call_target="tpu_custom_call" | custom-call | bytes 3690 | tf_op jit(solution)/shard_map/late_tiles/pallas_call | solution.py:341
  29.6 2.1 %collective-permute-start.6 = (bf16[384,128]{1,0:T(8,128)(2,1)S(1)}, bf16[384,128]{1,0:T(8,128)(2,1)S(1)}, u32[]{:S(2)}, u32[]{:S(2)}) collective-permute-start(bf16[384,128]{1,0:T(8,128)(2,1)S(1)} %get-tuple-element.21.refs_2_), channel_id=1, source_target_pairs={{0,2},{2,0},{1,3},{3,1},{4,6},{6,4},{5,7},{7,5},{8,10},{10,8},{9,1... | collective-permute-start | bytes 294920 | tf_op jit(solution)/shard_map/ppermute | solution.py:377
  31.8 2.7 %collective-permute-start.8 = (bf16[2,128,128]{2,1,0:T(8,128)(2,1)S(1)}, bf16[2,128,128]{2,1,0:T(8,128)(2,1)S(1)}, u32[]{:S(2)}, u32[]{:S(2)}) collective-permute-start(bf16[2,128,128]{2,1,0:T(8,128)(2,1)S(1)} %get-tuple-element.25), channel_id=1, source_target_pairs={{0,8},{4,12},{8,0},{12,4},{1,9},{5,13},{9,1},{13,5},{2,10},{6,14},... | collective-permute-start | bytes 196616 | tf_op jit(solution)/shard_map/ppermute | solution.py:372
  34.4 1.3 %collective-permute-start.9 = (bf16[2,128,128]{2,1,0:T(8,128)(2,1)S(1)}, bf16[2,128,128]{2,1,0:T(8,128)(2,1)S(1)}, u32[]{:S(2)}, u32[]{:S(2)}) collective-permute-start(bf16[2,128,128]{2,1,0:T(8,128)(2,1)S(1)} %get-tuple-element.26), channel_id=1, source_target_pairs={{0,12},{4,8},{8,4},{12,0},{1,13},{5,9},{9,5},{13,1},{2,14},{6,10},... | collective-permute-start | bytes 196616 | tf_op jit(solution)/shard_map/ppermute | solution.py:372
  36.0 2.4 %collective-permute-done.4.refs_3_ = bf16[1680,128]{1,0:T(8,128)(2,1)S(1)} collective-permute-done((bf16[1680,128]{1,0:T(8,128)(2,1)S(1)}, bf16[1680,128]{1,0:T(8,128)(2,1)S(1)}, u32[]{:S(2)}, u32[]{:S(2)}) %collective-permute-start.4) | collective-permute-done | bytes 430112 | tf_op jit(solution)/shard_map/ppermute | solution.py:377
  38.4 1.7 %place_early.1.refs_4_ = bf16[256,4096]{1,0:T(8,128)(2,1)} custom-call(bf16[16,128]{1,0:T(8,128)(2,1)S(1)} %slice.13.refs_0_, bf16[16,128]{1,0:T(8,128)(2,1)S(1)} %slice.16.refs_1_, bf16[1680,128]{1,0:T(8,128)(2,1)S(1)} %get-tuple-element.19.refs_2_, bf16[1680,128]{1,0:T(8,128)(2,1)S(1)} %collective-permute-done.4.refs_3_), custom_call_target="tpu_custom_call" | custom-call | bytes 3690 | tf_op jit(solution)/shard_map/place_early/pallas_call | solution.py:391
  40.2 0.7 %collective-permute-done.9.refs_7_ = bf16[2,128,128]{2,1,0:T(8,128)(2,1)S(1)} collective-permute-done((bf16[2,128,128]{2,1,0:T(8,128)(2,1)S(1)}, bf16[2,128,128]{2,1,0:T(8,128)(2,1)S(1)}, u32[]{:S(2)}, u32[]{:S(2)}) %collective-permute-start.9) | collective-permute-done | bytes 65568 | tf_op jit(solution)/shard_map/ppermute | solution.py:372
  40.9 0.3 collective-permute-done.10.refs_8_
  41.2 1.0 %place_late.1 = (bf16[256,4096]{1,0:T(8,128)(2,1)}, bf16[2,128,128]{2,1,0:T(8,128)(2,1)}) custom-call(bf16[16,128]{1,0:T(8,128)(2,1)S(1)} %slice.13.refs_0_, bf16[16,128]{1,0:T(8,128)(2,1)S(1)} %slice.16.refs_1_, bf16[384,128]{1,0:T(8,128)(2,1)S(1)} %get-tuple-element.21.refs_2_, ...), custom_call_target="tpu_custom_call", output_to_operand_aliasing={{0}: (4, {})} | custom-call | bytes 3690 | tf_op jit(solution)/shard_map/place_late/pallas_call | solution.py:401
  (17 shorter events, 0.5 us)
Async XLA Ops:
  0.6 11.6 %copy-start = (bf16[256,2048]{1,0:T(8,128)(2,1)S(1)}, bf16[256,2048]{1,0:T(8,128)(2,1)}, u32[]{:S(2)}) copy-start(bf16[256,2048]{1,0:T(8,128)(2,1)} %tokens.3) | copy-start | bytes 3145732
  2.0 22.8 %collective-permute-start.3 = (bf16[208,2048]{1,0:T(8,128)(2,1)S(1)}, bf16[208,2048]{1,0:T(8,128)(2,1)S(1)}, u32[]{:S(2)}, u32[]{:S(2)}) collective-permute-start(bf16[208,2048]{1,0:T(8,128)(2,1)S(1)} %slice.12), channel_id=1, source_target_pairs={{0,2},{2,0},{1,3},{3,1},{4,6},{6,4},{5,7},{7,5},{8,10},{10,8},{9,1... | collective-permute-start | bytes 2555912 | tf_op jit(solution)/shard_map/ppermute | solution.py:287
  5.0 0.9 %copy-start.1 = (bf16[1,1,2,2,128,128]{5,4,3,2,1,0:T(8,128)(2,1)S(1)}, bf16[1,1,2,2,128,128]{5,4,3,2,1,0:T(8,128)(2,1)}, u32[]{:S(2)}) copy-start(bf16[1,1,2,2,128,128]{5,4,3,2,1,0:T(8,128)(2,1)} %tiles.1) | copy-start | bytes 393220
  5.9 0.7 %copy-start.2 = (s32[1,1,2,2]{3,2,1,0:T(2,128)S(1)}, s32[1,1,2,2]{3,2,1,0:T(2,128)}, u32[]{:S(2)}) copy-start(s32[1,1,2,2]{3,2,1,0:T(2,128)} %keep.1) | copy-start | bytes 52
  6.6 0.7 %copy-start.3 = (s32[1,1,2]{2,1,0:T(1,128)S(1)}, s32[1,1,2]{2,1,0:T(1,128)}, u32[]{:S(2)}) copy-start(s32[1,1,2]{2,1,0:T(1,128)} %count.1) | copy-start | bytes 28
  7.8 8.4 %collective-permute-start.2 = (bf16[528,128]{1,0:T(8,128)(2,1)S(1)}, bf16[528,128]{1,0:T(8,128)(2,1)S(1)}, u32[]{:S(2)}, u32[]{:S(2)}) collective-permute-start(bf16[528,128]{1,0:T(8,128)(2,1)S(1)} %pack.1.refs_0_), channel_id=1, source_target_pairs={{0,12},{4,8},{8,4},{12,0},{1,13},{5,9},{9,5},{13,1},{2,14},{6,10},... | collective-permute-start | bytes 405512 | tf_op jit(solution)/shard_map/ppermute | solution.py:302
  11.5 11.1 %collective-permute-start.1 = (bf16[528,128]{1,0:T(8,128)(2,1)S(1)}, bf16[528,128]{1,0:T(8,128)(2,1)S(1)}, u32[]{:S(2)}, u32[]{:S(2)}) collective-permute-start(bf16[528,128]{1,0:T(8,128)(2,1)S(1)} %pack.1.refs_0_), channel_id=1, source_target_pairs={{0,8},{4,12},{8,0},{12,4},{1,9},{5,13},{9,1},{13,5},{2,10},{6,14},... | collective-permute-start | bytes 405512 | tf_op jit(solution)/shard_map/ppermute | solution.py:302
  11.5 11.1 %collective-permute-start = (bf16[528,128]{1,0:T(8,128)(2,1)S(1)}, bf16[528,128]{1,0:T(8,128)(2,1)S(1)}, u32[]{:S(2)}, u32[]{:S(2)}) collective-permute-start(bf16[528,128]{1,0:T(8,128)(2,1)S(1)} %pack.1.refs_0_), channel_id=1, source_target_pairs={{0,4},{4,0},{8,12},{12,8},{1,5},{5,1},{9,13},{13,9},{2,6},{6,2},{1... | collective-permute-start | bytes 405512 | tf_op jit(solution)/shard_map/ppermute | solution.py:302
  12.3 16.4 %collective-permute-start.5 = (bf16[48,2048]{1,0:T(8,128)(2,1)S(1)}, bf16[48,2048]{1,0:T(8,128)(2,1)S(1)}, u32[]{:S(2)}, u32[]{:S(2)}) collective-permute-start(bf16[48,2048]{1,0:T(8,128)(2,1)S(1)} %slice.15), channel_id=1, source_target_pairs={{0,2},{2,0},{1,3},{3,1},{4,6},{6,4},{5,7},{7,5},{8,10},{10,8},{9,1... | collective-permute-start | bytes 589832 | tf_op jit(solution)/shard_map/ppermute | solution.py:287
  26.4 12.0 %collective-permute-start.4 = (bf16[1680,128]{1,0:T(8,128)(2,1)S(1)}, bf16[1680,128]{1,0:T(8,128)(2,1)S(1)}, u32[]{:S(2)}, u32[]{:S(2)}) collective-permute-start(bf16[1680,128]{1,0:T(8,128)(2,1)S(1)} %get-tuple-element.19.refs_2_), channel_id=1, source_target_pairs={{0,2},{2,0},{1,3},{3,1},{4,6},{6,4},{5,7},{7,5},{8,10},{10,8},{9,1... | collective-permute-start | bytes 1290248 | tf_op jit(solution)/shard_map/ppermute | solution.py:377
  29.5 2.2 %collective-permute-start.7 = (bf16[4,2,128,128]{3,2,1,0:T(8,128)(2,1)S(1)}, bf16[4,2,128,128]{3,2,1,0:T(8,128)(2,1)S(1)}, u32[]{:S(2)}, u32[]{:S(2)}) collective-permute-start(bf16[4,2,128,128]{3,2,1,0:T(8,128)(2,1)S(1)} %get-tuple-element.23), channel_id=1, source_target_pairs={{0,1},{1,0},{2,3},{3,2},{4,5},{5,4},{6,7},{7,6},{8,9},{9,8},{10,11... | collective-permute-start | bytes 786440 | tf_op jit(solution)/shard_map/ppermute | solution.py:361
  29.6 10.6 %collective-permute-start.6 = (bf16[384,128]{1,0:T(8,128)(2,1)S(1)}, bf16[384,128]{1,0:T(8,128)(2,1)S(1)}, u32[]{:S(2)}, u32[]{:S(2)}) collective-permute-start(bf16[384,128]{1,0:T(8,128)(2,1)S(1)} %get-tuple-element.21.refs_2_), channel_id=1, source_target_pairs={{0,2},{2,0},{1,3},{3,1},{4,6},{6,4},{5,7},{7,5},{8,10},{10,8},{9,1... | collective-permute-start | bytes 294920 | tf_op jit(solution)/shard_map/ppermute | solution.py:377
  31.8 8.4 %collective-permute-start.8 = (bf16[2,128,128]{2,1,0:T(8,128)(2,1)S(1)}, bf16[2,128,128]{2,1,0:T(8,128)(2,1)S(1)}, u32[]{:S(2)}, u32[]{:S(2)}) collective-permute-start(bf16[2,128,128]{2,1,0:T(8,128)(2,1)S(1)} %get-tuple-element.25), channel_id=1, source_target_pairs={{0,8},{4,12},{8,0},{12,4},{1,9},{5,13},{9,1},{13,5},{2,10},{6,14},... | collective-permute-start | bytes 196616 | tf_op jit(solution)/shard_map/ppermute | solution.py:372
  34.4 6.4 %collective-permute-start.9 = (bf16[2,128,128]{2,1,0:T(8,128)(2,1)S(1)}, bf16[2,128,128]{2,1,0:T(8,128)(2,1)S(1)}, u32[]{:S(2)}, u32[]{:S(2)}) collective-permute-start(bf16[2,128,128]{2,1,0:T(8,128)(2,1)S(1)} %get-tuple-element.26), channel_id=1, source_target_pairs={{0,12},{4,8},{8,4},{12,0},{1,13},{5,9},{9,5},{13,1},{2,14},{6,10},... | collective-permute-start | bytes 196616 | tf_op jit(solution)/shard_map/ppermute | solution.py:372
  35.8 5.4 %collective-permute-start.10 = (bf16[2,128,128]{2,1,0:T(8,128)(2,1)S(1)}, bf16[2,128,128]{2,1,0:T(8,128)(2,1)S(1)}, u32[]{:S(2)}, u32[]{:S(2)}) collective-permute-start(bf16[2,128,128]{2,1,0:T(8,128)(2,1)S(1)} %get-tuple-element.27), channel_id=1, source_target_pairs={{0,4},{4,0},{8,12},{12,8},{1,5},{5,1},{9,13},{13,9},{2,6},{6,2},{1... | collective-permute-start | bytes 196616 | tf_op jit(solution)/shard_map/ppermute | solution.py:372

commit v6 on v5

--- a/solution.py
+++ b/solution.py
@@ -244,21 +244,17 @@
     place_chunk(n_tensor, count, 0, refs)
 
 
-def place_late_kernel(n_tensor, shards, lo, count, *refs):
-    first, refs = refs[: 2 * n_tensor], refs[2 * n_tensor :]
-    _, mine, *others = refs[: shards + 1]
-    out, tile_grads, *scratch, tile_sum, tile_sem = refs[shards + 1 :]
-    tile_copy = pltpu.make_async_copy(tile_sum, tile_grads, tile_sem)
-
-    def add_tiles():
-        total = mine[...]
-        for other in others:
-            total = total + other[...].astype(F32)
-        tile_sum[...] = total.astype(BF16)
-        tile_copy.start()
-
-    place_chunk(n_tensor, count, lo, (*first, out, *scratch), add_tiles)
-    tile_copy.wait()
+def place_late_kernel(n_tensor, lo, count, *refs):
+    first, (_, *rest) = refs[: 2 * n_tensor], refs[2 * n_tensor :]
+    place_chunk(n_tensor, count, lo, (*first, *rest))
+
+
+def sum_kernel(mine, *refs):
+    *others, tile_grads = refs
+    total = mine[...]
+    for other in others:
+        total = total + other[...].astype(F32)
+    tile_grads[...] = total.astype(BF16)
 
 
 def local(sizes, tokens, hidden_grad, tile_blocks, tile_keep, tile_count):
@@ -398,21 +394,27 @@
         cost_estimate=cost(0.001),
         name="place_early",
     )(*infos, *parts)
-    token_grad, tile_grads = pl.pallas_call(
-        functools.partial(place_late_kernel, n_tensor, shards, cut, count),
-        out_shape=(shape((toks, width), BF16), shape((2, blk, blk), BF16)),
-        in_specs=[vmem] * (2 * n_tensor) + [hbm] + [vmem] * shards,
-        out_specs=(hbm, hbm),
-        scratch_shapes=[
-            *scratch(rest),
-            pltpu.VMEM((2, blk, blk), BF16),
-            pltpu.SemaphoreType.DMA,
-        ],
+    token_grad = pl.pallas_call(
+        functools.partial(place_late_kernel, n_tensor, cut, count),
+        out_shape=shape((toks, width), BF16),
+        in_specs=[vmem] * (2 * n_tensor) + [hbm],
+        out_specs=hbm,
+        scratch_shapes=scratch(rest),
         input_output_aliases={2 * n_tensor: 0},
         compiler_params=spare,
         cost_estimate=cost(0.001),
         name="place_late",
-    )(*infos, *of_all(back_late), token_grad, mine, *others)
+    )(*infos, *of_all(back_late), token_grad)
+    token_grad, mine = lax.optimization_barrier((token_grad, mine))
+    tile_grads = pl.pallas_call(
+        sum_kernel,
+        out_shape=shape((2, blk, blk), BF16),
+        in_specs=[vmem] * shards,
+        out_specs=vmem,
+        compiler_params=spare,
+        cost_estimate=cost(0.001),
+        name="sum",
+    )(mine, *others)
     return token_grad, tile_grads.reshape(1, 1, 1, 2, blk, blk)
 
 

time: 42.4 us -> 42.1 us (level)
  waiting for transfers between devices: 14.1 us -> 13 us
  Pallas kernels: 7.28 us -> 8.03 us
    ppermute x3, waiting for transfers between devices: 1.04 us -> 0.07 us  [local(): lax.ppermute(rounded[k - 1], 'fsdp', swaps(shards, k))]
    pallas_call x1 -> x2, Pallas kernels: 0.98 us -> 1.63 us  [the longest x1 0.96 us: local(): pl.pallas_call(functools.partial(place_late_kernel, n_tensor, cut, count)...]
  transfers between devices with their start and end apart: 11 -> 11, of which waited for: 7 -> 6; matrix products, arithmetic and copies ran while one was open for 0% -> 0% of each run, Pallas kernels for 15% -> 18%
where the time goes in v6:
time: 42.1 us; the launch traced here: 41.9 us
  starting transfers between devices  16.5 us (39%)
  waiting for transfers between devices  13 us (31%)
  Pallas kernels  8.03 us (19%)
  local copies, waits for them, and re-layouts  3.57 us (8%)
  between operations  0.74 us (2%)
    ppermute x3, waiting for transfers between devices, local(): lax.ppermute(packed, 'fsdp', swaps(shards, k))  9.88 us
    ppermute x3, starting transfers between devices, local(): lax.ppermute(packed, 'fsdp', swaps(shards, k))  4.45 us
    ppermute x2, starting transfers between devices, of_all(): return [a, lax.ppermute(a, 'tensor', swap)]  4.28 us
    ppermute x3, starting transfers between devices, local(): lax.ppermute(rounded[k - 1], 'fsdp', swaps(shards, k))  4.23 us
    ppermute x2, starting transfers between devices, to_partners(): lax.ppermute(a, 'tensor', shift(n_tensor, n_tensor - k))  3.46 us
    ppermute x2, waiting for transfers between devices, of_all(): return [a, lax.ppermute(a, 'tensor', swap)]  2.39 us
    unnamed x8, local copies, waits for them, and re-layouts  2.24 us
    pallas_call x1, Pallas kernels, local(): pl.pallas_call(functools.partial(place_early_kernel, n_tensor, count), ou...  1.73 us
  transfers between devices with their start and end apart: 11, of which 6 were waited for; matrix products, arithmetic and copies ran while one was open for 0% of the time, Pallas kernels for 18%

profile of v6, /device:TPU:0, one launch (start us, length us, event | category | flops | bytes accessed | tf_op | source)
XLA Modules:
  0.0 41.9 jit_solution(4664412082119892881)
XLA Ops:
  0.6 1.3 %slice.12 = bf16[208,2048]{1,0:T(8,128)(2,1)S(1)} slice(bf16[256,2048]{1,0:T(8,128)(2,1)} %tokens.3), slice={[0:208], [0:2048]} | slice | bytes 1703936 | tf_op jit(solution)/shard_map/slice | solution.py:286
  2.0 3.0 %collective-permute-start.3 = (bf16[208,2048]{1,0:T(8,128)(2,1)S(1)}, bf16[208,2048]{1,0:T(8,128)(2,1)S(1)}, u32[]{:S(2)}, u32[]{:S(2)}) collective-permute-start(bf16[208,2048]{1,0:T(8,128)(2,1)S(1)} %slice.12), channel_id=1, source_target_pairs={{0,2},{2,0},{1,3},{3,1},{4,6},{6,4},{5,7},{7,5},{8,10},{10,8},{9,1... | collective-permute-start | bytes 2555912 | tf_op jit(solution)/shard_map/ppermute | solution.py:283
  5.0 0.9 %copy-done.1 = bf16[1,1,2,2,128,128]{5,4,3,2,1,0:T(8,128)(2,1)S(1)} copy-done((bf16[1,1,2,2,128,128]{5,4,3,2,1,0:T(8,128)(2,1)S(1)}, bf16[1,1,2,2,128,128]{5,4,3,2,1,0:T(8,128)(2,1)}, u32[]{:S(2)}) %copy-start.1) | copy-done | bytes 131096
  5.9 0.7 %copy-done.2 = s32[1,1,2,2]{3,2,1,0:T(2,128)S(1)} copy-done((s32[1,1,2,2]{3,2,1,0:T(2,128)S(1)}, s32[1,1,2,2]{3,2,1,0:T(2,128)}, u32[]{:S(2)}) %copy-start.2) | copy-done | bytes 40
  6.6 0.7 %copy-done.3 = s32[1,1,2]{2,1,0:T(1,128)S(1)} copy-done((s32[1,1,2]{2,1,0:T(1,128)S(1)}, s32[1,1,2]{2,1,0:T(1,128)}, u32[]{:S(2)}) %copy-start.3) | copy-done | bytes 32
  7.2 0.6 %pack.1.refs_0_ = bf16[528,128]{1,0:T(8,128)(2,1)S(1)} custom-call(s32[1,1,2,2]{3,2,1,0:T(2,128)S(1)} %copy-done.2, s32[1,1,2]{2,1,0:T(1,128)S(1)} %copy-done.3, bf16[1,1,2,2,128,128]{5,4,3,2,1,0:T(8,128)(2,1)S(1)} %copy-done.1), custom_call_target="tpu_custom_call" | custom-call | bytes 3690 | tf_op jit(solution)/shard_map/pack/pallas_call | solution.py:287
  7.8 3.7 %collective-permute-start.2 = (bf16[528,128]{1,0:T(8,128)(2,1)S(1)}, bf16[528,128]{1,0:T(8,128)(2,1)S(1)}, u32[]{:S(2)}, u32[]{:S(2)}) collective-permute-start(bf16[528,128]{1,0:T(8,128)(2,1)S(1)} %pack.1.refs_0_), channel_id=1, source_target_pairs={{0,12},{4,8},{8,4},{12,0},{1,13},{5,9},{9,5},{13,1},{2,14},{6,10},... | collective-permute-start | bytes 405512 | tf_op jit(solution)/shard_map/ppermute | solution.py:298
  11.5 0.8 %collective-permute-start = (bf16[528,128]{1,0:T(8,128)(2,1)S(1)}, bf16[528,128]{1,0:T(8,128)(2,1)S(1)}, u32[]{:S(2)}, u32[]{:S(2)}) collective-permute-start(bf16[528,128]{1,0:T(8,128)(2,1)S(1)} %pack.1.refs_0_), channel_id=1, source_target_pairs={{0,4},{4,0},{8,12},{12,8},{1,5},{5,1},{9,13},{13,9},{2,6},{6,2},{1... | collective-permute-start | bytes 405512 | tf_op jit(solution)/shard_map/ppermute | solution.py:298
  12.3 0.5 %collective-permute-start.5 = (bf16[48,2048]{1,0:T(8,128)(2,1)S(1)}, bf16[48,2048]{1,0:T(8,128)(2,1)S(1)}, u32[]{:S(2)}, u32[]{:S(2)}) collective-permute-start(bf16[48,2048]{1,0:T(8,128)(2,1)S(1)} %slice.15), channel_id=1, source_target_pairs={{0,2},{2,0},{1,3},{3,1},{4,6},{6,4},{5,7},{7,5},{8,10},{10,8},{9,1... | collective-permute-start | bytes 589832 | tf_op jit(solution)/shard_map/ppermute | solution.py:283
  12.7 3.5 %collective-permute-done.2.refs_3_ = bf16[528,128]{1,0:T(8,128)(2,1)S(1)} collective-permute-done((bf16[528,128]{1,0:T(8,128)(2,1)S(1)}, bf16[528,128]{1,0:T(8,128)(2,1)S(1)}, u32[]{:S(2)}, u32[]{:S(2)}) %collective-permute-start.2) | collective-permute-done | bytes 135200 | tf_op jit(solution)/shard_map/ppermute | solution.py:298
  16.2 6.4 %collective-permute-done.1.refs_2_ = bf16[528,128]{1,0:T(8,128)(2,1)S(1)} collective-permute-done((bf16[528,128]{1,0:T(8,128)(2,1)S(1)}, bf16[528,128]{1,0:T(8,128)(2,1)S(1)}, u32[]{:S(2)}, u32[]{:S(2)}) %collective-permute-start.1) | collective-permute-done | bytes 135200 | tf_op jit(solution)/shard_map/ppermute | solution.py:298
  22.6 1.5 %prepare.1 = (s32[16,128]{1,0:T(8,128)S(1)}, bf16[9,128,128]{2,1,0:T(8,128)(2,1)S(1)}, bf16[8,256,128]{2,1,0:T(8,128)(2,1)S(1)}) custom-call(bf16[528,128]{1,0:T(8,128)(2,1)S(1)} %pack.1.refs_0_, bf16[528,128]{1,0:T(8,128)(2,1)S(1)} %collective-permute-done.refs_1_, bf16[528,128]{1,0:T(8,128)(2,1)S(1)} %collective-permute-done.1.refs_2_, ...), custom_call_target="tpu_custom_call" | custom-call | bytes 3690 | tf_op jit(solution)/shard_map/prepare/pallas_call | solution.py:301
  24.1 0.6 %collective-permute-done.3.refs_0_ = bf16[208,2048]{1,0:T(8,128)(2,1)S(1)} collective-permute-done((bf16[208,2048]{1,0:T(8,128)(2,1)S(1)}, bf16[208,2048]{1,0:T(8,128)(2,1)S(1)}, u32[]{:S(2)}, u32[]{:S(2)}) %collective-permute-start.3) | collective-permute-done | bytes 852000 | tf_op jit(solution)/shard_map/ppermute | solution.py:283
  24.7 1.7 %early_terms.1 = (bf16[1680,128]{1,0:T(8,128)(2,1)S(1)}, f32[8,128,128]{2,1,0:T(8,128)S(1)}) custom-call(s32[16,128]{1,0:T(8,128)S(1)} %get-tuple-element.16.table, bf16[9,128,128]{2,1,0:T(8,128)(2,1)S(1)} %get-tuple-element.17.weights, bf16[256,2048]{1,0:T(8,128)(2,1)S(1)} %copy-done, bf16[8,256,128]{2,1,0:T(8,128)(2,1)S(1)} %get-tuple-element.18.hb, ...), custom_call_target="tpu_custom_call" | custom-call | bytes 3690 | tf_op jit(solution)/shard_map/early_terms/pallas_call | solution.py:321
  26.4 2.1 %collective-permute-start.4 = (bf16[1680,128]{1,0:T(8,128)(2,1)S(1)}, bf16[1680,128]{1,0:T(8,128)(2,1)S(1)}, u32[]{:S(2)}, u32[]{:S(2)}) collective-permute-start(bf16[1680,128]{1,0:T(8,128)(2,1)S(1)} %get-tuple-element.19.refs_2_), channel_id=1, source_target_pairs={{0,2},{2,0},{1,3},{3,1},{4,6},{6,4},{5,7},{7,5},{8,10},{10,8},{9,1... | collective-permute-start | bytes 1290248 | tf_op jit(solution)/shard_map/ppermute | solution.py:373
  28.6 0.9 %late_tiles.1 = (f32[4,2,128,128]{3,2,1,0:T(8,128)S(1)}, bf16[4,2,128,128]{3,2,1,0:T(8,128)(2,1)S(1)}, bf16[384,128]{1,0:T(8,128)(2,1)S(1)}) custom-call(s32[16,128]{1,0:T(8,128)S(1)} %get-tuple-element.16.table, bf16[9,128,128]{2,1,0:T(8,128)(2,1)S(1)} %get-tuple-element.17.weights, bf16[256,2048]{1,0:T(8,128)(2,1)S(1)} %copy-done, ...), custom_call_target="tpu_custom_call" | custom-call | bytes 3690 | tf_op jit(solution)/shard_map/late_tiles/pallas_call | solution.py:337
  29.5 2.2 %collective-permute-start.6 = (bf16[384,128]{1,0:T(8,128)(2,1)S(1)}, bf16[384,128]{1,0:T(8,128)(2,1)S(1)}, u32[]{:S(2)}, u32[]{:S(2)}) collective-permute-start(bf16[384,128]{1,0:T(8,128)(2,1)S(1)} %get-tuple-element.21.refs_2_), channel_id=1, source_target_pairs={{0,2},{2,0},{1,3},{3,1},{4,6},{6,4},{5,7},{7,5},{8,10},{10,8},{9,1... | collective-permute-start | bytes 294920 | tf_op jit(solution)/shard_map/ppermute | solution.py:373
  31.8 2.7 %collective-permute-start.8 = (bf16[2,128,128]{2,1,0:T(8,128)(2,1)S(1)}, bf16[2,128,128]{2,1,0:T(8,128)(2,1)S(1)}, u32[]{:S(2)}, u32[]{:S(2)}) collective-permute-start(bf16[2,128,128]{2,1,0:T(8,128)(2,1)S(1)} %get-tuple-element.27), channel_id=1, source_target_pairs={{0,8},{4,12},{8,0},{12,4},{1,9},{5,13},{9,1},{13,5},{2,10},{6,14},... | collective-permute-start | bytes 196616 | tf_op jit(solution)/shard_map/ppermute | solution.py:368
  34.4 1.3 %collective-permute-start.9 = (bf16[2,128,128]{2,1,0:T(8,128)(2,1)S(1)}, bf16[2,128,128]{2,1,0:T(8,128)(2,1)S(1)}, u32[]{:S(2)}, u32[]{:S(2)}) collective-permute-start(bf16[2,128,128]{2,1,0:T(8,128)(2,1)S(1)} %get-tuple-element.28), channel_id=1, source_target_pairs={{0,12},{4,8},{8,4},{12,0},{1,13},{5,9},{9,5},{13,1},{2,14},{6,10},... | collective-permute-start | bytes 196616 | tf_op jit(solution)/shard_map/ppermute | solution.py:368
  35.8 0.2 collective-permute-start.10
  36.0 2.4 %collective-permute-done.4.refs_3_ = bf16[1680,128]{1,0:T(8,128)(2,1)S(1)} collective-permute-done((bf16[1680,128]{1,0:T(8,128)(2,1)S(1)}, bf16[1680,128]{1,0:T(8,128)(2,1)S(1)}, u32[]{:S(2)}, u32[]{:S(2)}) %collective-permute-start.4) | collective-permute-done | bytes 430112 | tf_op jit(solution)/shard_map/ppermute | solution.py:373
  38.4 1.7 %place_early.1.refs_4_ = bf16[256,4096]{1,0:T(8,128)(2,1)} custom-call(bf16[16,128]{1,0:T(8,128)(2,1)S(1)} %slice.13.refs_0_, bf16[16,128]{1,0:T(8,128)(2,1)S(1)} %slice.16.refs_1_, bf16[1680,128]{1,0:T(8,128)(2,1)S(1)} %get-tuple-element.19.refs_2_, bf16[1680,128]{1,0:T(8,128)(2,1)S(1)} %collective-permute-done.4.refs_3_), custom_call_target="tpu_custom_call" | custom-call | bytes 3690 | tf_op jit(solution)/shard_map/place_early/pallas_call | solution.py:387
  40.1 1.0 %place_late.1 = bf16[256,4096]{1,0:T(8,128)(2,1)} custom-call(bf16[16,128]{1,0:T(8,128)(2,1)S(1)} %slice.13.refs_0_, bf16[16,128]{1,0:T(8,128)(2,1)S(1)} %slice.16.refs_1_, bf16[384,128]{1,0:T(8,128)(2,1)S(1)} %get-tuple-element.21.refs_2_, bf16[384,128]{1,0:T(8,128)(2,1)S(1)} %collective-permute-done.6.refs_3_, ...), custom_call_target="tpu_custom_call", output_to_operand_aliasing={{}: (4, {})} | custom-call | bytes 3690 | tf_op jit(solution)/shard_map/place_late/pallas_call | solution.py:397
  41.2 0.7 %sum.1 = bf16[2,128,128]{2,1,0:T(8,128)(2,1)} custom-call(f32[2,128,128]{2,1,0:T(8,128)S(1)} %get-tuple-element.26.mine, bf16[2,128,128]{2,1,0:T(8,128)(2,1)S(1)} %collective-permute-done.8.refs_0_, bf16[2,128,128]{2,1,0:T(8,128)(2,1)S(1)} %collective-permute-done.9.refs_1_, bf16[2,128,128]{2,1,0:T(8,128)(2,1)S(1)} %collective-permute-done.10.refs_2_), custom_call_target="tpu_custom_call" | custom-call | bytes 3690 | tf_op jit(solution)/shard_map/sum/pallas_call | solution.py:409
  (18 shorter events, 0.3 us)
Async XLA Ops:
  0.6 11.6 %copy-start = (bf16[256,2048]{1,0:T(8,128)(2,1)S(1)}, bf16[256,2048]{1,0:T(8,128)(2,1)}, u32[]{:S(2)}) copy-start(bf16[256,2048]{1,0:T(8,128)(2,1)} %tokens.3) | copy-start | bytes 3145732
  2.0 22.8 %collective-permute-start.3 = (bf16[208,2048]{1,0:T(8,128)(2,1)S(1)}, bf16[208,2048]{1,0:T(8,128)(2,1)S(1)}, u32[]{:S(2)}, u32[]{:S(2)}) collective-permute-start(bf16[208,2048]{1,0:T(8,128)(2,1)S(1)} %slice.12), channel_id=1, source_target_pairs={{0,2},{2,0},{1,3},{3,1},{4,6},{6,4},{5,7},{7,5},{8,10},{10,8},{9,1... | collective-permute-start | bytes 2555912 | tf_op jit(solution)/shard_map/ppermute | solution.py:283
  5.0 0.9 %copy-start.1 = (bf16[1,1,2,2,128,128]{5,4,3,2,1,0:T(8,128)(2,1)S(1)}, bf16[1,1,2,2,128,128]{5,4,3,2,1,0:T(8,128)(2,1)}, u32[]{:S(2)}) copy-start(bf16[1,1,2,2,128,128]{5,4,3,2,1,0:T(8,128)(2,1)} %tiles.1) | copy-start | bytes 393220
  5.9 0.7 %copy-start.2 = (s32[1,1,2,2]{3,2,1,0:T(2,128)S(1)}, s32[1,1,2,2]{3,2,1,0:T(2,128)}, u32[]{:S(2)}) copy-start(s32[1,1,2,2]{3,2,1,0:T(2,128)} %keep.1) | copy-start | bytes 52
  6.6 0.7 %copy-start.3 = (s32[1,1,2]{2,1,0:T(1,128)S(1)}, s32[1,1,2]{2,1,0:T(1,128)}, u32[]{:S(2)}) copy-start(s32[1,1,2]{2,1,0:T(1,128)} %count.1) | copy-start | bytes 28
  7.8 8.4 %collective-permute-start.2 = (bf16[528,128]{1,0:T(8,128)(2,1)S(1)}, bf16[528,128]{1,0:T(8,128)(2,1)S(1)}, u32[]{:S(2)}, u32[]{:S(2)}) collective-permute-start(bf16[528,128]{1,0:T(8,128)(2,1)S(1)} %pack.1.refs_0_), channel_id=1, source_target_pairs={{0,12},{4,8},{8,4},{12,0},{1,13},{5,9},{9,5},{13,1},{2,14},{6,10},... | collective-permute-start | bytes 405512 | tf_op jit(solution)/shard_map/ppermute | solution.py:298
  11.5 11.1 %collective-permute-start.1 = (bf16[528,128]{1,0:T(8,128)(2,1)S(1)}, bf16[528,128]{1,0:T(8,128)(2,1)S(1)}, u32[]{:S(2)}, u32[]{:S(2)}) collective-permute-start(bf16[528,128]{1,0:T(8,128)(2,1)S(1)} %pack.1.refs_0_), channel_id=1, source_target_pairs={{0,8},{4,12},{8,0},{12,4},{1,9},{5,13},{9,1},{13,5},{2,10},{6,14},... | collective-permute-start | bytes 405512 | tf_op jit(solution)/shard_map/ppermute | solution.py:298
  11.5 11.1 %collective-permute-start = (bf16[528,128]{1,0:T(8,128)(2,1)S(1)}, bf16[528,128]{1,0:T(8,128)(2,1)S(1)}, u32[]{:S(2)}, u32[]{:S(2)}) collective-permute-start(bf16[528,128]{1,0:T(8,128)(2,1)S(1)} %pack.1.refs_0_), channel_id=1, source_target_pairs={{0,4},{4,0},{8,12},{12,8},{1,5},{5,1},{9,13},{13,9},{2,6},{6,2},{1... | collective-permute-start | bytes 405512 | tf_op jit(solution)/shard_map/ppermute | solution.py:298
  12.3 16.3 %collective-permute-start.5 = (bf16[48,2048]{1,0:T(8,128)(2,1)S(1)}, bf16[48,2048]{1,0:T(8,128)(2,1)S(1)}, u32[]{:S(2)}, u32[]{:S(2)}) collective-permute-start(bf16[48,2048]{1,0:T(8,128)(2,1)S(1)} %slice.15), channel_id=1, source_target_pairs={{0,2},{2,0},{1,3},{3,1},{4,6},{6,4},{5,7},{7,5},{8,10},{10,8},{9,1... | collective-permute-start | bytes 589832 | tf_op jit(solution)/shard_map/ppermute | solution.py:283
  26.4 12.0 %collective-permute-start.4 = (bf16[1680,128]{1,0:T(8,128)(2,1)S(1)}, bf16[1680,128]{1,0:T(8,128)(2,1)S(1)}, u32[]{:S(2)}, u32[]{:S(2)}) collective-permute-start(bf16[1680,128]{1,0:T(8,128)(2,1)S(1)} %get-tuple-element.19.refs_2_), channel_id=1, source_target_pairs={{0,2},{2,0},{1,3},{3,1},{4,6},{6,4},{5,7},{7,5},{8,10},{10,8},{9,1... | collective-permute-start | bytes 1290248 | tf_op jit(solution)/shard_map/ppermute | solution.py:373
  29.5 2.2 %collective-permute-start.7 = (bf16[4,2,128,128]{3,2,1,0:T(8,128)(2,1)S(1)}, bf16[4,2,128,128]{3,2,1,0:T(8,128)(2,1)S(1)}, u32[]{:S(2)}, u32[]{:S(2)}) collective-permute-start(bf16[4,2,128,128]{3,2,1,0:T(8,128)(2,1)S(1)} %get-tuple-element.23), channel_id=1, source_target_pairs={{0,1},{1,0},{2,3},{3,2},{4,5},{5,4},{6,7},{7,6},{8,9},{9,8},{10,11... | collective-permute-start | bytes 786440 | tf_op jit(solution)/shard_map/ppermute | solution.py:357
  29.5 10.6 %collective-permute-start.6 = (bf16[384,128]{1,0:T(8,128)(2,1)S(1)}, bf16[384,128]{1,0:T(8,128)(2,1)S(1)}, u32[]{:S(2)}, u32[]{:S(2)}) collective-permute-start(bf16[384,128]{1,0:T(8,128)(2,1)S(1)} %get-tuple-element.21.refs_2_), channel_id=1, source_target_pairs={{0,2},{2,0},{1,3},{3,1},{4,6},{6,4},{5,7},{7,5},{8,10},{10,8},{9,1... | collective-permute-start | bytes 294920 | tf_op jit(solution)/shard_map/ppermute | solution.py:373
  31.8 9.3 %collective-permute-start.8 = (bf16[2,128,128]{2,1,0:T(8,128)(2,1)S(1)}, bf16[2,128,128]{2,1,0:T(8,128)(2,1)S(1)}, u32[]{:S(2)}, u32[]{:S(2)}) collective-permute-start(bf16[2,128,128]{2,1,0:T(8,128)(2,1)S(1)} %get-tuple-element.27), channel_id=1, source_target_pairs={{0,8},{4,12},{8,0},{12,4},{1,9},{5,13},{9,1},{13,5},{2,10},{6,14},... | collective-permute-start | bytes 196616 | tf_op jit(solution)/shard_map/ppermute | solution.py:368
  34.4 6.7 %collective-permute-start.9 = (bf16[2,128,128]{2,1,0:T(8,128)(2,1)S(1)}, bf16[2,128,128]{2,1,0:T(8,128)(2,1)S(1)}, u32[]{:S(2)}, u32[]{:S(2)}) collective-permute-start(bf16[2,128,128]{2,1,0:T(8,128)(2,1)S(1)} %get-tuple-element.28), channel_id=1, source_target_pairs={{0,12},{4,8},{8,4},{12,0},{1,13},{5,9},{9,5},{13,1},{2,14},{6,10},... | collective-permute-start | bytes 196616 | tf_op jit(solution)/shard_map/ppermute | solution.py:368
  35.8 5.4 %collective-permute-start.10 = (bf16[2,128,128]{2,1,0:T(8,128)(2,1)S(1)}, bf16[2,128,128]{2,1,0:T(8,128)(2,1)S(1)}, u32[]{:S(2)}, u32[]{:S(2)}) collective-permute-start(bf16[2,128,128]{2,1,0:T(8,128)(2,1)S(1)} %get-tuple-element.29), channel_id=1, source_target_pairs={{0,4},{4,0},{8,12},{12,8},{1,5},{5,1},{9,13},{13,9},{2,6},{6,2},{1... | collective-permute-start | bytes 196616 | tf_op jit(solution)/shard_map/ppermute | solution.py:368

commit v7 on v6

--- a/solution.py
+++ b/solution.py
@@ -12,6 +12,7 @@
 I32 = jnp.int32
 ROW, COL, SLOT, CFIRST, RFIRST = range(5)
 INFO_ROWS = 16
+ZERO_PARTS = 8
 
 
 def shift(size, k):
@@ -28,6 +29,19 @@
             body(i)
     else:
         lax.fori_loop(0, count, lambda i, c: (body(i), c)[1], 0)
+
+
+def add_all(count, values, into, at):
+    if count <= 8:
+        done = [values(i) for i in range(count)]
+        for i in range(count):
+            into[at(i)] += done[i]
+    else:
+
+        def one(i):
+            into[at(i)] += values(i)
+
+        loop(count, one)
 
 
 def find_first(table, src, dst, count):
@@ -78,7 +92,13 @@
 
 def prepare_kernel(shards, cap, *refs):
     packed, refs = refs[:shards], refs[shards:]
-    hidden, listed, weights, hb, info, table, tsem, hsem = refs
+    hidden, listed, weights, hb, out, info, zeros, table, tsem, hsem, zsem = refs
+    zeros[...] = jnp.zeros_like(zeros)
+    high = zeros.shape[0]
+    clear = [
+        pltpu.make_async_copy(zeros, out.at[pl.ds(n * high, high), :], zsem.at[n])
+        for n in range(ZERO_PARTS)
+    ]
     blk = weights.shape[-1]
     base = 2 * cap * blk
     count = hb.shape[0]
@@ -100,6 +120,8 @@
         return pltpu.make_async_copy(hidden.at[:, pl.ds(at, blk)], hb.at[i], hsem.at[i])
 
     loop(count, lambda i: column(i).start())
+    for c in clear:
+        c.start()
     find_first(table, COL, CFIRST, count)
     find_first(table, ROW, RFIRST, count)
     done = pltpu.make_async_copy(table, listed, tsem)
@@ -112,6 +134,8 @@
                 p = p + jnp.where(info[k, 0, 2 * j + m] >= 0, 1, 0).astype(I32)
     loop(count, lambda i: column(i).wait())
     done.wait()
+    for c in clear:
+        c.wait()
 
 
 def forward_backward(lo, table, weights, tokens, hb, remote, xs, pre, grads):
@@ -122,7 +146,7 @@
     t = lax.axis_index("tensor")
     pre[...] = jnp.zeros_like(pre)
 
-    def forward(i):
+    def product(i):
         r = table[i, ROW]
         part = lax.rem(lax.div(r, rows_here) - t + n_tensor, n_tensor)
         at = pl.multiple_of(lax.rem(r, rows_here) * blk, blk)
@@ -130,9 +154,9 @@
         for n, ref in enumerate(remote):
             x = jnp.where(part == n + 1, ref[:, pl.ds(at, blk)], x)
         xs[i] = x
-        pre[i // live, table[i, CFIRST]] += dot(x, weights[i], ((1,), (0,)))
-
-    loop(count, forward)
+        return dot(x, weights[i], ((1,), (0,)))
+
+    add_all(count, product, pre, lambda i: (i // live, table[i, CFIRST]))
 
     def backward(i):
         m = i // live
@@ -160,13 +184,15 @@
     count, size, _ = acc.shape
     acc[...] = jnp.zeros_like(acc)
 
-    def one(i):
-        acc[table[i, RFIRST]] += dot(grads[i], weights[i], ((1,), (1,)))
-
     def put(i):
         back[pl.ds(pl.multiple_of(i * size, size), size), :] = acc[i].astype(BF16)
 
-    loop(count, one)
+    add_all(
+        count,
+        lambda i: dot(grads[i], weights[i], ((1,), (1,))),
+        acc,
+        lambda i: table[i, RFIRST],
+    )
     loop(count, put)
 
 
@@ -197,10 +223,12 @@
     s = lax.axis_index("seq")
     live = xs.shape[0] // 2
 
-    def tile(i):
-        value = tile_sums[i] + dot(xs[i], grads[i], ((0,), (0,)))
+    def put(i, value):
         slot = table[i, SLOT]
         both[lax.rem(slot + s, cap), lax.div(slot, cap), i // live] = value
+
+    def tile(i):
+        put(i, tile_sums[i] + dot(xs[i], grads[i], ((0,), (0,))))
 
     loop(xs.shape[0], tile)
     own[...] = both[0]
@@ -213,40 +241,53 @@
         total[...] = (own[k] + other[k].astype(F32)).astype(total.dtype)
 
 
-def place_chunk(n_tensor, count, lo, refs, meanwhile=None):
+def place_kernel(n_tensor, count, lo, *refs):
     infos, refs = refs[:n_tensor], refs[n_tensor:]
     parts, refs = refs[:n_tensor], refs[n_tensor:]
-    out, rows, block, wide, sem = refs
-    size = block.shape[0]
-    blk = parts[0].shape[1]
+    _, out, rows, total, wide, sems = refs
     for n, info in enumerate(infos):
         rows[n] = info[...].astype(F32).astype(I32)
-    total = block if n_tensor == 2 else wide
-    total[...] = jnp.zeros_like(total)
-    if meanwhile is not None:
-        meanwhile()
-    for n, part in enumerate(parts):
-
-        def add(i):
-            at = pl.ds(pl.multiple_of(rows[n, i, 0] * blk, blk), blk)
-            term = part[pl.ds(pl.multiple_of(i * size, size), size), :].astype(F32)
-            total[:, at] = (total[:, at].astype(F32) + term).astype(total.dtype)
-
-        loop(count, add)
     if n_tensor != 2:
-        block[...] = wide[...].astype(BF16)
-    copy = pltpu.make_async_copy(block, out.at[pl.ds(lo, size), :], sem)
-    copy.start()
-    copy.wait()
-
-
-def place_early_kernel(n_tensor, count, *refs):
-    place_chunk(n_tensor, count, 0, refs)
-
-
-def place_late_kernel(n_tensor, lo, count, *refs):
-    first, (_, *rest) = refs[: 2 * n_tensor], refs[2 * n_tensor :]
-    place_chunk(n_tensor, count, lo, (*first, *rest))
+        wide[...] = jnp.zeros_like(wide)
+        size, blk = wide.shape[0], parts[0].shape[1]
+        for n, part in enumerate(parts):
+
+            def add(i):
+                at = pl.ds(pl.multiple_of(rows[n, i, 0] * blk, blk), blk)
+                wide[:, at] += part[pl.ds(pl.multiple_of(i * size, size), size), :].astype(F32)
+
+            loop(count, add)
+        total[...] = wide[...].astype(BF16)
+        copy = pltpu.make_async_copy(total, out.at[pl.ds(lo, size), :], sems.at[0])
+        copy.start()
+        copy.wait()
+        return
+    _, size, blk = total.shape
+    where = [rows[n, i, 0] for n in range(2) for i in range(count)]
+    first = []
+    for e, r in enumerate(where):
+        f = jnp.int32(e)
+        for before in range(e - 1, -1, -1):
+            f = jnp.where(where[before] == r, before, f).astype(I32)
+        first.append(f)
+    for i in range(count):
+        total[i] = parts[0][pl.ds(i * size, size), :]
+    for i in range(count):
+        f = first[count + i]
+        term = parts[1][pl.ds(i * size, size), :].astype(F32)
+        so_far = jnp.where(f == count + i, 0.0, total[f].astype(F32))
+        total[f] = (so_far + term).astype(BF16)
+
+    def copy(e):
+        at = pl.ds(pl.multiple_of(where[e] * blk, blk), blk)
+        return pltpu.make_async_copy(total.at[e], out.at[pl.ds(lo, size), at], sems.at[e])
+
+    for act in ("start", "wait"):
+        for e in range(2 * count):
+
+            @pl.when(first[e] == e)
+            def _():
+                getattr(copy(e), act)()
 
 
 def sum_kernel(mine, *refs):
@@ -273,7 +314,7 @@
     hbm = pl.BlockSpec(memory_space=pltpu.HBM)
     spare = pltpu.CompilerParams(vmem_limit_bytes=(16 if count <= 8 else 40) * 2**20)
     swap = shift(2, 1)
-    order = [shards // 2] + [k for k in range(shards - 1, 0, -1) if k != shards // 2]
+    order = [3,1,2] if shards == 4 else list(range(1, shards))
 
     def shape(dims, kind):
         return jax.ShapeDtypeStruct(dims, kind)
@@ -298,20 +339,23 @@
         lax.ppermute(packed, "fsdp", swaps(shards, k)) for k in range(1, shards)
     ]
 
-    listed, weights, hb = pl.pallas_call(
+    listed, weights, hb, token_grad = pl.pallas_call(
         functools.partial(prepare_kernel, shards, cap),
         out_shape=(
             shape((lines, blk), I32),
             shape((count + 1, blk, blk), BF16),
             shape((count, toks, blk), BF16),
+            shape((toks, width), BF16),
         ),
         in_specs=[vmem] * shards + [hbm],
-        out_specs=(vmem, vmem, vmem),
+        out_specs=(vmem, vmem, vmem, hbm),
         scratch_shapes=[
             pltpu.VMEM((shards, 8, blk), I32),
+            pltpu.VMEM((toks // ZERO_PARTS, width), BF16),
             pltpu.SMEM((lines, blk), I32),
             pltpu.SemaphoreType.DMA,
             pltpu.SemaphoreType.DMA((count,)),
+            pltpu.SemaphoreType.DMA((ZERO_PARTS,)),
         ],
         compiler_params=pltpu.CompilerParams(vmem_limit_bytes=50 * 2**20),
         cost_estimate=cost(0.001),
@@ -375,36 +419,34 @@
         return [everyone[n] for n in range(n_tensor)]
 
     def scratch(size):
+        if n_tensor == 2:
+            total, wide = (2 * count, size, blk), (8, 128)
+        else:
+            total, wide = (size, width), (size, width)
         return [
             pltpu.VMEM((n_tensor, lines, blk), I32),
-            pltpu.VMEM((size, width), BF16),
-            pltpu.VMEM((size, width) if n_tensor != 2 else (8, 128), F32),
-            pltpu.SemaphoreType.DMA,
+            pltpu.VMEM(total, BF16),
+            pltpu.VMEM(wide, F32),
+            pltpu.SemaphoreType.DMA((2 * count,)),
         ]
 
     parts = of_all(back_early)
     infos = [part[count * cut :] for part in parts]
-    token_grad = pl.pallas_call(
-        functools.partial(place_early_kernel, n_tensor, count),
-        out_shape=shape((toks, width), BF16),
-        in_specs=[vmem] * (2 * n_tensor),
-        out_specs=hbm,
-        scratch_shapes=scratch(cut),
-        compiler_params=spare,
-        cost_estimate=cost(0.001),
-        name="place_early",
-    )(*infos, *parts)
-    token_grad = pl.pallas_call(
-        functools.partial(place_late_kernel, n_tensor, cut, count),
-        out_shape=shape((toks, width), BF16),
-        in_specs=[vmem] * (2 * n_tensor) + [hbm],
-        out_specs=hbm,
-        scratch_shapes=scratch(rest),
-        input_output_aliases={2 * n_tensor: 0},
-        compiler_params=spare,
-        cost_estimate=cost(0.001),
-        name="place_late",
-    )(*infos, *of_all(back_late), token_grad)
+    for name, lo, size, chunk in (
+        ("place_early", 0, cut, parts),
+        ("place_late", cut, rest, of_all(back_late)),
+    ):
+        token_grad = pl.pallas_call(
+            functools.partial(place_kernel, n_tensor, count, lo),
+            out_shape=shape((toks, width), BF16),
+            in_specs=[vmem] * (2 * n_tensor) + [hbm],
+            out_specs=hbm,
+            scratch_shapes=scratch(size),
+            input_output_aliases={2 * n_tensor: 0},
+            compiler_params=spare,
+            cost_estimate=cost(0.001),
+            name=name,
+        )(*infos, *chunk, token_grad)
     token_grad, mine = lax.optimization_barrier((token_grad, mine))
     tile_grads = pl.pallas_call(
         sum_kernel,

time: 42.1 us -> 42.2 us (level)
    ppermute x3, waiting for transfers between devices: 0.07 us -> 0.75 us  [local(): lax.ppermute(rounded[k - 1], 'fsdp', swaps(shards, k))]
    pallas_call x2, Pallas kernels: 2.69 us -> 2.04 us  [local(): pl.pallas_call(functools.partial(place_kernel, n_tensor, count, lo), out_...]
    pallas_call x1, Pallas kernels: 1.49 us -> 2.09 us  [local(): pl.pallas_call(functools.partial(prepare_kernel, shards, cap), out_shape=...]
  transfers between devices with their start and end apart: 11 -> 11, of which waited for: 6 -> 7; matrix products, arithmetic and copies ran while one was open for 0% -> 0% of each run, Pallas kernels for 18% -> 17%
where the time goes in v7:
time: 42.2 us; the launch traced here: 41.9 us
  starting transfers between devices  16.4 us (39%)
  waiting for transfers between devices  13.3 us (32%)
  Pallas kernels  7.9 us (19%)
  local copies, waits for them, and re-layouts  3.57 us (8%)
  between operations  0.73 us (2%)
    ppermute x3, waiting for transfers between devices, local(): lax.ppermute(packed, 'fsdp', swaps(shards, k))  9.74 us
    ppermute x3, starting transfers between devices, local(): lax.ppermute(packed, 'fsdp', swaps(shards, k))  4.45 us
    ppermute x2, starting transfers between devices, of_all(): return [a, lax.ppermute(a, 'tensor', swap)]  4.25 us
    ppermute x3, starting transfers between devices, local(): lax.ppermute(rounded[k - 1], 'fsdp', swaps(shards, k))  4.23 us
    ppermute x2, starting transfers between devices, to_partners(): lax.ppermute(a, 'tensor', shift(n_tensor, n_tensor - k))  3.39 us
    ppermute x2, waiting for transfers between devices, of_all(): return [a, lax.ppermute(a, 'tensor', swap)]  2.36 us
    unnamed x8, local copies, waits for them, and re-layouts  2.24 us
    pallas_call x1, Pallas kernels, local(): pl.pallas_call(functools.partial(prepare_kernel, shards, cap), out_shape=...  2.09 us
  transfers between devices with their start and end apart: 11, of which 7 were waited for; matrix products, arithmetic and copies ran while one was open for 0% of the time, Pallas kernels for 17%

profile of v7, /device:TPU:0, one launch (start us, length us, event | category | flops | bytes accessed | tf_op | source)
XLA Modules:
  0.0 41.9 jit_solution(16617963881975292466)
XLA Ops:
  0.6 1.3 %slice.12 = bf16[208,2048]{1,0:T(8,128)(2,1)S(1)} slice(bf16[256,2048]{1,0:T(8,128)(2,1)} %tokens.3), slice={[0:208], [0:2048]} | slice | bytes 1703936 | tf_op jit(solution)/shard_map/slice | solution.py:327
  2.0 3.0 %collective-permute-start.3 = (bf16[208,2048]{1,0:T(8,128)(2,1)S(1)}, bf16[208,2048]{1,0:T(8,128)(2,1)S(1)}, u32[]{:S(2)}, u32[]{:S(2)}) collective-permute-start(bf16[208,2048]{1,0:T(8,128)(2,1)S(1)} %slice.12), channel_id=1, source_target_pairs={{0,2},{2,0},{1,3},{3,1},{4,6},{6,4},{5,7},{7,5},{8,10},{10,8},{9,1... | collective-permute-start | bytes 2555912 | tf_op jit(solution)/shard_map/ppermute | solution.py:324
  5.0 0.9 %copy-done.1 = bf16[1,1,2,2,128,128]{5,4,3,2,1,0:T(8,128)(2,1)S(1)} copy-done((bf16[1,1,2,2,128,128]{5,4,3,2,1,0:T(8,128)(2,1)S(1)}, bf16[1,1,2,2,128,128]{5,4,3,2,1,0:T(8,128)(2,1)}, u32[]{:S(2)}) %copy-start.1) | copy-done | bytes 131096
  5.9 0.7 %copy-done.2 = s32[1,1,2,2]{3,2,1,0:T(2,128)S(1)} copy-done((s32[1,1,2,2]{3,2,1,0:T(2,128)S(1)}, s32[1,1,2,2]{3,2,1,0:T(2,128)}, u32[]{:S(2)}) %copy-start.2) | copy-done | bytes 40
  6.6 0.7 %copy-done.3 = s32[1,1,2]{2,1,0:T(1,128)S(1)} copy-done((s32[1,1,2]{2,1,0:T(1,128)S(1)}, s32[1,1,2]{2,1,0:T(1,128)}, u32[]{:S(2)}) %copy-start.3) | copy-done | bytes 32
  7.2 0.6 %pack.1.refs_0_ = bf16[528,128]{1,0:T(8,128)(2,1)S(1)} custom-call(s32[1,1,2,2]{3,2,1,0:T(2,128)S(1)} %copy-done.2, s32[1,1,2]{2,1,0:T(1,128)S(1)} %copy-done.3, bf16[1,1,2,2,128,128]{5,4,3,2,1,0:T(8,128)(2,1)S(1)} %copy-done.1), custom_call_target="tpu_custom_call" | custom-call | bytes 3690 | tf_op jit(solution)/shard_map/pack/pallas_call | solution.py:328
  7.8 1.6 %collective-permute-start = (bf16[528,128]{1,0:T(8,128)(2,1)S(1)}, bf16[528,128]{1,0:T(8,128)(2,1)S(1)}, u32[]{:S(2)}, u32[]{:S(2)}) collective-permute-start(bf16[528,128]{1,0:T(8,128)(2,1)S(1)} %pack.1.refs_0_), channel_id=1, source_target_pairs={{0,4},{4,0},{8,12},{12,8},{1,5},{5,1},{9,13},{13,9},{2,6},{6,2},{1... | collective-permute-start | bytes 405512 | tf_op jit(solution)/shard_map/ppermute | solution.py:339
  9.4 2.6 %collective-permute-start.1 = (bf16[528,128]{1,0:T(8,128)(2,1)S(1)}, bf16[528,128]{1,0:T(8,128)(2,1)S(1)}, u32[]{:S(2)}, u32[]{:S(2)}) collective-permute-start(bf16[528,128]{1,0:T(8,128)(2,1)S(1)} %pack.1.refs_0_), channel_id=1, source_target_pairs={{0,8},{4,12},{8,0},{12,4},{1,9},{5,13},{9,1},{13,5},{2,10},{6,14},... | collective-permute-start | bytes 405512 | tf_op jit(solution)/shard_map/ppermute | solution.py:339
  12.3 0.4 collective-permute-start.5
  12.6 1.8 %collective-permute-done.refs_1_ = bf16[528,128]{1,0:T(8,128)(2,1)S(1)} collective-permute-done((bf16[528,128]{1,0:T(8,128)(2,1)S(1)}, bf16[528,128]{1,0:T(8,128)(2,1)S(1)}, u32[]{:S(2)}, u32[]{:S(2)}) %collective-permute-start) | collective-permute-done | bytes 135200 | tf_op jit(solution)/shard_map/ppermute | solution.py:339
  14.5 7.9 %collective-permute-done.1.refs_2_ = bf16[528,128]{1,0:T(8,128)(2,1)S(1)} collective-permute-done((bf16[528,128]{1,0:T(8,128)(2,1)S(1)}, bf16[528,128]{1,0:T(8,128)(2,1)S(1)}, u32[]{:S(2)}, u32[]{:S(2)}) %collective-permute-start.1) | collective-permute-done | bytes 135200 | tf_op jit(solution)/shard_map/ppermute | solution.py:339
  22.4 2.1 %prepare.1 = (s32[16,128]{1,0:T(8,128)S(1)}, bf16[9,128,128]{2,1,0:T(8,128)(2,1)S(1)}, bf16[8,256,128]{2,1,0:T(8,128)(2,1)S(1)}, bf16[256,4096]{1,0:T(8,128)(2,1)}) custom-call(bf16[528,128]{1,0:T(8,128)(2,1)S(1)} %pack.1.refs_0_, bf16[528,128]{1,0:T(8,128)(2,1)S(1)} %collective-permute-done.refs_1_, bf16[528,128]{1,0:T(8,128)(2,1)S(1)} %collective-permute-done.1.refs_2_, ...), custom_call_target="tpu_custom_call" | custom-call | bytes 3690 | tf_op jit(solution)/shard_map/prepare/pallas_call | solution.py:342
  24.7 1.6 %early_terms.1 = (bf16[1680,128]{1,0:T(8,128)(2,1)S(1)}, f32[8,128,128]{2,1,0:T(8,128)S(1)}) custom-call(s32[16,128]{1,0:T(8,128)S(1)} %get-tuple-element.17.table, bf16[9,128,128]{2,1,0:T(8,128)(2,1)S(1)} %get-tuple-element.18.weights, bf16[256,2048]{1,0:T(8,128)(2,1)S(1)} %copy-done, bf16[8,256,128]{2,1,0:T(8,128)(2,1)S(1)} %get-tuple-element.19.hb, ...), custom_call_target="tpu_custom_call" | custom-call | bytes 3690 | tf_op jit(solution)/shard_map/early_terms/pallas_call | solution.py:365
  26.4 2.1 %collective-permute-start.4 = (bf16[1680,128]{1,0:T(8,128)(2,1)S(1)}, bf16[1680,128]{1,0:T(8,128)(2,1)S(1)}, u32[]{:S(2)}, u32[]{:S(2)}) collective-permute-start(bf16[1680,128]{1,0:T(8,128)(2,1)S(1)} %get-tuple-element.20.refs_2_), channel_id=1, source_target_pairs={{0,2},{2,0},{1,3},{3,1},{4,6},{6,4},{5,7},{7,5},{8,10},{10,8},{9,1... | collective-permute-start | bytes 1290248 | tf_op jit(solution)/shard_map/ppermute | solution.py:417
  28.7 0.8 %late_tiles.1 = (f32[4,2,128,128]{3,2,1,0:T(8,128)S(1)}, bf16[4,2,128,128]{3,2,1,0:T(8,128)(2,1)S(1)}, bf16[384,128]{1,0:T(8,128)(2,1)S(1)}) custom-call(s32[16,128]{1,0:T(8,128)S(1)} %get-tuple-element.17.table, bf16[9,128,128]{2,1,0:T(8,128)(2,1)S(1)} %get-tuple-element.18.weights, bf16[256,2048]{1,0:T(8,128)(2,1)S(1)} %copy-done, ...), custom_call_target="tpu_custom_call" | custom-call | bytes 3690 | tf_op jit(solution)/shard_map/late_tiles/pallas_call | solution.py:381
  29.6 2.1 %collective-permute-start.6 = (bf16[384,128]{1,0:T(8,128)(2,1)S(1)}, bf16[384,128]{1,0:T(8,128)(2,1)S(1)}, u32[]{:S(2)}, u32[]{:S(2)}) collective-permute-start(bf16[384,128]{1,0:T(8,128)(2,1)S(1)} %get-tuple-element.22.refs_2_), channel_id=1, source_target_pairs={{0,2},{2,0},{1,3},{3,1},{4,6},{6,4},{5,7},{7,5},{8,10},{10,8},{9,1... | collective-permute-start | bytes 294920 | tf_op jit(solution)/shard_map/ppermute | solution.py:417
  31.8 2.6 %collective-permute-start.10 = (bf16[2,128,128]{2,1,0:T(8,128)(2,1)S(1)}, bf16[2,128,128]{2,1,0:T(8,128)(2,1)S(1)}, u32[]{:S(2)}, u32[]{:S(2)}) collective-permute-start(bf16[2,128,128]{2,1,0:T(8,128)(2,1)S(1)} %get-tuple-element.31), channel_id=1, source_target_pairs={{0,8},{4,12},{8,0},{12,4},{1,9},{5,13},{9,1},{13,5},{2,10},{6,14},... | collective-permute-start | bytes 196616 | tf_op jit(solution)/shard_map/ppermute | solution.py:412
  34.4 1.4 %collective-permute-start.8 = (bf16[2,128,128]{2,1,0:T(8,128)(2,1)S(1)}, bf16[2,128,128]{2,1,0:T(8,128)(2,1)S(1)}, u32[]{:S(2)}, u32[]{:S(2)}) collective-permute-start(bf16[2,128,128]{2,1,0:T(8,128)(2,1)S(1)} %get-tuple-element.29), channel_id=1, source_target_pairs={{0,12},{4,8},{8,4},{12,0},{1,13},{5,9},{9,5},{13,1},{2,14},{6,10},... | collective-permute-start | bytes 196616 | tf_op jit(solution)/shard_map/ppermute | solution.py:412
  36.0 2.4 %collective-permute-done.4.refs_3_ = bf16[1680,128]{1,0:T(8,128)(2,1)S(1)} collective-permute-done((bf16[1680,128]{1,0:T(8,128)(2,1)S(1)}, bf16[1680,128]{1,0:T(8,128)(2,1)S(1)}, u32[]{:S(2)}, u32[]{:S(2)}) %collective-permute-start.4) | collective-permute-done | bytes 430112 | tf_op jit(solution)/shard_map/ppermute | solution.py:417
  38.4 1.1 %place_early.1.refs_4_ = bf16[256,4096]{1,0:T(8,128)(2,1)} custom-call(bf16[16,128]{1,0:T(8,128)(2,1)S(1)} %slice.13.refs_0_, bf16[16,128]{1,0:T(8,128)(2,1)S(1)} %slice.16.refs_1_, bf16[1680,128]{1,0:T(8,128)(2,1)S(1)} %get-tuple-element.20.refs_2_, bf16[1680,128]{1,0:T(8,128)(2,1)S(1)} %collective-permute-done.4.refs_3_, ...), custom_call_target="tpu_custom_call", output_to_operand_aliasing={{}: (4, {})} | custom-call | bytes 3690 | tf_op jit(solution)/shard_map/place_early/pallas_call | solution.py:439
  39.5 0.9 %place_late.1 = bf16[256,4096]{1,0:T(8,128)(2,1)} custom-call(bf16[16,128]{1,0:T(8,128)(2,1)S(1)} %slice.13.refs_0_, bf16[16,128]{1,0:T(8,128)(2,1)S(1)} %slice.16.refs_1_, bf16[384,128]{1,0:T(8,128)(2,1)S(1)} %get-tuple-element.22.refs_2_, bf16[384,128]{1,0:T(8,128)(2,1)S(1)} %collective-permute-done.6.refs_3_, ...), custom_call_target="tpu_custom_call", output_to_operand_aliasing={{}: (4, {})} | custom-call | bytes 3690 | tf_op jit(solution)/shard_map/place_late/pallas_call | solution.py:439
  40.5 0.4 collective-permute-done.8.refs_0_
  40.9 0.4 collective-permute-done.9.refs_1_
  41.2 0.7 %sum.1 = bf16[2,128,128]{2,1,0:T(8,128)(2,1)} custom-call(f32[2,128,128]{2,1,0:T(8,128)S(1)} %get-tuple-element.28.mine, bf16[2,128,128]{2,1,0:T(8,128)(2,1)S(1)} %collective-permute-done.8.refs_0_, bf16[2,128,128]{2,1,0:T(8,128)(2,1)S(1)} %collective-permute-done.9.refs_1_, bf16[2,128,128]{2,1,0:T(8,128)(2,1)S(1)} %collective-permute-done.10.refs_2_), custom_call_target="tpu_custom_call" | custom-call | bytes 3690 | tf_op jit(solution)/shard_map/sum/pallas_call | solution.py:451
  (18 shorter events, 1.1 us)
Async XLA Ops:
  0.6 11.6 %copy-start = (bf16[256,2048]{1,0:T(8,128)(2,1)S(1)}, bf16[256,2048]{1,0:T(8,128)(2,1)}, u32[]{:S(2)}) copy-start(bf16[256,2048]{1,0:T(8,128)(2,1)} %tokens.3) | copy-start | bytes 3145732
  2.0 22.8 %collective-permute-start.3 = (bf16[208,2048]{1,0:T(8,128)(2,1)S(1)}, bf16[208,2048]{1,0:T(8,128)(2,1)S(1)}, u32[]{:S(2)}, u32[]{:S(2)}) collective-permute-start(bf16[208,2048]{1,0:T(8,128)(2,1)S(1)} %slice.12), channel_id=1, source_target_pairs={{0,2},{2,0},{1,3},{3,1},{4,6},{6,4},{5,7},{7,5},{8,10},{10,8},{9,1... | collective-permute-start | bytes 2555912 | tf_op jit(solution)/shard_map/ppermute | solution.py:324
  5.0 0.9 %copy-start.1 = (bf16[1,1,2,2,128,128]{5,4,3,2,1,0:T(8,128)(2,1)S(1)}, bf16[1,1,2,2,128,128]{5,4,3,2,1,0:T(8,128)(2,1)}, u32[]{:S(2)}) copy-start(bf16[1,1,2,2,128,128]{5,4,3,2,1,0:T(8,128)(2,1)} %tiles.1) | copy-start | bytes 393220
  5.9 0.7 %copy-start.2 = (s32[1,1,2,2]{3,2,1,0:T(2,128)S(1)}, s32[1,1,2,2]{3,2,1,0:T(2,128)}, u32[]{:S(2)}) copy-start(s32[1,1,2,2]{3,2,1,0:T(2,128)} %keep.1) | copy-start | bytes 52
  6.6 0.7 %copy-start.3 = (s32[1,1,2]{2,1,0:T(1,128)S(1)}, s32[1,1,2]{2,1,0:T(1,128)}, u32[]{:S(2)}) copy-start(s32[1,1,2]{2,1,0:T(1,128)} %count.1) | copy-start | bytes 28
  7.8 6.7 %collective-permute-start = (bf16[528,128]{1,0:T(8,128)(2,1)S(1)}, bf16[528,128]{1,0:T(8,128)(2,1)S(1)}, u32[]{:S(2)}, u32[]{:S(2)}) collective-permute-start(bf16[528,128]{1,0:T(8,128)(2,1)S(1)} %pack.1.refs_0_), channel_id=1, source_target_pairs={{0,4},{4,0},{8,12},{12,8},{1,5},{5,1},{9,13},{13,9},{2,6},{6,2},{1... | collective-permute-start | bytes 405512 | tf_op jit(solution)/shard_map/ppermute | solution.py:339
  9.4 13.0 %collective-permute-start.1 = (bf16[528,128]{1,0:T(8,128)(2,1)S(1)}, bf16[528,128]{1,0:T(8,128)(2,1)S(1)}, u32[]{:S(2)}, u32[]{:S(2)}) collective-permute-start(bf16[528,128]{1,0:T(8,128)(2,1)S(1)} %pack.1.refs_0_), channel_id=1, source_target_pairs={{0,8},{4,12},{8,0},{12,4},{1,9},{5,13},{9,1},{13,5},{2,10},{6,14},... | collective-permute-start | bytes 405512 | tf_op jit(solution)/shard_map/ppermute | solution.py:339
  12.0 10.4 %collective-permute-start.2 = (bf16[528,128]{1,0:T(8,128)(2,1)S(1)}, bf16[528,128]{1,0:T(8,128)(2,1)S(1)}, u32[]{:S(2)}, u32[]{:S(2)}) collective-permute-start(bf16[528,128]{1,0:T(8,128)(2,1)S(1)} %pack.1.refs_0_), channel_id=1, source_target_pairs={{0,12},{4,8},{8,4},{12,0},{1,13},{5,9},{9,5},{13,1},{2,14},{6,10},... | collective-permute-start | bytes 405512 | tf_op jit(solution)/shard_map/ppermute | solution.py:339
  12.3 16.4 %collective-permute-start.5 = (bf16[48,2048]{1,0:T(8,128)(2,1)S(1)}, bf16[48,2048]{1,0:T(8,128)(2,1)S(1)}, u32[]{:S(2)}, u32[]{:S(2)}) collective-permute-start(bf16[48,2048]{1,0:T(8,128)(2,1)S(1)} %slice.15), channel_id=1, source_target_pairs={{0,2},{2,0},{1,3},{3,1},{4,6},{6,4},{5,7},{7,5},{8,10},{10,8},{9,1... | collective-permute-start | bytes 589832 | tf_op jit(solution)/shard_map/ppermute | solution.py:324
  26.4 12.0 %collective-permute-start.4 = (bf16[1680,128]{1,0:T(8,128)(2,1)S(1)}, bf16[1680,128]{1,0:T(8,128)(2,1)S(1)}, u32[]{:S(2)}, u32[]{:S(2)}) collective-permute-start(bf16[1680,128]{1,0:T(8,128)(2,1)S(1)} %get-tuple-element.20.refs_2_), channel_id=1, source_target_pairs={{0,2},{2,0},{1,3},{3,1},{4,6},{6,4},{5,7},{7,5},{8,10},{10,8},{9,1... | collective-permute-start | bytes 1290248 | tf_op jit(solution)/shard_map/ppermute | solution.py:417
  29.5 2.2 %collective-permute-start.7 = (bf16[4,2,128,128]{3,2,1,0:T(8,128)(2,1)S(1)}, bf16[4,2,128,128]{3,2,1,0:T(8,128)(2,1)S(1)}, u32[]{:S(2)}, u32[]{:S(2)}) collective-permute-start(bf16[4,2,128,128]{3,2,1,0:T(8,128)(2,1)S(1)} %get-tuple-element.25), channel_id=1, source_target_pairs={{0,1},{1,0},{2,3},{3,2},{4,5},{5,4},{6,7},{7,6},{8,9},{9,8},{10,11... | collective-permute-start | bytes 786440 | tf_op jit(solution)/shard_map/ppermute | solution.py:401
  29.6 9.9 %collective-permute-start.6 = (bf16[384,128]{1,0:T(8,128)(2,1)S(1)}, bf16[384,128]{1,0:T(8,128)(2,1)S(1)}, u32[]{:S(2)}, u32[]{:S(2)}) collective-permute-start(bf16[384,128]{1,0:T(8,128)(2,1)S(1)} %get-tuple-element.22.refs_2_), channel_id=1, source_target_pairs={{0,2},{2,0},{1,3},{3,1},{4,6},{6,4},{5,7},{7,5},{8,10},{10,8},{9,1... | collective-permute-start | bytes 294920 | tf_op jit(solution)/shard_map/ppermute | solution.py:417
  31.8 8.7 %collective-permute-start.10 = (bf16[2,128,128]{2,1,0:T(8,128)(2,1)S(1)}, bf16[2,128,128]{2,1,0:T(8,128)(2,1)S(1)}, u32[]{:S(2)}, u32[]{:S(2)}) collective-permute-start(bf16[2,128,128]{2,1,0:T(8,128)(2,1)S(1)} %get-tuple-element.31), channel_id=1, source_target_pairs={{0,8},{4,12},{8,0},{12,4},{1,9},{5,13},{9,1},{13,5},{2,10},{6,14},... | collective-permute-start | bytes 196616 | tf_op jit(solution)/shard_map/ppermute | solution.py:412
  34.4 6.4 %collective-permute-start.8 = (bf16[2,128,128]{2,1,0:T(8,128)(2,1)S(1)}, bf16[2,128,128]{2,1,0:T(8,128)(2,1)S(1)}, u32[]{:S(2)}, u32[]{:S(2)}) collective-permute-start(bf16[2,128,128]{2,1,0:T(8,128)(2,1)S(1)} %get-tuple-element.29), channel_id=1, source_target_pairs={{0,12},{4,8},{8,4},{12,0},{1,13},{5,9},{9,5},{13,1},{2,14},{6,10},... | collective-permute-start | bytes 196616 | tf_op jit(solution)/shard_map/ppermute | solution.py:412
  35.8 5.4 %collective-permute-start.9 = (bf16[2,128,128]{2,1,0:T(8,128)(2,1)S(1)}, bf16[2,128,128]{2,1,0:T(8,128)(2,1)S(1)}, u32[]{:S(2)}, u32[]{:S(2)}) collective-permute-start(bf16[2,128,128]{2,1,0:T(8,128)(2,1)S(1)} %get-tuple-element.30), channel_id=1, source_target_pairs={{0,4},{4,0},{8,12},{12,8},{1,5},{5,1},{9,13},{13,9},{2,6},{6,2},{1... | collective-permute-start | bytes 196616 | tf_op jit(solution)/shard_map/ppermute | solution.py:412

commit v8 on v6

--- a/solution.py
+++ b/solution.py
@@ -28,6 +28,19 @@
             body(i)
     else:
         lax.fori_loop(0, count, lambda i, c: (body(i), c)[1], 0)
+
+
+def add_all(count, values, into, at):
+    if count <= 8:
+        done = [values(i) for i in range(count)]
+        for i in range(count):
+            into[at(i)] += done[i]
+    else:
+
+        def one(i):
+            into[at(i)] += values(i)
+
+        loop(count, one)
 
 
 def find_first(table, src, dst, count):
@@ -122,7 +135,7 @@
     t = lax.axis_index("tensor")
     pre[...] = jnp.zeros_like(pre)
 
-    def forward(i):
+    def product(i):
         r = table[i, ROW]
         part = lax.rem(lax.div(r, rows_here) - t + n_tensor, n_tensor)
         at = pl.multiple_of(lax.rem(r, rows_here) * blk, blk)
@@ -130,9 +143,9 @@
         for n, ref in enumerate(remote):
             x = jnp.where(part == n + 1, ref[:, pl.ds(at, blk)], x)
         xs[i] = x
-        pre[i // live, table[i, CFIRST]] += dot(x, weights[i], ((1,), (0,)))
-
-    loop(count, forward)
+        return dot(x, weights[i], ((1,), (0,)))
+
+    add_all(count, product, pre, lambda i: (i // live, table[i, CFIRST]))
 
     def backward(i):
         m = i // live
@@ -160,13 +173,15 @@
     count, size, _ = acc.shape
     acc[...] = jnp.zeros_like(acc)
 
-    def one(i):
-        acc[table[i, RFIRST]] += dot(grads[i], weights[i], ((1,), (1,)))
-
     def put(i):
         back[pl.ds(pl.multiple_of(i * size, size), size), :] = acc[i].astype(BF16)
 
-    loop(count, one)
+    add_all(
+        count,
+        lambda i: dot(grads[i], weights[i], ((1,), (1,))),
+        acc,
+        lambda i: table[i, RFIRST],
+    )
     loop(count, put)
 
 
@@ -197,10 +212,12 @@
     s = lax.axis_index("seq")
     live = xs.shape[0] // 2
 
-    def tile(i):
-        value = tile_sums[i] + dot(xs[i], grads[i], ((0,), (0,)))
+    def put(i, value):
         slot = table[i, SLOT]
         both[lax.rem(slot + s, cap), lax.div(slot, cap), i // live] = value
+
+    def tile(i):
+        put(i, tile_sums[i] + dot(xs[i], grads[i], ((0,), (0,))))
 
     loop(xs.shape[0], tile)
     own[...] = both[0]

time: 42.1 us -> 42.1 us (level)
  transfers between devices with their start and end apart: 11 -> 11, of which waited for: 6 -> 6; matrix products, arithmetic and copies ran while one was open for 0% -> 0% of each run, Pallas kernels for 18% -> 17%
where the time goes in v8:
time: 42.1 us; the launch traced here: 41.9 us
  starting transfers between devices  16.5 us (39%)
  waiting for transfers between devices  13.3 us (32%)
  Pallas kernels  7.88 us (19%)
  local copies, waits for them, and re-layouts  3.57 us (8%)
  between operations  0.74 us (2%)
    ppermute x3, waiting for transfers between devices, local(): lax.ppermute(packed, 'fsdp', swaps(shards, k))  9.88 us
    ppermute x3, starting transfers between devices, local(): lax.ppermute(packed, 'fsdp', swaps(shards, k))  4.45 us
    ppermute x2, starting transfers between devices, of_all(): return [a, lax.ppermute(a, 'tensor', swap)]  4.24 us
    ppermute x3, starting transfers between devices, local(): lax.ppermute(rounded[k - 1], 'fsdp', swaps(shards, k))  4.23 us
    ppermute x2, starting transfers between devices, to_partners(): lax.ppermute(a, 'tensor', shift(n_tensor, n_tensor - k))  3.46 us
    ppermute x2, waiting for transfers between devices, of_all(): return [a, lax.ppermute(a, 'tensor', swap)]  2.36 us
    unnamed x8, local copies, waits for them, and re-layouts  2.24 us
    pallas_call x1, Pallas kernels, local(): pl.pallas_call(functools.partial(place_early_kernel, n_tensor, count), ou...  1.74 us
  transfers between devices with their start and end apart: 11, of which 6 were waited for; matrix products, arithmetic and copies ran while one was open for 0% of the time, Pallas kernels for 17%

profile of v8, /device:TPU:0, one launch (start us, length us, event | category | flops | bytes accessed | tf_op | source)
XLA Modules:
  0.0 41.9 jit_solution(6374133341145073690)
XLA Ops:
  0.6 1.3 %slice.12 = bf16[208,2048]{1,0:T(8,128)(2,1)S(1)} slice(bf16[256,2048]{1,0:T(8,128)(2,1)} %tokens.3), slice={[0:208], [0:2048]} | slice | bytes 1703936 | tf_op jit(solution)/shard_map/slice | solution.py:303
  2.0 3.0 %collective-permute-start.3 = (bf16[208,2048]{1,0:T(8,128)(2,1)S(1)}, bf16[208,2048]{1,0:T(8,128)(2,1)S(1)}, u32[]{:S(2)}, u32[]{:S(2)}) collective-permute-start(bf16[208,2048]{1,0:T(8,128)(2,1)S(1)} %slice.12), channel_id=1, source_target_pairs={{0,2},{2,0},{1,3},{3,1},{4,6},{6,4},{5,7},{7,5},{8,10},{10,8},{9,1... | collective-permute-start | bytes 2555912 | tf_op jit(solution)/shard_map/ppermute | solution.py:300
  5.0 0.9 %copy-done.1 = bf16[1,1,2,2,128,128]{5,4,3,2,1,0:T(8,128)(2,1)S(1)} copy-done((bf16[1,1,2,2,128,128]{5,4,3,2,1,0:T(8,128)(2,1)S(1)}, bf16[1,1,2,2,128,128]{5,4,3,2,1,0:T(8,128)(2,1)}, u32[]{:S(2)}) %copy-start.1) | copy-done | bytes 131096
  5.9 0.7 %copy-done.2 = s32[1,1,2,2]{3,2,1,0:T(2,128)S(1)} copy-done((s32[1,1,2,2]{3,2,1,0:T(2,128)S(1)}, s32[1,1,2,2]{3,2,1,0:T(2,128)}, u32[]{:S(2)}) %copy-start.2) | copy-done | bytes 40
  6.6 0.7 %copy-done.3 = s32[1,1,2]{2,1,0:T(1,128)S(1)} copy-done((s32[1,1,2]{2,1,0:T(1,128)S(1)}, s32[1,1,2]{2,1,0:T(1,128)}, u32[]{:S(2)}) %copy-start.3) | copy-done | bytes 32
  7.2 0.6 %pack.1.refs_0_ = bf16[528,128]{1,0:T(8,128)(2,1)S(1)} custom-call(s32[1,1,2,2]{3,2,1,0:T(2,128)S(1)} %copy-done.2, s32[1,1,2]{2,1,0:T(1,128)S(1)} %copy-done.3, bf16[1,1,2,2,128,128]{5,4,3,2,1,0:T(8,128)(2,1)S(1)} %copy-done.1), custom_call_target="tpu_custom_call" | custom-call | bytes 3690 | tf_op jit(solution)/shard_map/pack/pallas_call | solution.py:304
  7.8 3.7 %collective-permute-start.2 = (bf16[528,128]{1,0:T(8,128)(2,1)S(1)}, bf16[528,128]{1,0:T(8,128)(2,1)S(1)}, u32[]{:S(2)}, u32[]{:S(2)}) collective-permute-start(bf16[528,128]{1,0:T(8,128)(2,1)S(1)} %pack.1.refs_0_), channel_id=1, source_target_pairs={{0,12},{4,8},{8,4},{12,0},{1,13},{5,9},{9,5},{13,1},{2,14},{6,10},... | collective-permute-start | bytes 405512 | tf_op jit(solution)/shard_map/ppermute | solution.py:315
  11.5 0.8 %collective-permute-start = (bf16[528,128]{1,0:T(8,128)(2,1)S(1)}, bf16[528,128]{1,0:T(8,128)(2,1)S(1)}, u32[]{:S(2)}, u32[]{:S(2)}) collective-permute-start(bf16[528,128]{1,0:T(8,128)(2,1)S(1)} %pack.1.refs_0_), channel_id=1, source_target_pairs={{0,4},{4,0},{8,12},{12,8},{1,5},{5,1},{9,13},{13,9},{2,6},{6,2},{1... | collective-permute-start | bytes 405512 | tf_op jit(solution)/shard_map/ppermute | solution.py:315
  12.3 0.5 %collective-permute-start.5 = (bf16[48,2048]{1,0:T(8,128)(2,1)S(1)}, bf16[48,2048]{1,0:T(8,128)(2,1)S(1)}, u32[]{:S(2)}, u32[]{:S(2)}) collective-permute-start(bf16[48,2048]{1,0:T(8,128)(2,1)S(1)} %slice.15), channel_id=1, source_target_pairs={{0,2},{2,0},{1,3},{3,1},{4,6},{6,4},{5,7},{7,5},{8,10},{10,8},{9,1... | collective-permute-start | bytes 589832 | tf_op jit(solution)/shard_map/ppermute | solution.py:300
  12.7 3.5 %collective-permute-done.2.refs_3_ = bf16[528,128]{1,0:T(8,128)(2,1)S(1)} collective-permute-done((bf16[528,128]{1,0:T(8,128)(2,1)S(1)}, bf16[528,128]{1,0:T(8,128)(2,1)S(1)}, u32[]{:S(2)}, u32[]{:S(2)}) %collective-permute-start.2) | collective-permute-done | bytes 135200 | tf_op jit(solution)/shard_map/ppermute | solution.py:315
  16.2 6.4 %collective-permute-done.1.refs_2_ = bf16[528,128]{1,0:T(8,128)(2,1)S(1)} collective-permute-done((bf16[528,128]{1,0:T(8,128)(2,1)S(1)}, bf16[528,128]{1,0:T(8,128)(2,1)S(1)}, u32[]{:S(2)}, u32[]{:S(2)}) %collective-permute-start.1) | collective-permute-done | bytes 135200 | tf_op jit(solution)/shard_map/ppermute | solution.py:315
  22.6 1.4 %prepare.1 = (s32[16,128]{1,0:T(8,128)S(1)}, bf16[9,128,128]{2,1,0:T(8,128)(2,1)S(1)}, bf16[8,256,128]{2,1,0:T(8,128)(2,1)S(1)}) custom-call(bf16[528,128]{1,0:T(8,128)(2,1)S(1)} %pack.1.refs_0_, bf16[528,128]{1,0:T(8,128)(2,1)S(1)} %collective-permute-done.refs_1_, bf16[528,128]{1,0:T(8,128)(2,1)S(1)} %collective-permute-done.1.refs_2_, ...), custom_call_target="tpu_custom_call" | custom-call | bytes 3690 | tf_op jit(solution)/shard_map/prepare/pallas_call | solution.py:318
  24.0 0.7 %collective-permute-done.3.refs_0_ = bf16[208,2048]{1,0:T(8,128)(2,1)S(1)} collective-permute-done((bf16[208,2048]{1,0:T(8,128)(2,1)S(1)}, bf16[208,2048]{1,0:T(8,128)(2,1)S(1)}, u32[]{:S(2)}, u32[]{:S(2)}) %collective-permute-start.3) | collective-permute-done | bytes 852000 | tf_op jit(solution)/shard_map/ppermute | solution.py:300
  24.7 1.6 %early_terms.1 = (bf16[1680,128]{1,0:T(8,128)(2,1)S(1)}, f32[8,128,128]{2,1,0:T(8,128)S(1)}) custom-call(s32[16,128]{1,0:T(8,128)S(1)} %get-tuple-element.16.table, bf16[9,128,128]{2,1,0:T(8,128)(2,1)S(1)} %get-tuple-element.17.weights, bf16[256,2048]{1,0:T(8,128)(2,1)S(1)} %copy-done, bf16[8,256,128]{2,1,0:T(8,128)(2,1)S(1)} %get-tuple-element.18.hb, ...), custom_call_target="tpu_custom_call" | custom-call | bytes 3690 | tf_op jit(solution)/shard_map/early_terms/pallas_call | solution.py:338
  26.4 2.1 %collective-permute-start.4 = (bf16[1680,128]{1,0:T(8,128)(2,1)S(1)}, bf16[1680,128]{1,0:T(8,128)(2,1)S(1)}, u32[]{:S(2)}, u32[]{:S(2)}) collective-permute-start(bf16[1680,128]{1,0:T(8,128)(2,1)S(1)} %get-tuple-element.19.refs_2_), channel_id=1, source_target_pairs={{0,2},{2,0},{1,3},{3,1},{4,6},{6,4},{5,7},{7,5},{8,10},{10,8},{9,1... | collective-permute-start | bytes 1290248 | tf_op jit(solution)/shard_map/ppermute | solution.py:390
  28.7 0.8 %late_tiles.1 = (f32[4,2,128,128]{3,2,1,0:T(8,128)S(1)}, bf16[4,2,128,128]{3,2,1,0:T(8,128)(2,1)S(1)}, bf16[384,128]{1,0:T(8,128)(2,1)S(1)}) custom-call(s32[16,128]{1,0:T(8,128)S(1)} %get-tuple-element.16.table, bf16[9,128,128]{2,1,0:T(8,128)(2,1)S(1)} %get-tuple-element.17.weights, bf16[256,2048]{1,0:T(8,128)(2,1)S(1)} %copy-done, ...), custom_call_target="tpu_custom_call" | custom-call | bytes 3690 | tf_op jit(solution)/shard_map/late_tiles/pallas_call | solution.py:354
  29.6 2.1 %collective-permute-start.6 = (bf16[384,128]{1,0:T(8,128)(2,1)S(1)}, bf16[384,128]{1,0:T(8,128)(2,1)S(1)}, u32[]{:S(2)}, u32[]{:S(2)}) collective-permute-start(bf16[384,128]{1,0:T(8,128)(2,1)S(1)} %get-tuple-element.21.refs_2_), channel_id=1, source_target_pairs={{0,2},{2,0},{1,3},{3,1},{4,6},{6,4},{5,7},{7,5},{8,10},{10,8},{9,1... | collective-permute-start | bytes 294920 | tf_op jit(solution)/shard_map/ppermute | solution.py:390
  31.8 2.7 %collective-permute-start.8 = (bf16[2,128,128]{2,1,0:T(8,128)(2,1)S(1)}, bf16[2,128,128]{2,1,0:T(8,128)(2,1)S(1)}, u32[]{:S(2)}, u32[]{:S(2)}) collective-permute-start(bf16[2,128,128]{2,1,0:T(8,128)(2,1)S(1)} %get-tuple-element.27), channel_id=1, source_target_pairs={{0,8},{4,12},{8,0},{12,4},{1,9},{5,13},{9,1},{13,5},{2,10},{6,14},... | collective-permute-start | bytes 196616 | tf_op jit(solution)/shard_map/ppermute | solution.py:385
  34.5 1.3 %collective-permute-start.9 = (bf16[2,128,128]{2,1,0:T(8,128)(2,1)S(1)}, bf16[2,128,128]{2,1,0:T(8,128)(2,1)S(1)}, u32[]{:S(2)}, u32[]{:S(2)}) collective-permute-start(bf16[2,128,128]{2,1,0:T(8,128)(2,1)S(1)} %get-tuple-element.28), channel_id=1, source_target_pairs={{0,12},{4,8},{8,4},{12,0},{1,13},{5,9},{9,5},{13,1},{2,14},{6,10},... | collective-permute-start | bytes 196616 | tf_op jit(solution)/shard_map/ppermute | solution.py:385
  35.8 0.2 collective-permute-start.10
  36.0 2.4 %collective-permute-done.4.refs_3_ = bf16[1680,128]{1,0:T(8,128)(2,1)S(1)} collective-permute-done((bf16[1680,128]{1,0:T(8,128)(2,1)S(1)}, bf16[1680,128]{1,0:T(8,128)(2,1)S(1)}, u32[]{:S(2)}, u32[]{:S(2)}) %collective-permute-start.4) | collective-permute-done | bytes 430112 | tf_op jit(solution)/shard_map/ppermute | solution.py:390
  38.4 1.7 %place_early.1.refs_4_ = bf16[256,4096]{1,0:T(8,128)(2,1)} custom-call(bf16[16,128]{1,0:T(8,128)(2,1)S(1)} %slice.13.refs_0_, bf16[16,128]{1,0:T(8,128)(2,1)S(1)} %slice.16.refs_1_, bf16[1680,128]{1,0:T(8,128)(2,1)S(1)} %get-tuple-element.19.refs_2_, bf16[1680,128]{1,0:T(8,128)(2,1)S(1)} %collective-permute-done.4.refs_3_), custom_call_target="tpu_custom_call" | custom-call | bytes 3690 | tf_op jit(solution)/shard_map/place_early/pallas_call | solution.py:404
  40.2 1.0 %place_late.1 = bf16[256,4096]{1,0:T(8,128)(2,1)} custom-call(bf16[16,128]{1,0:T(8,128)(2,1)S(1)} %slice.13.refs_0_, bf16[16,128]{1,0:T(8,128)(2,1)S(1)} %slice.16.refs_1_, bf16[384,128]{1,0:T(8,128)(2,1)S(1)} %get-tuple-element.21.refs_2_, bf16[384,128]{1,0:T(8,128)(2,1)S(1)} %collective-permute-done.6.refs_3_, ...), custom_call_target="tpu_custom_call", output_to_operand_aliasing={{}: (4, {})} | custom-call | bytes 3690 | tf_op jit(solution)/shard_map/place_late/pallas_call | solution.py:414
  41.2 0.7 %sum.1 = bf16[2,128,128]{2,1,0:T(8,128)(2,1)} custom-call(f32[2,128,128]{2,1,0:T(8,128)S(1)} %get-tuple-element.26.mine, bf16[2,128,128]{2,1,0:T(8,128)(2,1)S(1)} %collective-permute-done.8.refs_0_, bf16[2,128,128]{2,1,0:T(8,128)(2,1)S(1)} %collective-permute-done.9.refs_1_, bf16[2,128,128]{2,1,0:T(8,128)(2,1)S(1)} %collective-permute-done.10.refs_2_), custom_call_target="tpu_custom_call" | custom-call | bytes 3690 | tf_op jit(solution)/shard_map/sum/pallas_call | solution.py:426
  (18 shorter events, 0.5 us)
Async XLA Ops:
  0.6 11.6 %copy-start = (bf16[256,2048]{1,0:T(8,128)(2,1)S(1)}, bf16[256,2048]{1,0:T(8,128)(2,1)}, u32[]{:S(2)}) copy-start(bf16[256,2048]{1,0:T(8,128)(2,1)} %tokens.3) | copy-start | bytes 3145732
  2.0 22.8 %collective-permute-start.3 = (bf16[208,2048]{1,0:T(8,128)(2,1)S(1)}, bf16[208,2048]{1,0:T(8,128)(2,1)S(1)}, u32[]{:S(2)}, u32[]{:S(2)}) collective-permute-start(bf16[208,2048]{1,0:T(8,128)(2,1)S(1)} %slice.12), channel_id=1, source_target_pairs={{0,2},{2,0},{1,3},{3,1},{4,6},{6,4},{5,7},{7,5},{8,10},{10,8},{9,1... | collective-permute-start | bytes 2555912 | tf_op jit(solution)/shard_map/ppermute | solution.py:300
  5.0 0.9 %copy-start.1 = (bf16[1,1,2,2,128,128]{5,4,3,2,1,0:T(8,128)(2,1)S(1)}, bf16[1,1,2,2,128,128]{5,4,3,2,1,0:T(8,128)(2,1)}, u32[]{:S(2)}) copy-start(bf16[1,1,2,2,128,128]{5,4,3,2,1,0:T(8,128)(2,1)} %tiles.1) | copy-start | bytes 393220
  5.9 0.7 %copy-start.2 = (s32[1,1,2,2]{3,2,1,0:T(2,128)S(1)}, s32[1,1,2,2]{3,2,1,0:T(2,128)}, u32[]{:S(2)}) copy-start(s32[1,1,2,2]{3,2,1,0:T(2,128)} %keep.1) | copy-start | bytes 52
  6.6 0.7 %copy-start.3 = (s32[1,1,2]{2,1,0:T(1,128)S(1)}, s32[1,1,2]{2,1,0:T(1,128)}, u32[]{:S(2)}) copy-start(s32[1,1,2]{2,1,0:T(1,128)} %count.1) | copy-start | bytes 28
  7.8 8.4 %collective-permute-start.2 = (bf16[528,128]{1,0:T(8,128)(2,1)S(1)}, bf16[528,128]{1,0:T(8,128)(2,1)S(1)}, u32[]{:S(2)}, u32[]{:S(2)}) collective-permute-start(bf16[528,128]{1,0:T(8,128)(2,1)S(1)} %pack.1.refs_0_), channel_id=1, source_target_pairs={{0,12},{4,8},{8,4},{12,0},{1,13},{5,9},{9,5},{13,1},{2,14},{6,10},... | collective-permute-start | bytes 405512 | tf_op jit(solution)/shard_map/ppermute | solution.py:315
  11.5 11.1 %collective-permute-start.1 = (bf16[528,128]{1,0:T(8,128)(2,1)S(1)}, bf16[528,128]{1,0:T(8,128)(2,1)S(1)}, u32[]{:S(2)}, u32[]{:S(2)}) collective-permute-start(bf16[528,128]{1,0:T(8,128)(2,1)S(1)} %pack.1.refs_0_), channel_id=1, source_target_pairs={{0,8},{4,12},{8,0},{12,4},{1,9},{5,13},{9,1},{13,5},{2,10},{6,14},... | collective-permute-start | bytes 405512 | tf_op jit(solution)/shard_map/ppermute | solution.py:315
  11.5 11.1 %collective-permute-start = (bf16[528,128]{1,0:T(8,128)(2,1)S(1)}, bf16[528,128]{1,0:T(8,128)(2,1)S(1)}, u32[]{:S(2)}, u32[]{:S(2)}) collective-permute-start(bf16[528,128]{1,0:T(8,128)(2,1)S(1)} %pack.1.refs_0_), channel_id=1, source_target_pairs={{0,4},{4,0},{8,12},{12,8},{1,5},{5,1},{9,13},{13,9},{2,6},{6,2},{1... | collective-permute-start | bytes 405512 | tf_op jit(solution)/shard_map/ppermute | solution.py:315
  12.3 16.4 %collective-permute-start.5 = (bf16[48,2048]{1,0:T(8,128)(2,1)S(1)}, bf16[48,2048]{1,0:T(8,128)(2,1)S(1)}, u32[]{:S(2)}, u32[]{:S(2)}) collective-permute-start(bf16[48,2048]{1,0:T(8,128)(2,1)S(1)} %slice.15), channel_id=1, source_target_pairs={{0,2},{2,0},{1,3},{3,1},{4,6},{6,4},{5,7},{7,5},{8,10},{10,8},{9,1... | collective-permute-start | bytes 589832 | tf_op jit(solution)/shard_map/ppermute | solution.py:300
  26.4 12.0 %collective-permute-start.4 = (bf16[1680,128]{1,0:T(8,128)(2,1)S(1)}, bf16[1680,128]{1,0:T(8,128)(2,1)S(1)}, u32[]{:S(2)}, u32[]{:S(2)}) collective-permute-start(bf16[1680,128]{1,0:T(8,128)(2,1)S(1)} %get-tuple-element.19.refs_2_), channel_id=1, source_target_pairs={{0,2},{2,0},{1,3},{3,1},{4,6},{6,4},{5,7},{7,5},{8,10},{10,8},{9,1... | collective-permute-start | bytes 1290248 | tf_op jit(solution)/shard_map/ppermute | solution.py:390
  29.5 2.2 %collective-permute-start.7 = (bf16[4,2,128,128]{3,2,1,0:T(8,128)(2,1)S(1)}, bf16[4,2,128,128]{3,2,1,0:T(8,128)(2,1)S(1)}, u32[]{:S(2)}, u32[]{:S(2)}) collective-permute-start(bf16[4,2,128,128]{3,2,1,0:T(8,128)(2,1)S(1)} %get-tuple-element.23), channel_id=1, source_target_pairs={{0,1},{1,0},{2,3},{3,2},{4,5},{5,4},{6,7},{7,6},{8,9},{9,8},{10,11... | collective-permute-start | bytes 786440 | tf_op jit(solution)/shard_map/ppermute | solution.py:374
  29.6 10.5 %collective-permute-start.6 = (bf16[384,128]{1,0:T(8,128)(2,1)S(1)}, bf16[384,128]{1,0:T(8,128)(2,1)S(1)}, u32[]{:S(2)}, u32[]{:S(2)}) collective-permute-start(bf16[384,128]{1,0:T(8,128)(2,1)S(1)} %get-tuple-element.21.refs_2_), channel_id=1, source_target_pairs={{0,2},{2,0},{1,3},{3,1},{4,6},{6,4},{5,7},{7,5},{8,10},{10,8},{9,1... | collective-permute-start | bytes 294920 | tf_op jit(solution)/shard_map/ppermute | solution.py:390
  31.8 9.3 %collective-permute-start.8 = (bf16[2,128,128]{2,1,0:T(8,128)(2,1)S(1)}, bf16[2,128,128]{2,1,0:T(8,128)(2,1)S(1)}, u32[]{:S(2)}, u32[]{:S(2)}) collective-permute-start(bf16[2,128,128]{2,1,0:T(8,128)(2,1)S(1)} %get-tuple-element.27), channel_id=1, source_target_pairs={{0,8},{4,12},{8,0},{12,4},{1,9},{5,13},{9,1},{13,5},{2,10},{6,14},... | collective-permute-start | bytes 196616 | tf_op jit(solution)/shard_map/ppermute | solution.py:385
  34.5 6.7 %collective-permute-start.9 = (bf16[2,128,128]{2,1,0:T(8,128)(2,1)S(1)}, bf16[2,128,128]{2,1,0:T(8,128)(2,1)S(1)}, u32[]{:S(2)}, u32[]{:S(2)}) collective-permute-start(bf16[2,128,128]{2,1,0:T(8,128)(2,1)S(1)} %get-tuple-element.28), channel_id=1, source_target_pairs={{0,12},{4,8},{8,4},{12,0},{1,13},{5,9},{9,5},{13,1},{2,14},{6,10},... | collective-permute-start | bytes 196616 | tf_op jit(solution)/shard_map/ppermute | solution.py:385
  35.8 5.4 %collective-permute-start.10 = (bf16[2,128,128]{2,1,0:T(8,128)(2,1)S(1)}, bf16[2,128,128]{2,1,0:T(8,128)(2,1)S(1)}, u32[]{:S(2)}, u32[]{:S(2)}) collective-permute-start(bf16[2,128,128]{2,1,0:T(8,128)(2,1)S(1)} %get-tuple-element.29), channel_id=1, source_target_pairs={{0,4},{4,0},{8,12},{12,8},{1,5},{5,1},{9,13},{13,9},{2,6},{6,2},{1... | collective-permute-start | bytes 196616 | tf_op jit(solution)/shard_map/ppermute | solution.py:385
